TPU v7x, 256 devices: a whole 4x4x8 slice. The times are simulated.
256 devices in a mesh: rep: 8 (over x, y_lo), ep: 32 (over y_hi, z, core).
Axes of the slice: x: 4, y: 4 (y_hi: 2, y_lo: 2; y = y_hi * 2 + y_lo), z: 8, core: 2. Of those that a mesh axis runs over, the one named last changes fastest.
Arguments:
- hidden_in: bfloat16 [4, 64, 7168], P(None, 'ep'), may hold values from -6 to 6
- queries: bfloat16 [4, 64, 8192], P(None, None, 'ep'), may hold values from -216 to 216
- new_keys: bfloat16 [4, 64, 8192], P(None, None, 'ep'), may hold values from -6 to 6
- new_values: bfloat16 [4, 64, 8192], P(None, None, 'ep'), may hold values from -6 to 6
- cache_keys: bfloat16 [64, 32, 8192], P(None, None, 'ep'), may hold values from -6 to 6
- cache_values: bfloat16 [64, 32, 8192], P(None, None, 'ep'), may hold values from -6 to 6
- cache_lengths: int32 [64], replicated, may hold values from 1 to 32, 1056 in all
- expert_ids: int32 [4, 64, 8], P(None, 'ep'), may hold values from 0 to 31, all different within a row; in each aligned block of 2 rows (0 to 1, 2 to 3, ..., all dimensions but the last counted through in order) at most 2 rows name the same one
- router_logits: float32 [4, 64, 8], P(None, 'ep'), may hold values from -6 to 6
- norm_gain: float32 [7168], replicated, may hold values from 0.1 to 1.9
- out_sectioned: bfloat16 [8192, 7168], P('ep', 'rep'), may hold values from -0.0625 to 0.0625
- expert_sectioned: bfloat16 [32, 7168, 3, 1024], P('ep', 'rep'), may hold values from -0.09375 to 0.09375
- bucket_owner: int32 [32, 8], P('ep'), may hold values from 0 to 7, each once within a row
Outputs:
- layer_out: bfloat16 [4, 64, 7168], P(None, 'ep')
Inputs may be any that keep to these rules, and one draw needn't show every extreme that they name: `expert_ids`: within one step, the rows of one device (aligned blocks of 2 rows) name no expert more than 2 times; some expert is named exactly 2 times. Each row names distinct experts. `bucket_owner`: for each expert the owners of its 8 buckets are distinct.
All inputs are finite; a program needn't handle non-finite values.
Results may differ from a plain program's by a relative error of at most 0.025.
Values may be sent and summed in bfloat16 or wider, within the bound.
No kernel may reach another device: no remote copies, remote signals or barrier semaphores. Data moves between devices by JAX's collectives and lax.ppermute only.
A program may use at most 128 MiB of HBM per device.

v0:
```python
import math

import jax
import jax.numpy as jnp
from jax import lax
from jax.sharding import PartitionSpec as P

DH = 128


ROUTE_SCALE = 2.827
EPSILON = 1e-06


def attention(
    query_rows, key_cache, value_cache, fresh_keys, fresh_values, row_lengths, step_index, head_size
):
    row_count, feature_count = query_rows.shape
    head_count = feature_count // head_size
    cached = key_cache.shape[1]
    step_count = fresh_keys.shape[0]
    query_heads = query_rows.reshape(row_count, head_count, head_size)
    keys_old = key_cache.reshape(row_count, cached, head_count, head_size)
    values_old = value_cache.reshape(row_count, cached, head_count, head_size)
    keys_recent = fresh_keys.reshape(step_count, row_count, head_count, head_size)
    values_recent = fresh_values.reshape(step_count, row_count, head_count, head_size)
    factor = 1.0 / math.sqrt(head_size)
    scores_old = (
        jnp.einsum("rhd,rchd->rhc", query_heads, keys_old, preferred_element_type=jnp.float32)
        * factor
    )
    in_cache = jnp.arange(cached, dtype=jnp.int32)[None, :] < row_lengths[:, None]
    scores_old = jnp.where(in_cache[:, None, :], scores_old, -1e30)
    scores_recent = (
        jnp.einsum("rhd,srhd->rhs", query_heads, keys_recent, preferred_element_type=jnp.float32)
        * factor
    )
    visible = jnp.arange(step_count, dtype=jnp.int32) <= step_index
    scores_recent = jnp.where(visible[None, None, :], scores_recent, -1e30)
    scores = jnp.concatenate([scores_old, scores_recent], axis=2)
    largest = jnp.max(scores, axis=2, keepdims=True)
    expsum = jnp.exp(scores - largest)
    denominator = jnp.sum(expsum, axis=2)
    probs = expsum.astype(jnp.bfloat16)
    weighted = jnp.einsum(
        "rhc,rchd->rhd", probs[:, :, :cached], values_old, preferred_element_type=jnp.float32
    )
    weighted = weighted + jnp.einsum(
        "rhs,srhd->rhd", probs[:, :, cached:], values_recent, preferred_element_type=jnp.float32
    )
    return (
        (weighted / denominator[:, :, None]).astype(jnp.bfloat16).reshape(row_count, feature_count)
    )


def on_device(
    hidden_in,
    queries,
    new_keys,
    new_values,
    cache_keys,
    cache_values,
    cache_lengths,
    expert_ids,
    router_logits,
    norm_gain,
    out_sectioned,
    expert_sectioned,
    bucket_owner,
):
    step_count, row_block, model_width = hidden_in.shape
    all_rows = queries.shape[1]
    choose_count = expert_ids.shape[2]
    expert_ranks = lax.axis_size("ep")
    replica_ranks = lax.axis_size("rep")
    share_width = model_width // replica_ranks
    owners = bucket_owner[0]
    relaid = lax.all_to_all(expert_sectioned, "rep", split_axis=3, concat_axis=1, tiled=True)
    hidden_share = relaid.shape[3]
    row_blocks = relaid.reshape(replica_ranks, share_width, 3, hidden_share)
    expert_local = jnp.take(row_blocks, owners, axis=0).reshape(model_width, 3, hidden_share)
    gate_weight = expert_local[:, 0]
    up_weight = expert_local[:, 1]
    down_weight = expert_local[:, 2]
    head_list = [
        attention(
            queries[step_index],
            cache_keys,
            cache_values,
            new_keys,
            new_values,
            cache_lengths,
            step_index,
            DH,
        )
        for step_index in range(step_count)
    ]
    head_matrix = jnp.stack(head_list).reshape(step_count * all_rows, -1)
    partials = jnp.dot(
        head_matrix,
        lax.all_gather(out_sectioned, "rep", axis=1, tiled=True),
        preferred_element_type=jnp.float32,
    )
    head_total = lax.psum_scatter(
        partials.reshape(step_count, all_rows, model_width).astype(jnp.bfloat16),
        "ep",
        scatter_dimension=1,
        tiled=True,
    )
    residual = hidden_in.astype(jnp.float32) + head_total.astype(jnp.float32)
    mean_square = jnp.mean(residual * residual, axis=2, keepdims=True)
    normalized = (residual * lax.rsqrt(mean_square + EPSILON) * norm_gain).astype(jnp.bfloat16)
    capacity = min(row_block, max(2, 2 * all_rows * choose_count // (expert_ranks * expert_ranks)))
    chosen = expert_ids.reshape(step_count, row_block * choose_count)
    one_hot = (chosen[:, :, None] == jnp.arange(expert_ranks, dtype=jnp.int32)).astype(jnp.int32)
    earlier_count = jnp.sum((jnp.cumsum(one_hot, axis=1) - one_hot) * one_hot, axis=2)
    step_offset = jnp.arange(step_count, dtype=jnp.int32)[:, None] * capacity
    slot_order = (chosen * (step_count * capacity) + step_offset + earlier_count).reshape(-1)
    slot_count = expert_ranks * step_count * capacity
    placement = (jnp.arange(slot_count, dtype=jnp.int32)[:, None] == slot_order[None, :]).astype(
        jnp.bfloat16
    )
    repeated = jnp.repeat(
        normalized.reshape(step_count * row_block, model_width), choose_count, axis=0
    )
    outgoing = jnp.dot(placement, repeated, preferred_element_type=jnp.float32).astype(jnp.bfloat16)
    outgoing = outgoing.reshape(expert_ranks, step_count * capacity, model_width)
    parcel = lax.all_to_all(outgoing, "ep", split_axis=0, concat_axis=0, tiled=True)
    item_count = parcel.shape[1]
    arrivals = parcel.reshape(-1, model_width)
    gate_value = jnp.dot(arrivals, gate_weight, preferred_element_type=jnp.float32)
    up_value = jnp.dot(arrivals, up_weight, preferred_element_type=jnp.float32)
    activated = (jax.nn.silu(gate_value) * up_value).astype(jnp.bfloat16)
    expert_part = jnp.einsum(
        "nf,df->nd", activated, down_weight, preferred_element_type=jnp.float32
    )
    summed_share = lax.psum_scatter(
        expert_part.astype(jnp.bfloat16), "rep", scatter_dimension=1, tiled=True
    )
    finished = lax.all_gather(summed_share, "rep", axis=1, tiled=True)
    result = lax.all_to_all(
        finished.reshape(expert_ranks, item_count, model_width),
        "ep",
        split_axis=0,
        concat_axis=0,
        tiled=True,
    )
    affinity = jax.nn.sigmoid(router_logits)
    gate_share = ROUTE_SCALE * affinity / jnp.sum(affinity, axis=2, keepdims=True)
    owner_row = jnp.arange(step_count * row_block * choose_count, dtype=jnp.int32) // choose_count
    mixing = jnp.where(
        jnp.arange(step_count * row_block, dtype=jnp.int32)[:, None] == owner_row[None, :],
        gate_share.reshape(-1)[None, :],
        0.0,
    )
    selecting = (slot_order[:, None] == jnp.arange(slot_count, dtype=jnp.int32)[None, :]).astype(
        jnp.float32
    )
    combining = jnp.dot(mixing, selecting, precision=lax.Precision.HIGHEST)
    routed = jnp.dot(
        combining,
        result.reshape(slot_count, -1).astype(jnp.float32),
        precision=lax.Precision.HIGHEST,
    )
    layer_out = (residual + routed.reshape(step_count, row_block, model_width)).astype(jnp.bfloat16)
    return layer_out


def solution(mesh):
    return jax.shard_map(
        on_device,
        mesh=mesh,
        in_specs=(
            P(None, "ep", None),
            P(None, None, "ep"),
            P(None, None, "ep"),
            P(None, None, "ep"),
            P(None, None, "ep"),
            P(None, None, "ep"),
            P(),
            P(None, "ep", None),
            P(None, "ep", None),
            P(),
            P("ep", "rep"),
            P("ep", "rep", None, None),
            P("ep", None),
        ),
        out_specs=P(None, "ep", None),
        check_vma=False,
    )
```

profile of v0, /device:TPU:8, one launch (start us, length us, event | category | flops | bytes accessed | tf_op | source)
XLA Modules:
  0.0 781.2 jit_solution(15184940118133974751)
XLA Ops:
  8.2 1.9 fusion.28
  10.1 1.9 fusion.26
  21.9 71.5 %all-gather.3.cloned.1.call-done = bf16[256,7168]{1,0:T(8,128)(2,1)} async-done(((bf16[256,896]{1,0:T(8,128)(2,1)}), bf16[256,7168]{1,0:T(8,128)(2,1)}) %all-gather.3.cloned.1.call-update) | async-done | bytes 3670032 | tf_op jit(solution)/shard_map/all_gather | solution.py:101
  93.5 3.2 convolution_convert_fusion.2
  96.6 4.7 copy.54
  101.3 11.9 %copy.56 = bf16[1,896,3,1024]{1,2,0,3:T(4,128)(2,1)} copy(bf16[1,896,3,1024]{3,1,2,0:T(8,128)(2,1)} %param.24) | data formatting | bytes 11010048 | tf_op args[11]
  113.2 7.0 all-to-all-start.1
  122.2 271.7 %all-reduce.3.cloned.1.call-done = bf16[4,64,7168]{2,0,1:T(4,128)(2,1)} async-done(((bf16[4,64,7168]{2,0,1:T(4,128)(2,1)}), bf16[4,64,7168]{2,0,1:T(4,128)(2,1)}) %all-reduce.3.cloned.1.call-update) | async-done | bytes 3670032
  396.1 3.0 fusion.1
  399.1 7.3 all-to-all-start
  406.6 11.3 %copy.58 = bf16[1,896,3,8,128]{4,1,2,3,0:T(8,128)(2,1)} copy(bf16[1,896,3,8,128]{1,2,4,3,0:T(4,128)(2,1)} %bitcast.37) | data formatting | bytes 11010048 | tf_op jit(solution)/shard_map/all_to_all | solution.py:78
  417.9 6.2 gather_fusion
  424.1 3.1 copy.59
  427.2 4.9 bitcast_select_fusion
  432.1 59.8 %all-to-all-done = bf16[32,8,7168]{2,1,0:T(8,128)(2,1)} async-done(((bf16[32,8,7168]{2,1,0:T(8,128)(2,1)}), bf16[32,8,7168]{2,1,0:T(8,128)(2,1)}, u32[]{:S(2)}, u32[]{:S(2)}) %all-to-all-start) | async-done | bytes 3670048 | tf_op jit(solution)/shard_map/all_to_all | solution.py:128
  491.9 3.7 fusion.6
  495.6 7.2 convolution_convert_fusion
  502.8 5.9 copy.96
  508.8 80.8 %reduce-scatter.4.cloned.1.call-done = bf16[896,256]{1,0:T(8,128)(2,1)} async-done(((bf16[7168,256]{1,0:T(8,128)(2,1)}), bf16[896,256]{1,0:T(8,128)(2,1)}) %reduce-scatter.4.cloned.1.call-update) | async-done | bytes 458768
  589.5 2.0 copy.97
  591.5 83.6 %all-gather.5.cloned.1.call-done = bf16[256,7168]{1,0:T(8,128)(2,1)} async-done(((bf16[256,896]{1,0:T(8,128)(2,1)}), bf16[256,7168]{1,0:T(8,128)(2,1)}) %all-gather.5.cloned.1.call-update) | async-done | bytes 3670032 | tf_op jit(solution)/shard_map/all_gather | solution.py:140
  675.1 9.7 %all-to-all-start.2 = ((bf16[32,8,7168]{2,1,0:T(8,128)(2,1)}), bf16[32,8,7168]{2,1,0:T(8,128)(2,1)}, u32[]{:S(2)}, u32[]{:S(2)}) async-start(bf16[32,8,7168]{2,1,0:T(8,128)(2,1)} %bitcast.189), calls=%async_computation.2 | async-start | bytes 7340032 | tf_op jit(solution)/shard_map/all_to_all | solution.py:141
  685.2 85.1 %all-to-all-done.2 = bf16[32,8,7168]{2,1,0:T(8,128)(2,1)} async-done(((bf16[32,8,7168]{2,1,0:T(8,128)(2,1)}), bf16[32,8,7168]{2,1,0:T(8,128)(2,1)}, u32[]{:S(2)}, u32[]{:S(2)}) %all-to-all-start.2) | async-done | bytes 3670048 | tf_op jit(solution)/shard_map/all_to_all | solution.py:141
  770.3 3.6 fusion.2
  (131 shorter events, 16.3 us)
Async XLA Ops:
  6.5 10.0 %copy-start = (bf16[64,32,256]{2,1,0:T(8,128)(2,1)S(1)}, bf16[64,32,256]{2,1,0:T(8,128)(2,1)}, u32[]{:S(2)}) copy-start(bf16[64,32,256]{2,1,0:T(8,128)(2,1)} %param.18) | copy-start | bytes 3145732
  6.5 7.0 copy-start.7
  6.5 7.7 copy-start.6
  6.5 86.9 %all-gather.3.cloned.1.call-start = ((), (), s32[]{:S(2)}) async-start(), calls=%async_computation.4 | async-start | bytes 4128768 | tf_op jit(solution)/shard_map/all_gather | solution.py:101
  7.3 386.6 %all-reduce.3.cloned.1.call-start = ((), (), s32[]{:S(2)}) async-start(), calls=%async_computation.7 | async-start | bytes 7340032
  8.2 8.0 %copy-start.3 = (bf16[4,64,256]{2,1,0:T(8,128)(2,1)S(1)}, bf16[4,64,256]{2,1,0:T(8,128)(2,1)}, u32[]{:S(2)}) copy-start(bf16[4,64,256]{2,1,0:T(8,128)(2,1)} %param.16) | copy-start | bytes 393220
  113.2 7.0 copy-start.5
  113.2 7.7 copy-start.10
  113.2 280.6 %copy-start.2 = (bf16[4,2,7168]{2,1,0:T(2,128)(2,1)S(1)}, bf16[4,2,7168]{2,1,0:T(2,128)(2,1)}, u32[]{:S(2)}) copy-start(bf16[4,2,7168]{2,1,0:T(2,128)(2,1)} %param.13) | copy-start | bytes 344068
  113.2 281.7 %copy-start.4 = (f32[7168]{0:T(1024)S(1)}, f32[7168]{0:T(1024)}, u32[]{:S(2)}) copy-start(f32[7168]{0:T(1024)} %param.22) | copy-start | bytes 86020
  113.2 285.9 %all-to-all-start.1 = ((bf16[1,896,3,1024]{1,2,0,3:T(4,128)(2,1)}), bf16[1,896,3,1024]{1,2,0,3:T(4,128)(2,1)}, u32[]{:S(2)}, u32[]{:S(2)}) async-start(bf16[1,896,3,1024]{1,2,0,3:T(4,128)(2,1)} %copy.56), calls=%async_computation.1 | async-start | bytes 14680064 | tf_op jit(solution)/shard_map/all_to_all | solution.py:78
  399.1 7.4 copy-start.9
  399.1 92.8 %all-to-all-start = ((bf16[32,8,7168]{2,1,0:T(8,128)(2,1)}), bf16[32,8,7168]{2,1,0:T(8,128)(2,1)}, u32[]{:S(2)}, u32[]{:S(2)}) async-start(bf16[32,8,7168]{2,1,0:T(8,128)(2,1)} %fusion.1), calls=%async_computation | async-start | bytes 7340032 | tf_op jit(solution)/shard_map/all_to_all | solution.py:128
  406.4 183.1 %reduce-scatter.4.cloned.1.call-start = ((), (), s32[]{:S(2)}) async-start(), calls=%async_computation.6 | async-start | bytes 4128768
  508.7 166.4 %all-gather.5.cloned.1.call-start = ((), (), s32[]{:S(2)}) async-start(), calls=%async_computation.5 | async-start | bytes 4128768 | tf_op jit(solution)/shard_map/all_gather | solution.py:140
  675.1 9.7 %copy-start.8 = (f32[4,2,8]{2,1,0:T(2,128)S(1)}, f32[4,2,8]{2,1,0:T(2,128)}, u32[]{:S(2)}) copy-start(f32[4,2,8]{2,1,0:T(2,128)} %param.21) | copy-start | bytes 772
  675.1 95.2 %all-to-all-start.2 = ((bf16[32,8,7168]{2,1,0:T(8,128)(2,1)}), bf16[32,8,7168]{2,1,0:T(8,128)(2,1)}, u32[]{:S(2)}, u32[]{:S(2)}) async-start(bf16[32,8,7168]{2,1,0:T(8,128)(2,1)} %bitcast.189), calls=%async_computation.2 | async-start | bytes 7340032 | tf_op jit(solution)/shard_map/all_to_all | solution.py:141
  684.8 89.8 %copy-start.1 = (bf16[64,32,256]{2,1,0:T(8,128)(2,1)S(1)}, bf16[64,32,256]{2,1,0:T(8,128)(2,1)}, u32[]{:S(2)}) copy-start(bf16[64,32,256]{2,1,0:T(8,128)(2,1)} %param.18) | copy-start | bytes 3145732
Sparse Core Ops, SparseCore 0:
  9.2 84.2 all-gather.2
  101.5 292.3 all-reduce.2
  508.8 80.6 reduce-scatter.3
  591.7 83.3 all-gather.4
where the time goes:
time: 785 us; the launch traced here: 781 us
  waiting for transfers between devices  653 us (83%)
  local copies, waits for them, and re-layouts  51.3 us (7%)
  matrix products  29.6 us (4%)
  starting transfers between devices  24 us (3%)
  between operations  14.3 us (2%)
  other arithmetic  8.82 us (1%)
    unnamed x6, waiting for transfers between devices  353 us
    all_to_all x1, waiting for transfers between devices, on_device(): lax.all_to_all(finished.reshape(expert_ranks, item_count, model_width), '...  85.1 us
    all_gather x1, waiting for transfers between devices, on_device(): finished = lax.all_gather(summed_share, 'rep', axis=1, tiled=True)  83.6 us
    all_gather x1, waiting for transfers between devices, on_device(): lax.all_gather(out_sectioned, 'rep', axis=1, tiled=True)  71.5 us
    all_to_all x1, waiting for transfers between devices, on_device(): lax.all_to_all(outgoing, 'ep', split_axis=0, concat_axis=0, tiled=True)  59.8 us
    unnamed x26, local copies, waits for them, and re-layouts  20.4 us
  transfers between devices with their start and end apart: 7, of which 6 were waited for; matrix products, arithmetic and copies ran while one was open for 8% of the time, Pallas kernels for 0%

commit v1 on v0

v1 whole, which is shorter than its diff:
```python
import math

import jax
import jax.numpy as jnp
from jax import lax
from jax.sharding import PartitionSpec as P

DH = 128
ROUTE_SCALE = 2.827
EPSILON = 1e-06


def attention(queries, cache_keys, cache_values, new_keys, new_values, lengths):
    steps, rows, width = queries.shape
    heads = width // DH
    cached = cache_keys.shape[1]
    q = queries.reshape(steps, rows, heads, DH)
    ko = cache_keys.reshape(rows, cached, heads, DH)
    vo = cache_values.reshape(rows, cached, heads, DH)
    kn = new_keys.reshape(steps, rows, heads, DH)
    vn = new_values.reshape(steps, rows, heads, DH)
    factor = 1.0 / math.sqrt(DH)
    so = jnp.einsum("trhd,rchd->rhtc", q, ko, preferred_element_type=jnp.float32) * factor
    sn = jnp.einsum("trhd,srhd->rhts", q, kn, preferred_element_type=jnp.float32) * factor
    live = jnp.arange(cached, dtype=jnp.int32)[None, :] < lengths[:, None]
    so = jnp.where(live[:, None, None, :], so, -1e30)
    order = jnp.arange(steps, dtype=jnp.int32)
    sn = jnp.where(order[None, :] <= order[:, None], sn, -1e30)
    scores = jnp.concatenate([so, sn], axis=3)
    e = jnp.exp(scores - jnp.max(scores, axis=3, keepdims=True))
    total = jnp.sum(e, axis=3)
    p = e.astype(jnp.bfloat16)
    w = jnp.einsum("rhtc,rchd->rthd", p[..., :cached], vo, preferred_element_type=jnp.float32)
    w = w + jnp.einsum("rhts,srhd->rthd", p[..., cached:], vn, preferred_element_type=jnp.float32)
    w = w / jnp.transpose(total, (0, 2, 1))[..., None]
    return w.astype(jnp.bfloat16).reshape(rows, steps, width)


def on_device(
    hidden_in,
    queries,
    new_keys,
    new_values,
    cache_keys,
    cache_values,
    cache_lengths,
    expert_ids,
    router_logits,
    norm_gain,
    out_sectioned,
    expert_sectioned,
    bucket_owner,
):
    steps, own_rows, width = hidden_in.shape
    rows = queries.shape[1]
    n_ep = lax.axis_size("ep")
    n_rep = lax.axis_size("rep")
    block = width // n_rep
    mine = own_rows * steps
    me = lax.axis_index("rep")
    owners = lax.all_to_all(
        jnp.broadcast_to(bucket_owner, (n_ep, n_rep)), "ep", 0, 0, tiled=True
    )
    bucket = jnp.argmax(owners == me, axis=1).astype(jnp.int32)
    heads = attention(queries, cache_keys, cache_values, new_keys, new_values, cache_lengths)
    partial = jnp.dot(
        heads.reshape(rows * steps, -1), out_sectioned, preferred_element_type=jnp.float32
    ).astype(jnp.bfloat16)
    parts = lax.all_to_all(partial.reshape(n_ep, mine, block), "ep", 0, 0, tiled=True)
    attended = jnp.sum(parts.astype(jnp.float32), axis=0).astype(jnp.bfloat16)
    attended = lax.all_to_all(
        jnp.broadcast_to(attended, (n_rep, mine, block)), "rep", 0, 0, tiled=True
    )
    own = jnp.transpose(hidden_in, (1, 0, 2)).reshape(mine, n_rep, block)
    residual = jnp.transpose(own, (1, 0, 2)).astype(jnp.float32) + attended.astype(jnp.float32)
    mean_square = jnp.sum(residual * residual, axis=(0, 2), keepdims=True) / width
    gain = norm_gain.reshape(n_rep, 1, block)
    normalized = (residual * lax.rsqrt(mean_square + EPSILON) * gain).astype(jnp.bfloat16)
    arrivals = lax.all_to_all(jnp.take(normalized, bucket, axis=0), "ep", 0, 0, tiled=True)
    arrivals = arrivals.reshape(n_ep * mine, block)
    weight = expert_sectioned[0]
    gate = jnp.dot(arrivals, weight[:, 0], preferred_element_type=jnp.float32)
    up = jnp.dot(arrivals, weight[:, 1], preferred_element_type=jnp.float32)
    both = jnp.concatenate([gate.astype(jnp.bfloat16), up.astype(jnp.bfloat16)], axis=1)
    hidden = gate.shape[1]
    both = lax.all_to_all(both.reshape(n_rep, -1, 2 * hidden), "rep", 0, 0, tiled=True)
    both = jnp.sum(both.astype(jnp.float32), axis=0)
    activated = (jax.nn.silu(both[:, :hidden]) * both[:, hidden:]).astype(jnp.bfloat16)
    activated = lax.all_to_all(
        jnp.broadcast_to(activated, (n_rep,) + activated.shape), "rep", 0, 0, tiled=True
    ).reshape(-1, hidden)
    out = jnp.einsum("nf,df->nd", activated, weight[:, 2], preferred_element_type=jnp.float32)
    out = out.astype(jnp.bfloat16).reshape(n_ep, mine, block)
    back = lax.all_to_all(out, "ep", 0, 0, tiled=True)
    affinity = jax.nn.sigmoid(router_logits)
    share = ROUTE_SCALE * affinity / jnp.sum(affinity, axis=2, keepdims=True)
    chosen = expert_ids[..., None] == jnp.arange(n_ep, dtype=jnp.int32)
    share = jnp.sum(jnp.where(chosen, share[..., None], 0.0), axis=2)
    share = jnp.transpose(share, (2, 1, 0)).reshape(n_ep, mine, 1)
    scaled = back.astype(jnp.float32) * share
    place = (bucket[None, :] == jnp.arange(n_rep, dtype=jnp.int32)[:, None]).astype(jnp.float32)
    routed = jnp.dot(
        place, scaled.reshape(n_ep, -1), precision=lax.Precision.HIGHEST
    ).astype(jnp.bfloat16)
    routed = lax.all_to_all(
        jnp.broadcast_to(routed, (n_rep,) + routed.shape), "rep", 0, 0, tiled=True
    )
    routed = jnp.sum(routed.astype(jnp.float32), axis=0).reshape(n_rep, mine, block)
    out = jnp.transpose((residual + routed).astype(jnp.bfloat16), (1, 0, 2))
    return jnp.transpose(out.reshape(own_rows, steps, width), (1, 0, 2))


def solution(mesh):
    return jax.shard_map(
        on_device,
        mesh=mesh,
        in_specs=(
            P(None, "ep", None),
            P(None, None, "ep"),
            P(None, None, "ep"),
            P(None, None, "ep"),
            P(None, None, "ep"),
            P(None, None, "ep"),
            P(),
            P(None, "ep", None),
            P(None, "ep", None),
            P(),
            P("ep", "rep"),
            P("ep", "rep", None, None),
            P("ep", None),
        ),
        out_specs=P(None, "ep", None),
        check_vma=False,
    )
```

time: 785 us -> 162 us (0.21)
  waiting for transfers between devices: 653 us -> 42.1 us
  blocking collectives: 0 us -> 65.7 us
  local copies, waits for them, and re-layouts: 51.3 us -> 7.5 us
  matrix products: 29.6 us -> 12.1 us
  between operations: 14.3 us -> 0.32 us
    unnamed x6 -> x0, waiting for transfers between devices: 353 us -> none
    all_gather x2 -> x0, waiting for transfers between devices: 155 us -> none  [the longest x1 83.6 us: on_device(): finished = lax.all_gather(summed_share, 'rep', axis=1, tiled=True)]
    all_to_all x3 -> x4, waiting for transfers between devices: 145 us -> 42.1 us  [the longest x1 18.4 us: on_device(): back = lax.all_to_all(out, 'ep', 0, 0, tiled=True)]
    all_to_all x0 -> x4, blocking collectives: none -> 65.7 us  [the longest x1 21.7 us: on_device(): lax.all_to_all(jnp.take(normalized, bucket, axis=0), 'ep', 0, 0, tiled=True)]
    unnamed x26 -> x13, local copies, waits for them, and re-layouts: 20.4 us -> 0.7 us
    dot_general x22 -> x9, matrix products: 29.6 us -> 12.1 us  [the longest x1 3.04 us: on_device(): jnp.einsum('nf,df->nd', activated, weight[:, 2], preferred_element_type=j...]
    all_to_all x1, local copies, waits for them, and re-layouts: 11.3 us -> 0.07 us  [on_device(): lax.all_to_all(jnp.broadcast_to(bucket_owner, (n_ep, n_rep)), 'ep', 0, 0,...]
    gather x2 -> x1, local copies, waits for them, and re-layouts: 9.28 us -> 0.63 us  [on_device(): jnp.take(normalized, bucket, axis=0)]
  transfers between devices with their start and end apart: 7 -> 4, of which waited for: 6 -> 4; matrix products, arithmetic and copies ran while one was open for 8% -> 6% of each run, Pallas kernels for 0% -> 0%
where the time goes in v1:
time: 162 us
  blocking collectives  65.7 us (41%)
  waiting for transfers between devices  42.1 us (26%)
  starting transfers between devices  30.5 us (19%)
  matrix products  12.1 us (7%)
  local copies, waits for them, and re-layouts  7.5 us (5%)
  other arithmetic  3.24 us (2%)
    all_to_all x1, blocking collectives, on_device(): lax.all_to_all(jnp.take(normalized, bucket, axis=0), 'ep', 0, 0, tiled=True)  21.7 us
    all_to_all x1, waiting for transfers between devices, on_device(): back = lax.all_to_all(out, 'ep', 0, 0, tiled=True)  18.4 us
    all_to_all x1, waiting for transfers between devices, on_device(): lax.all_to_all(partial.reshape(n_ep, mine, block), 'ep', 0, 0, tiled=True)  17.7 us
    all_to_all x1, blocking collectives, on_device(): lax.all_to_all(both.reshape(n_rep, -1, 2 * hidden), 'rep', 0, 0, tiled=True)  16.9 us
    all_to_all x1, blocking collectives, on_device(): lax.all_to_all(jnp.broadcast_to(routed, (n_rep,) + routed.shape), 'rep',...  15.9 us
    all_to_all x1, blocking collectives, on_device(): lax.all_to_all(jnp.broadcast_to(activated, (n_rep,) + activated.shape), '...  11.2 us
    all_to_all x1, starting transfers between devices, on_device(): lax.all_to_all(jnp.broadcast_to(bucket_owner, (n_ep, n_rep)), 'ep', 0, 0,...  10.6 us
    all_to_all x1, starting transfers between devices, on_device(): lax.all_to_all(partial.reshape(n_ep, mine, block), 'ep', 0, 0, tiled=True)  9.1 us
  transfers between devices with their start and end apart: 4, of which 4 were waited for; matrix products, arithmetic and copies ran while one was open for 6% of the time, Pallas kernels for 0%

profile of v1, /device:TPU:8, one launch (start us, length us, event | category | flops | bytes accessed | tf_op | source)
XLA Modules:
  0.0 161.5 jit_solution(4723462793506031231)
XLA Ops:
  0.0 1.4 broadcast_in_dim.77
  1.4 10.6 %all-to-all-start.2 = ((s32[32,1,8]{2,1,0:T(1,128)}), s32[32,1,8]{2,1,0:T(1,128)S(1)}, u32[]{:S(2)}, u32[]{:S(2)}) async-start(s32[32,1,8]{2,1,0:T(1,128)} %broadcast_in_dim.77), calls=%async_computation.2 | async-start | bytes 32768 | tf_op jit(solution)/shard_map/all_to_all | solution.py:61
  12.0 0.9 reshape.94
  12.9 0.9 reshape.96
  13.9 0.7 iota_compare_fusion.1
  14.6 0.9 reshape.98
  16.0 2.0 %fusion.36 = (f32[64,2,4]{2,1,0:T(2,128)S(1)}, f32[64,2,4,32]{3,2,1,0:T(4,128)S(1)}) fusion(bf16[4,64,2,128]{3,2,1,0:T(2,128)(2,1)S(1)} %reshape.94, pred[64,32]{1,0:T(8,128)(4,1)S(1)} %iota_compare_fusion.1, bf16[64,32,256]{2,1,0:T(8,128)(2,1)} %param.17), kind=kOutput, calls=%fused_computation.69 | convolution fusion | flops 4242944 | bytes 1249280 | tf_op jit(solution)/shard_map/trhd,rchd->rhtc/dot_general | solution.py:23
  20.0 1.1 fusion.6
  21.1 0.7 all-to-all-done.2
  21.8 9.1 %all-to-all-start = ((bf16[32,8,896]{2,1,0:T(8,128)(2,1)}), bf16[32,8,896]{2,1,0:T(8,128)(2,1)S(1)}, u32[]{:S(2)}, u32[]{:S(2)}) async-start(bf16[32,8,896]{2,1,0:T(8,128)(2,1)} %fusion.6), calls=%async_computation | async-start | bytes 917504 | tf_op jit(solution)/shard_map/all_to_all | solution.py:69
  31.8 17.7 %all-to-all-done = bf16[32,8,896]{2,1,0:T(8,128)(2,1)S(1)} async-done(((bf16[32,8,896]{2,1,0:T(8,128)(2,1)}), bf16[32,8,896]{2,1,0:T(8,128)(2,1)S(1)}, u32[]{:S(2)}, u32[]{:S(2)}) %all-to-all-start) | async-done | bytes 458784 | tf_op jit(solution)/shard_map/all_to_all | solution.py:69
  49.7 0.7 broadcast_in_dim.76
  50.3 5.8 %all-to-all-start.1 = ((bf16[8,8,896]{2,1,0:T(8,128)(2,1)}), bf16[8,8,896]{2,1,0:T(8,128)(2,1)S(1)}, u32[]{:S(2)}, u32[]{:S(2)}) async-start(bf16[8,8,896]{2,1,0:T(8,128)(2,1)} %broadcast_in_dim.76), calls=%async_computation.1 | async-start | bytes 229376 | tf_op jit(solution)/shard_map/all_to_all | solution.py:71
  56.1 5.3 %all-to-all-done.1 = bf16[8,8,896]{2,1,0:T(8,128)(2,1)S(1)} async-done(((bf16[8,8,896]{2,1,0:T(8,128)(2,1)}), bf16[8,8,896]{2,1,0:T(8,128)(2,1)S(1)}, u32[]{:S(2)}, u32[]{:S(2)}) %all-to-all-start.1) | async-done | bytes 114720 | tf_op jit(solution)/shard_map/all_to_all | solution.py:71
  62.5 21.7 %all_to_all.41 = bf16[32,8,896]{2,1,0:T(8,128)(2,1)S(1)} all-to-all(bf16[32,8,896]{2,1,0:T(8,128)(2,1)S(1)} %broadcast_select_fusion), channel_id=1, replica_groups=mesh['rep'=8,'ep'=32] {'ep'}, dimensions={0} | all-to-all | bytes 917504 | tf_op jit(solution)/shard_map/all_to_all | solution.py:79
  84.1 2.2 %fusion.3 = bf16[256,1024]{1,0:T(8,128)(2,1)S(1)} fusion(bf16[896,3,1024]{2,0,1:T(8,128)(2,1)} %bitcast.98, bf16[32,8,896]{2,1,0:T(8,128)(2,1)S(1)} %all_to_all.41), kind=kOutput, calls=%fused_computation.10 | convolution fusion | flops 470024192 | bytes 2818048 | tf_op jit(solution)/shard_map/dot_general | solution.py:82
  86.4 2.2 %fusion.4 = bf16[256,1024]{1,0:T(8,128)(2,1)S(1)} fusion(bf16[896,3,1024]{2,0,1:T(8,128)(2,1)} %bitcast.99, bf16[32,8,896]{2,1,0:T(8,128)(2,1)S(1)} %all_to_all.41), kind=kOutput, calls=%fused_computation.11 | convolution fusion | flops 470024192 | bytes 2818048 | tf_op jit(solution)/shard_map/dot_general | solution.py:83
  88.7 16.9 %all_to_all.42 = bf16[8,32,2048]{2,1,0:T(8,128)(2,1)S(1)} all-to-all(bf16[8,32,2048]{2,1,0:T(8,128)(2,1)S(1)} %bitcast.87), channel_id=1, replica_groups=mesh['rep'=8,'ep'=32] {'rep'}, dimensions={0} | all-to-all | bytes 2097152 | tf_op jit(solution)/shard_map/all_to_all | solution.py:86
  105.9 11.2 %all_to_all.43 = bf16[8,32,1024]{2,1,0:T(8,128)(2,1)S(1)} all-to-all(bf16[8,32,1024]{2,1,0:T(8,128)(2,1)S(1)} %broadcast_in_dim.81), channel_id=1, replica_groups=mesh['rep'=8,'ep'=32] {'rep'}, dimensions={0} | all-to-all | bytes 1048576 | tf_op jit(solution)/shard_map/all_to_all | solution.py:89
  117.1 3.0 %fusion.7 = bf16[32,8,896]{2,1,0:T(8,128)(2,1)} fusion(bf16[256,1024]{1,0:T(8,128)(2,1)S(1)} %bitcast.91, bf16[896,3,1024]{2,0,1:T(8,128)(2,1)} %bitcast.100), kind=kOutput, calls=%fused_computation.15 | convolution fusion | flops 469991424 | bytes 2818048 | tf_op jit(solution)/shard_map/nf,df->nd/dot_general | solution.py:92
  120.1 5.0 %all-to-all-start.6 = ((bf16[32,8,896]{2,1,0:T(8,128)(2,1)}), bf16[32,8,896]{2,1,0:T(8,128)(2,1)S(1)}, u32[]{:S(2)}, u32[]{:S(2)}) async-start(bf16[32,8,896]{2,1,0:T(8,128)(2,1)} %fusion.7), calls=%async_computation.6 | async-start | bytes 917504 | tf_op jit(solution)/shard_map/all_to_all | solution.py:94
  125.5 18.4 %all-to-all-done.6 = bf16[32,8,896]{2,1,0:T(8,128)(2,1)S(1)} async-done(((bf16[32,8,896]{2,1,0:T(8,128)(2,1)}), bf16[32,8,896]{2,1,0:T(8,128)(2,1)S(1)}, u32[]{:S(2)}, u32[]{:S(2)}) %all-to-all-start.6) | async-done | bytes 458784 | tf_op jit(solution)/shard_map/all_to_all | solution.py:94
  144.6 15.9 %all_to_all.44 = bf16[8,8,7168]{2,1,0:T(8,128)(2,1)S(1)} all-to-all(bf16[8,8,7168]{2,1,0:T(8,128)(2,1)S(1)} %broadcast_in_dim.84), channel_id=1, replica_groups=mesh['rep'=8,'ep'=32] {'rep'}, dimensions={0} | all-to-all | bytes 1835008 | tf_op jit(solution)/shard_map/all_to_all | solution.py:105
  160.8 0.7 copy.58
  (50 shorter events, 6.0 us)
Async XLA Ops:
  0.0 18.6 %copy-start = (bf16[64,32,256]{2,1,0:T(8,128)(2,1)S(1)}, bf16[64,32,256]{2,1,0:T(8,128)(2,1)}, u32[]{:S(2)}) copy-start(bf16[64,32,256]{2,1,0:T(8,128)(2,1)} %param.18) | copy-start | bytes 3145732
  1.4 20.4 %all-to-all-start.2 = ((s32[32,1,8]{2,1,0:T(1,128)}), s32[32,1,8]{2,1,0:T(1,128)S(1)}, u32[]{:S(2)}, u32[]{:S(2)}) async-start(s32[32,1,8]{2,1,0:T(1,128)} %broadcast_in_dim.77), calls=%async_computation.2 | async-start | bytes 32768 | tf_op jit(solution)/shard_map/all_to_all | solution.py:61
  19.0 1.0 copy-start.1
  19.4 11.5 %copy-start.2 = (bf16[4,2,7168]{2,1,0:T(2,128)(2,1)S(1)}, bf16[4,2,7168]{2,1,0:T(2,128)(2,1)}, u32[]{:S(2)}) copy-start(bf16[4,2,7168]{2,1,0:T(2,128)(2,1)} %param.13) | copy-start | bytes 344068
  19.4 11.8 %copy-start.3 = (f32[7168]{0:T(1024)S(1)}, f32[7168]{0:T(1024)}, u32[]{:S(2)}) copy-start(f32[7168]{0:T(1024)} %param.22) | copy-start | bytes 86020
  21.8 27.8 %all-to-all-start = ((bf16[32,8,896]{2,1,0:T(8,128)(2,1)}), bf16[32,8,896]{2,1,0:T(8,128)(2,1)S(1)}, u32[]{:S(2)}, u32[]{:S(2)}) async-start(bf16[32,8,896]{2,1,0:T(8,128)(2,1)} %fusion.6), calls=%async_computation | async-start | bytes 917504 | tf_op jit(solution)/shard_map/all_to_all | solution.py:69
  50.3 11.1 %all-to-all-start.1 = ((bf16[8,8,896]{2,1,0:T(8,128)(2,1)}), bf16[8,8,896]{2,1,0:T(8,128)(2,1)S(1)}, u32[]{:S(2)}, u32[]{:S(2)}) async-start(bf16[8,8,896]{2,1,0:T(8,128)(2,1)} %broadcast_in_dim.76), calls=%async_computation.1 | async-start | bytes 229376 | tf_op jit(solution)/shard_map/all_to_all | solution.py:71
  117.1 8.1 %copy-start.5 = (f32[4,2,8]{2,1,0:T(2,128)S(1)}, f32[4,2,8]{2,1,0:T(2,128)}, u32[]{:S(2)}) copy-start(f32[4,2,8]{2,1,0:T(2,128)} %param.21) | copy-start | bytes 772
  117.1 8.2 %copy-start.4 = (s32[4,2,8]{2,1,0:T(2,128)S(1)}, s32[4,2,8]{2,1,0:T(2,128)}, u32[]{:S(2)}) copy-start(s32[4,2,8]{2,1,0:T(2,128)} %param.20) | copy-start | bytes 772
  120.1 23.7 %all-to-all-start.6 = ((bf16[32,8,896]{2,1,0:T(8,128)(2,1)}), bf16[32,8,896]{2,1,0:T(8,128)(2,1)S(1)}, u32[]{:S(2)}, u32[]{:S(2)}) async-start(bf16[32,8,896]{2,1,0:T(8,128)(2,1)} %fusion.7), calls=%async_computation.6 | async-start | bytes 917504 | tf_op jit(solution)/shard_map/all_to_all | solution.py:94

commit v2 on v1

v2 whole, which is shorter than its diff:
```python
import math

import jax
import jax.numpy as jnp
from jax import lax
from jax.experimental import pallas as pl
from jax.experimental.pallas import tpu as pltpu
from jax.sharding import PartitionSpec as P

DH = 128
ROUTE_SCALE = 2.827
EPSILON = 1e-06
GROUP = 16
NEVER = -1e30
VMEM = pltpu.VMEM
SMEM = pltpu.SMEM
F32 = jnp.float32
BF16 = jnp.bfloat16


def dot_nt(a, b):
    return lax.dot_general(a, b, (((1,), (1,)), ((), ())), preferred_element_type=F32)


def attention_kernel(
    info_ref, q_ref, kn_ref, vn_ref, ck_ref, cv_ref, len_ref, out_ref, keep_ref, send_ref, heads
):
    g = pl.program_id(0)
    steps, _, width = q_ref.shape
    cached = ck_ref.shape[1]
    m = steps * GROUP
    n = GROUP * cached
    factor = 1.0 / math.sqrt(DH)
    row = lax.broadcasted_iota(jnp.int32, (m, n), 0)
    col = lax.broadcasted_iota(jnp.int32, (m, n), 1)
    lengths = jnp.concatenate([len_ref[...]] * steps, axis=0)
    live = (col // cached == row % GROUP) & (col % cached < lengths)
    row = lax.broadcasted_iota(jnp.int32, (m, m), 0)
    col = lax.broadcasted_iota(jnp.int32, (m, m), 1)
    recent = (col % GROUP == row % GROUP) & (col // GROUP <= row // GROUP)
    for h in range(width // DH):
        cut = slice(h * DH, (h + 1) * DH)
        q = q_ref[:, :, cut].reshape(m, DH)
        so = dot_nt(q, ck_ref[:, :, cut].reshape(n, DH)) * factor
        sn = dot_nt(q, kn_ref[:, :, cut].reshape(m, DH)) * factor
        so = jnp.where(live, so, NEVER)
        sn = jnp.where(recent, sn, NEVER)
        top = jnp.maximum(
            jnp.max(so, axis=1, keepdims=True), jnp.max(sn, axis=1, keepdims=True)
        )
        eo = jnp.exp(so - top)
        en = jnp.exp(sn - top)
        total = jnp.sum(eo, axis=1, keepdims=True) + jnp.sum(en, axis=1, keepdims=True)
        w = jnp.dot(
            eo.astype(BF16), cv_ref[:, :, cut].reshape(n, DH), preferred_element_type=F32
        ) + jnp.dot(
            en.astype(BF16), vn_ref[:, :, cut].reshape(m, DH), preferred_element_type=F32
        )
        heads[:, pl.ds(g * GROUP, GROUP), cut] = (w / total).astype(BF16).reshape(steps, GROUP, DH)

    @pl.when(g == pl.num_programs(0) - 1)
    def _():
        rows = heads.shape[1]
        every = steps * rows
        half = every // 2
        mine = keep_ref.shape[1]
        own = mine // steps
        parity = info_ref[0]
        j = lax.broadcasted_iota(jnp.int32, (every, every), 0)
        source = lax.broadcasted_iota(jnp.int32, (every, every), 1)
        side = j // half
        chip = (j % half) // mine
        step = (j % mine) // own
        core = jnp.where(side == 0, parity, 1 - parity)
        wanted = step * rows + (chip * 2 + core) * own + j % own
        order = jnp.where(source == wanted, 1.0, 0.0).astype(BF16)
        h = jnp.dot(order, heads[...].reshape(every, width), preferred_element_type=F32)
        part = jnp.dot(h.astype(BF16), out_ref[...], preferred_element_type=F32).astype(BF16)
        block = out_ref.shape[1]
        chips = half // mine
        keep_ref[:, :, :block] = part[:half].reshape(chips, mine, block)
        send_ref[:, :, :block] = part[half:].reshape(chips, mine, block)
        extra = keep_ref.shape[2] - block
        lane = lax.broadcasted_iota(jnp.int32, (chips, mine, extra), 2)
        bucket = info_ref[1]
        keep_ref[:, :, block:] = jnp.where(lane == 0, bucket, 0).astype(F32).astype(BF16)
        send_ref[:, :, block:] = jnp.where(lane == 1, bucket, 0).astype(F32).astype(BF16)


def attention(info, queries, new_keys, new_values, cache_keys, cache_values, lengths, out, chips):
    steps, rows, width = queries.shape
    cached = cache_keys.shape[1]
    block = out.shape[1]
    mine = steps * rows // (2 * chips)
    fresh = pl.BlockSpec((steps, GROUP, width), lambda g: (0, g, 0))
    old = pl.BlockSpec((GROUP, cached, width), lambda g: (g, 0, 0))
    shape = (chips, mine, block + 128)
    whole = pl.BlockSpec(shape, lambda g: (0, 0, 0))
    return pl.pallas_call(
        attention_kernel,
        grid=(rows // GROUP,),
        in_specs=[
            pl.BlockSpec(memory_space=SMEM),
            fresh,
            fresh,
            fresh,
            old,
            old,
            pl.BlockSpec((GROUP, 1), lambda g: (g, 0)),
            pl.BlockSpec(out.shape, lambda g: (0, 0)),
        ],
        out_specs=[whole, whole],
        out_shape=[jax.ShapeDtypeStruct(shape, BF16)] * 2,
        scratch_shapes=[VMEM((steps, rows, width), BF16)],
        name="attention",
    )(info, queries, new_keys, new_values, cache_keys, cache_values, lengths, out)


def select_kernel(bucket_ref, att_ref, hid_ref, gain_ref, out_ref, res, norm):
    blocks, rows, block = att_ref.shape
    total = jnp.zeros((rows, block), F32)
    for b in range(blocks):
        x = att_ref[b].astype(F32) + hid_ref[:, b * block : (b + 1) * block].astype(F32)
        res[b] = x
        total = total + x * x
    mean = jnp.sum(total, axis=1, keepdims=True) / (blocks * block)
    scale = lax.rsqrt(mean + EPSILON)
    for b in range(blocks):
        gain = gain_ref[:, b * block : (b + 1) * block]
        norm[b] = (res[b] * scale * gain).astype(BF16)
    for c in range(out_ref.shape[0]):
        out_ref[c] = norm[bucket_ref[c]]


def select(buckets, att, hid, gain):
    blocks, rows, block = att.shape
    chips = buckets.shape[0]
    vm = pl.BlockSpec(memory_space=VMEM)
    return pl.pallas_call(
        select_kernel,
        in_specs=[pl.BlockSpec(memory_space=SMEM), vm, vm, vm],
        out_specs=vm,
        out_shape=jax.ShapeDtypeStruct((chips, rows, block), BF16),
        scratch_shapes=[VMEM(att.shape, F32), VMEM(att.shape, BF16)],
        name="select",
    )(buckets, att, hid, gain)


def gate_up_kernel(x_ref, w_ref, out_ref):
    out_ref[...] = jnp.dot(x_ref[...], w_ref[0], preferred_element_type=F32).astype(BF16)


def gate_up(x, weight, tile=512):
    rows, block = x.shape
    hidden = weight.shape[2]
    per = hidden // tile
    return pl.pallas_call(
        gate_up_kernel,
        grid=(2 * per,),
        in_specs=[
            pl.BlockSpec((rows, block), lambda j: (0, 0)),
            pl.BlockSpec((1, block, tile), lambda j: (j // per, 0, j % per)),
        ],
        out_specs=pl.BlockSpec((rows, tile), lambda j: (0, j)),
        out_shape=jax.ShapeDtypeStruct((rows, 2 * hidden), BF16),
        name="gate_up",
    )(x, weight)


def down_kernel(x_ref, w_ref, out_ref):
    out_ref[...] = dot_nt(x_ref[...], w_ref[0]).astype(BF16)


def down(x, weight):
    rows, hidden = x.shape
    block = weight.shape[1]
    return pl.pallas_call(
        down_kernel,
        grid=(1,),
        in_specs=[
            pl.BlockSpec((rows, hidden), lambda j: (0, 0)),
            pl.BlockSpec((1, block, hidden), lambda j: (2, 0, 0)),
        ],
        out_specs=pl.BlockSpec((rows, block), lambda j: (0, 0)),
        out_shape=jax.ShapeDtypeStruct((rows, block), BF16),
        name="down",
    )(x, weight)


def combine_kernel(bucket_ref, share_ref, keep_ref, got_ref, out_ref, acc):
    acc[...] = jnp.zeros_like(acc)
    chips = keep_ref.shape[0]
    share = share_ref[...]
    for side, ref in enumerate((keep_ref, got_ref)):
        for c in range(chips):
            e = side * chips + c
            b = bucket_ref[e]
            acc[b] = acc[b] + share[:, e : e + 1] * ref[c].astype(F32)
    done = acc[...].astype(BF16)
    for r in range(out_ref.shape[0]):
        out_ref[r] = done


def combine(buckets, share, keep, got, ranks):
    _, rows, block = keep.shape
    vm = pl.BlockSpec(memory_space=VMEM)
    return pl.pallas_call(
        combine_kernel,
        in_specs=[pl.BlockSpec(memory_space=SMEM), vm, vm, vm],
        out_specs=vm,
        out_shape=jax.ShapeDtypeStruct((ranks, ranks, rows, block), BF16),
        scratch_shapes=[VMEM((ranks, rows, block), F32)],
        name="combine",
    )(buckets, share, keep, got)


def on_device(
    hidden_in,
    queries,
    new_keys,
    new_values,
    cache_keys,
    cache_values,
    cache_lengths,
    expert_ids,
    router_logits,
    norm_gain,
    out_sectioned,
    expert_sectioned,
    bucket_owner,
):
    steps, own_rows, width = hidden_in.shape
    n_ep = lax.axis_size("ep")
    n_rep = lax.axis_size("rep")
    chips = n_ep // 2
    block = width // n_rep
    mine = own_rows * steps
    rank = lax.axis_index("rep")
    parity = lax.axis_index("ep") % 2
    pair = [(j, j ^ 1) for j in range(n_ep)]
    cores = [[j for j in range(n_ep) if j % 2 == k] for k in range(2)]

    def swap(x):
        return lax.ppermute(x, "ep", pair)

    def across(x):
        return lax.all_to_all(x, "ep", 0, 0, tiled=True, axis_index_groups=cores)

    def over_rep(x):
        return lax.all_to_all(x, "rep", 0, 0, tiled=True)

    bucket = jnp.argmax(bucket_owner[0] == rank).astype(jnp.int32)
    info = jnp.stack([parity, bucket])
    own_hidden = hidden_in.reshape(mine, width)
    keep, send = attention(
        info,
        queries,
        new_keys,
        new_values,
        cache_keys,
        cache_values,
        cache_lengths[:, None],
        out_sectioned,
        chips,
    )
    both = (keep.astype(F32) + swap(send).astype(F32)).astype(BF16)
    parts = across(both)
    buckets = parts[:, 0, block : block + 2].astype(jnp.int32).T
    attended = jnp.sum(parts[:, :, :block].astype(F32), axis=0).astype(BF16)
    attended = jnp.concatenate([attended, swap(attended)], axis=0)
    attended = over_rep(jnp.broadcast_to(attended, (n_rep,) + attended.shape))
    hidden16 = jnp.concatenate([own_hidden, swap(own_hidden)], axis=0)
    chosen = select(buckets[0], attended, hidden16, norm_gain.reshape(1, width))
    arrivals = across(chosen).reshape(-1, block)
    weight = jnp.transpose(expert_sectioned[0], (1, 0, 2))
    hidden = weight.shape[2]
    partial = gate_up(arrivals, weight)
    partial = over_rep(partial.reshape(n_rep, -1, 2 * hidden))
    partial = jnp.sum(partial.astype(F32), axis=0)
    activated = (jax.nn.silu(partial[:, :hidden]) * partial[:, hidden:]).astype(BF16)
    activated = over_rep(jnp.broadcast_to(activated, (n_rep,) + activated.shape))
    result = down(activated.reshape(-1, hidden), weight)
    back = across(result.reshape(chips, 2 * mine, block))
    affinity = jax.nn.sigmoid(router_logits)
    share = ROUTE_SCALE * affinity / jnp.sum(affinity, axis=2, keepdims=True)
    picked = expert_ids[..., None] == jnp.arange(n_ep, dtype=jnp.int32)
    share = jnp.sum(jnp.where(picked, share[..., None], 0.0), axis=2).reshape(mine, chips, 2)
    share = jnp.where(parity == 0, share, share[:, :, ::-1])
    share = jnp.transpose(share, (0, 2, 1)).reshape(mine, n_ep)
    routed = combine(buckets.reshape(-1), share, back[:, :mine], swap(back[:, mine:]), n_rep)
    routed = over_rep(routed)
    routed = jnp.sum(routed.astype(F32), axis=0)
    residual = jnp.transpose(own_hidden.reshape(mine, n_rep, block), (1, 0, 2)).astype(F32)
    residual = residual + attended[:, :mine].astype(F32)
    out = jnp.transpose((residual + routed).astype(BF16), (1, 0, 2))
    return out.reshape(steps, own_rows, width)


def solution(mesh):
    return jax.shard_map(
        on_device,
        mesh=mesh,
        in_specs=(
            P(None, "ep", None),
            P(None, None, "ep"),
            P(None, None, "ep"),
            P(None, None, "ep"),
            P(None, None, "ep"),
            P(None, None, "ep"),
            P(),
            P(None, "ep", None),
            P(None, "ep", None),
            P(),
            P("ep", "rep"),
            P("ep", "rep", None, None),
            P("ep", None),
        ),
        out_specs=P(None, "ep", None),
        check_vma=False,
    )
```

time: 162 us -> 156 us (0.963)
  Pallas kernels: 0 us -> 18.3 us
  blocking collectives: 65.7 us -> 47.7 us
  matrix products: 12.1 us -> 0 us
  waiting for transfers between devices: 42.1 us -> 47.7 us
  starting transfers between devices: 30.5 us -> 27.5 us
  other arithmetic: 3.24 us -> 5.78 us
    pallas_call x0 -> x5, Pallas kernels: none -> 18.3 us  [the longest x1 5.81 us: attention(): pl.pallas_call(attention_kernel, grid=(rows // GROUP,), in_specs=[pl.Bloc...]
    all_to_all x4 -> x3, blocking collectives: 65.7 us -> 47.7 us  [the longest x2 28.6 us: over_rep(): return lax.all_to_all(x, 'rep', 0, 0, tiled=True)]
    dot_general x9 -> x0, matrix products: 12.1 us -> none  [the longest x1 3.04 us: on_device(): jnp.einsum('nf,df->nd', activated, weight[:, 2], preferred_element_type=j...]
    all_to_all x4, starting transfers between devices: 30.5 us -> 26.8 us  [the longest x2 16.5 us: across(): return lax.all_to_all(x, 'ep', 0, 0, tiled=True, axis_index_groups=cores)]
    all_to_all x4, waiting for transfers between devices: 42.1 us -> 45.5 us  [the longest x2 24.5 us: across(): return lax.all_to_all(x, 'ep', 0, 0, tiled=True, axis_index_groups=cores)]
    another operation x1 -> x2, other arithmetic: 0.54 us -> 2.74 us  [the longest x1 1.39 us: on_device(): bucket = jnp.argmax(bucket_owner[0] == rank).astype(jnp.int32)]
    ppermute x0 -> x4, waiting for transfers between devices: none -> 2.16 us  [swap(): return lax.ppermute(x, 'ep', pair)]
  transfers between devices with their start and end apart: 4 -> 8, of which waited for: 4 -> 6; matrix products, arithmetic and copies ran while one was open for 6% -> 3% of each run, Pallas kernels for 0% -> 0%
where the time goes in v2:
time: 156 us; the launch traced here: 154 us
  waiting for transfers between devices  47.7 us (31%)
  blocking collectives  47.7 us (31%)
  starting transfers between devices  27.5 us (18%)
  Pallas kernels  18.3 us (12%)
  local copies, waits for them, and re-layouts  7.22 us (5%)
  other arithmetic  5.78 us (4%)
    all_to_all x2, blocking collectives, over_rep(): return lax.all_to_all(x, 'rep', 0, 0, tiled=True)  28.6 us
    all_to_all x2, waiting for transfers between devices, across(): return lax.all_to_all(x, 'ep', 0, 0, tiled=True, axis_index_groups=cores)  24.5 us
    all_to_all x2, waiting for transfers between devices, over_rep(): return lax.all_to_all(x, 'rep', 0, 0, tiled=True)  21 us
    all_to_all x1, blocking collectives, across(): return lax.all_to_all(x, 'ep', 0, 0, tiled=True, axis_index_groups=cores)  19.1 us
    all_to_all x2, starting transfers between devices, across(): return lax.all_to_all(x, 'ep', 0, 0, tiled=True, axis_index_groups=cores)  16.5 us
    all_to_all x2, starting transfers between devices, over_rep(): return lax.all_to_all(x, 'rep', 0, 0, tiled=True)  10.3 us
    pallas_call x1, Pallas kernels, attention(): pl.pallas_call(attention_kernel, grid=(rows // GROUP,), in_specs=[pl.Bloc...  5.81 us
    pallas_call x1, Pallas kernels, gate_up(): pl.pallas_call(gate_up_kernel, grid=(2 * per,), in_specs=[pl.BlockSpec((r...  4.86 us
  transfers between devices with their start and end apart: 8, of which 6 were waited for; matrix products, arithmetic and copies ran while one was open for 3% of the time, Pallas kernels for 0%

profile of v2, /device:TPU:8, one launch (start us, length us, event | category | flops | bytes accessed | tf_op | source)
XLA Modules:
  0.0 154.3 jit_solution(17589232153908578829)
XLA Ops:
  0.0 1.4 copy.27.len_ref
  1.4 1.4 bitcast_reduce_fusion
  2.8 1.4 pad_add_fusion.info_ref
  4.1 5.8 %attention.1 = (bf16[16,8,1024]{2,1,0:T(8,128)(2,1)}, bf16[16,8,1024]{2,1,0:T(8,128)(2,1)}) custom-call(s32[2]{0:T(128)} %pad_add_fusion.info_ref, bf16[4,64,256]{2,1,0:T(8,128)(2,1)} %q_ref.1, bf16[4,64,256]{2,1,0:T(8,128)(2,1)} %kn_ref.1, bf16[4,64,256]{2,1,0:T(8,128)(2,1)} %vn_ref.1, bf16[64,32,256]{2,1,0:T(8,128)(2,1)} %ck_ref.1, ...), custom_call_target="tpu_custom_call" | custom-call | tf_op jit(solution)/shard_map/attention/pallas_call | solution.py:99
  10.6 1.1 collective-permute-done
  11.7 1.7 %add_convert_fusion = bf16[16,8,1024]{2,1,0:T(8,128)(2,1)} fusion(bf16[16,8,1024]{2,1,0:T(8,128)(2,1)S(1)} %collective-permute-done, bf16[16,8,1024]{2,1,0:T(8,128)(2,1)} %get-tuple-element.9), kind=kLoop, calls=%fused_computation.2 | loop fusion | flops 524288 | bytes 786432 | tf_op jit(solution)/shard_map/convert_element_type | solution.py:266
  13.4 10.3 %all-to-all-start = ((bf16[16,8,1024]{2,1,0:T(8,128)(2,1)}), bf16[16,8,1024]{2,1,0:T(8,128)(2,1)S(1)}, u32[]{:S(2)}, u32[]{:S(2)}) async-start(bf16[16,8,1024]{2,1,0:T(8,128)(2,1)} %add_convert_fusion), calls=%async_computation | async-start | bytes 524288 | tf_op jit(solution)/shard_map/all_to_all | solution.py:247
  23.7 0.7 pad_maximum_fusion.hid_ref
  24.4 11.2 %all-to-all-done = bf16[16,8,1024]{2,1,0:T(8,128)(2,1)S(1)} async-done(((bf16[16,8,1024]{2,1,0:T(8,128)(2,1)}), bf16[16,8,1024]{2,1,0:T(8,128)(2,1)S(1)}, u32[]{:S(2)}, u32[]{:S(2)}) %all-to-all-start) | async-done | bytes 262176 | tf_op jit(solution)/shard_map/all_to_all | solution.py:247
  35.9 1.1 collective-permute-done.1
  37.7 5.8 %all-to-all-start.1 = ((bf16[8,16,896]{2,1,0:T(8,128)(2,1)}), bf16[8,16,896]{2,1,0:T(8,128)(2,1)S(1)}, u32[]{:S(2)}, u32[]{:S(2)}) async-start(bf16[8,16,896]{2,1,0:T(8,128)(2,1)} %broadcast_in_dim.26), calls=%async_computation.1 | async-start | bytes 458752 | tf_op jit(solution)/shard_map/all_to_all | solution.py:250
  43.9 5.6 %all-to-all-done.1.att_ref = bf16[8,16,896]{2,1,0:T(8,128)(2,1)S(1)} async-done(((bf16[8,16,896]{2,1,0:T(8,128)(2,1)}), bf16[8,16,896]{2,1,0:T(8,128)(2,1)S(1)}, u32[]{:S(2)}, u32[]{:S(2)}) %all-to-all-start.1) | async-done | bytes 229408 | tf_op jit(solution)/shard_map/all_to_all | solution.py:250
  50.2 2.0 %select.3 = bf16[16,16,896]{2,1,0:T(8,128)(2,1)} custom-call(s32[16]{0:T(128)} %slice_bitcast_fusion.bucket_ref, bf16[8,16,896]{2,1,0:T(8,128)(2,1)} %copy-done, bf16[16,7168]{1,0:T(8,128)(2,1)} %pad_maximum_fusion.hid_ref, f32[1,7168]{1,0:T(1,128)} %bitcast.36), custom_call_target="tpu_custom_call" | custom-call | tf_op jit(solution)/shard_map/select/pallas_call | solution.py:139
  52.3 19.1 %all_to_all.35 = bf16[16,16,896]{2,1,0:T(8,128)(2,1)} all-to-all(bf16[16,16,896]{2,1,0:T(8,128)(2,1)} %select.3), channel_id=1, replica_groups={{0,2,4,6,8,10,12,14,16,18,20,22,24,26,28,30},{1,3,5,7,9,11,13,15,17,19,..., dimensions={0} | all-to-all | bytes 917504 | tf_op jit(solution)/shard_map/all_to_all | solution.py:247
  71.4 4.9 %gate_up.1 = bf16[256,2048]{1,0:T(8,128)(2,1)} custom-call(bf16[256,896]{1,0:T(8,128)(2,1)} %bitcast.35, bf16[3,896,1024]{2,1,0:T(8,128)(2,1)} %bitcast.30), custom_call_target="tpu_custom_call" | custom-call | tf_op jit(solution)/shard_map/gate_up/pallas_call | solution.py:157
  76.3 17.2 %all_to_all.36 = bf16[8,32,2048]{2,1,0:T(8,128)(2,1)S(1)} all-to-all(bf16[8,32,2048]{2,1,0:T(8,128)(2,1)} %bitcast.32), channel_id=1, replica_groups=mesh['rep'=8,'ep'=32] {'rep'}, dimensions={0} | all-to-all | bytes 2097152 | tf_op jit(solution)/shard_map/all_to_all | solution.py:250
  93.7 11.4 %all_to_all.37 = bf16[8,32,1024]{2,1,0:T(8,128)(2,1)} all-to-all(bf16[8,32,1024]{2,1,0:T(8,128)(2,1)S(1)} %broadcast_in_dim.29), channel_id=1, replica_groups=mesh['rep'=8,'ep'=32] {'rep'}, dimensions={0} | all-to-all | bytes 1048576 | tf_op jit(solution)/shard_map/all_to_all | solution.py:250
  105.1 3.2 %down.1 = bf16[256,896]{1,0:T(8,128)(2,1)} custom-call(bf16[256,1024]{1,0:T(8,128)(2,1)} %bitcast.33, bf16[3,896,1024]{2,1,0:T(8,128)(2,1)} %bitcast.31), custom_call_target="tpu_custom_call" | custom-call | tf_op jit(solution)/shard_map/down/pallas_call | solution.py:177
  108.3 6.2 %all-to-all-start.5 = ((bf16[16,16,896]{2,1,0:T(8,128)(2,1)}), bf16[16,16,896]{2,1,0:T(8,128)(2,1)S(1)}, u32[]{:S(2)}, u32[]{:S(2)}) async-start(bf16[16,16,896]{2,1,0:T(8,128)(2,1)} %bitcast.34), calls=%async_computation.5 | async-start | bytes 917504 | tf_op jit(solution)/shard_map/all_to_all | solution.py:247
  114.6 13.2 %all-to-all-done.5 = bf16[16,16,896]{2,1,0:T(8,128)(2,1)S(1)} async-done(((bf16[16,16,896]{2,1,0:T(8,128)(2,1)}), bf16[16,16,896]{2,1,0:T(8,128)(2,1)S(1)}, u32[]{:S(2)}, u32[]{:S(2)}) %all-to-all-start.5) | async-done | bytes 458784 | tf_op jit(solution)/shard_map/all_to_all | solution.py:247
  127.9 0.7 fusion.5
  131.0 2.3 %combine.1 = bf16[8,8,8,896]{3,2,1,0:T(8,128)(2,1)} custom-call(s32[32]{0:T(128)} %reshape.39.bucket_ref, f32[8,32]{1,0:T(8,128)} %reshape.41.share_ref, bf16[16,8,896]{2,1,0:T(8,128)(2,1)} %get-tuple-element.12.keep_ref, bf16[16,8,896]{2,1,0:T(8,128)(2,1)} %copy-done.3), custom_call_target="tpu_custom_call" | custom-call | tf_op jit(solution)/shard_map/combine/pallas_call | solution.py:207
  133.4 4.5 %all-to-all-start.6 = ((bf16[8,8,8,896]{3,2,1,0:T(8,128)(2,1)}), bf16[8,8,8,896]{3,2,1,0:T(8,128)(2,1)S(1)}, u32[]{:S(2)}, u32[]{:S(2)}) async-start(bf16[8,8,8,896]{3,2,1,0:T(8,128)(2,1)} %combine.1), calls=%async_computation.6 | async-start | bytes 1835008 | tf_op jit(solution)/shard_map/all_to_all | solution.py:250
  138.0 15.4 %all-to-all-done.6 = bf16[8,8,8,896]{3,2,1,0:T(8,128)(2,1)S(1)} async-done(((bf16[8,8,8,896]{3,2,1,0:T(8,128)(2,1)}), bf16[8,8,8,896]{3,2,1,0:T(8,128)(2,1)S(1)}, u32[]{:S(2)}, u32[]{:S(2)}) %all-to-all-start.6) | async-done | bytes 917536 | tf_op jit(solution)/shard_map/all_to_all | solution.py:250
  (41 shorter events, 6.4 us)
Async XLA Ops:
  0.0 10.0 %copy-start.2 = (bf16[4,2,7168]{2,1,0:T(2,128)(2,1)S(1)}, bf16[4,2,7168]{2,1,0:T(2,128)(2,1)}, u32[]{:S(2)}) copy-start(bf16[4,2,7168]{2,1,0:T(2,128)(2,1)} %param.13) | copy-start | bytes 344068
  9.9 1.7 %collective-permute-start = (bf16[16,8,1024]{2,1,0:T(8,128)(2,1)}, bf16[16,8,1024]{2,1,0:T(8,128)(2,1)S(1)}, u32[]{:S(2)}, u32[]{:S(2)}) collective-permute-start(bf16[16,8,1024]{2,1,0:T(8,128)(2,1)} %get-tuple-element.10), channel_id=1, source_target_pairs={{0,1},{1,0},{2,3},{3,2},{4,5},{5,4},{6,7},{7,6},{8,9},{9,8},{10,11... | collective-permute-start | bytes 786440 | tf_op jit(solution)/shard_map/ppermute | solution.py:244
  10.0 13.7 %collective-permute-start.2 = (bf16[8,7168]{1,0:T(8,128)(2,1)S(1)}, bf16[8,7168]{1,0:T(8,128)(2,1)S(1)}, u32[]{:S(2)}, u32[]{:S(2)}) collective-permute-start(bf16[8,7168]{1,0:T(8,128)(2,1)S(1)} %reshape.42), channel_id=1, source_target_pairs={{0,1},{1,0},{2,3},{3,2},{4,5},{5,4},{6,7},{7,6},{8,9},{9,8},{10,11... | collective-permute-start | bytes 344072 | tf_op jit(solution)/shard_map/ppermute | solution.py:244
  13.4 22.3 %all-to-all-start = ((bf16[16,8,1024]{2,1,0:T(8,128)(2,1)}), bf16[16,8,1024]{2,1,0:T(8,128)(2,1)S(1)}, u32[]{:S(2)}, u32[]{:S(2)}) async-start(bf16[16,8,1024]{2,1,0:T(8,128)(2,1)} %add_convert_fusion), calls=%async_computation | async-start | bytes 524288 | tf_op jit(solution)/shard_map/all_to_all | solution.py:247
  35.7 1.3 collective-permute-start.1
  37.7 11.8 %all-to-all-start.1 = ((bf16[8,16,896]{2,1,0:T(8,128)(2,1)}), bf16[8,16,896]{2,1,0:T(8,128)(2,1)S(1)}, u32[]{:S(2)}, u32[]{:S(2)}) async-start(bf16[8,16,896]{2,1,0:T(8,128)(2,1)} %broadcast_in_dim.26), calls=%async_computation.1 | async-start | bytes 458752 | tf_op jit(solution)/shard_map/all_to_all | solution.py:250
  49.5 0.7 copy-start
  105.1 9.5 %copy-start.5 = (f32[4,2,8]{2,1,0:T(2,128)S(1)}, f32[4,2,8]{2,1,0:T(2,128)}, u32[]{:S(2)}) copy-start(f32[4,2,8]{2,1,0:T(2,128)} %param.21) | copy-start | bytes 772
  105.1 23.5 %copy-start.4 = (s32[4,2,8]{2,1,0:T(2,128)S(1)}, s32[4,2,8]{2,1,0:T(2,128)}, u32[]{:S(2)}) copy-start(s32[4,2,8]{2,1,0:T(2,128)} %param.20) | copy-start | bytes 772
  108.3 19.6 %all-to-all-start.5 = ((bf16[16,16,896]{2,1,0:T(8,128)(2,1)}), bf16[16,16,896]{2,1,0:T(8,128)(2,1)S(1)}, u32[]{:S(2)}, u32[]{:S(2)}) async-start(bf16[16,16,896]{2,1,0:T(8,128)(2,1)} %bitcast.34), calls=%async_computation.5 | async-start | bytes 917504 | tf_op jit(solution)/shard_map/all_to_all | solution.py:247
  128.6 1.7 %collective-permute-start.3 = (bf16[16,8,896]{2,1,0:T(8,128)(2,1)S(1)}, bf16[16,8,896]{2,1,0:T(8,128)(2,1)S(1)}, u32[]{:S(2)}, u32[]{:S(2)}) collective-permute-start(bf16[16,8,896]{2,1,0:T(8,128)(2,1)S(1)} %get-tuple-element.11), channel_id=1, source_target_pairs={{0,1},{1,0},{2,3},{3,2},{4,5},{5,4},{6,7},{7,6},{8,9},{9,8},{10,11... | collective-permute-start | bytes 688136 | tf_op jit(solution)/shard_map/ppermute | solution.py:244
  130.3 0.7 copy-start.3
  131.0 22.5 %copy-start.1 = (bf16[8,16,896]{2,1,0:T(8,128)(2,1)S(1)}, bf16[8,16,896]{2,1,0:T(8,128)(2,1)}, u32[]{:S(2)}) copy-start(bf16[8,16,896]{2,1,0:T(8,128)(2,1)} %copy-done) | copy-start | bytes 688132
  133.4 20.0 %all-to-all-start.6 = ((bf16[8,8,8,896]{3,2,1,0:T(8,128)(2,1)}), bf16[8,8,8,896]{3,2,1,0:T(8,128)(2,1)S(1)}, u32[]{:S(2)}, u32[]{:S(2)}) async-start(bf16[8,8,8,896]{3,2,1,0:T(8,128)(2,1)} %combine.1), calls=%async_computation.6 | async-start | bytes 1835008 | tf_op jit(solution)/shard_map/all_to_all | solution.py:250

commit v3 on v2

v3 whole, which is shorter than its diff:
```python
import math

import jax
import jax.numpy as jnp
from jax import lax
from jax.experimental import pallas as pl
from jax.experimental.pallas import tpu as pltpu
from jax.sharding import PartitionSpec as P

DH = 128
ROUTE_SCALE = 2.827
EPSILON = 1e-06
GROUP = 16
NEVER = -1e30
VMEM = pltpu.VMEM
SMEM = pltpu.SMEM
F32 = jnp.float32
BF16 = jnp.bfloat16
MIB = 1024 * 1024
ROOM = pltpu.CompilerParams(vmem_limit_bytes=16 * MIB)
MOST = pltpu.CompilerParams(vmem_limit_bytes=49 * MIB)
FETCH = pltpu.CompilerParams(vmem_limit_bytes=58 * MIB)


def dot_nt(a, b):
    return lax.dot_general(a, b, (((1,), (1,)), ((), ())), preferred_element_type=F32)


def attention_kernel(
    owner_ref,
    len_ref,
    q_hbm,
    kn_hbm,
    vn_hbm,
    ck_hbm,
    cv_hbm,
    out_hbm,
    keep_ref,
    send_ref,
    q_ref,
    kn_ref,
    vn_ref,
    ck_ref,
    cv_ref,
    out_ref,
    heads,
    sems,
):
    steps, rows, width = q_hbm.shape
    cached = ck_hbm.shape[1]
    groups = rows // GROUP
    fresh = [
        pltpu.make_async_copy(src, dst, sems.at[i])
        for i, (src, dst) in enumerate(
            ((q_hbm, q_ref), (kn_hbm, kn_ref), (vn_hbm, vn_ref), (out_hbm, out_ref))
        )
    ]
    old = []
    for g in range(2):
        part = pl.ds(g * (rows // 2), rows // 2)
        for i, (src, dst) in enumerate(((ck_hbm, ck_ref), (cv_hbm, cv_ref))):
            sem = sems.at[4 + 2 * g + i]
            old.append(pltpu.make_async_copy(src.at[part], dst.at[part], sem))
    for copy in fresh[:3] + old + fresh[3:]:
        copy.start()
    rank = lax.axis_index("rep")
    parity = lax.axis_index("ep") % 2
    bucket = jnp.int32(0)
    for b in range(owner_ref.shape[1]):
        bucket = jnp.where(owner_ref[0, b] == rank, b, bucket)
    m = steps * GROUP
    n = GROUP * cached
    factor = 1.0 / math.sqrt(DH)
    row = lax.broadcasted_iota(jnp.int32, (m, n), 0)
    col = lax.broadcasted_iota(jnp.int32, (m, n), 1)
    own = col // cached == row % GROUP
    place = col % cached
    row = lax.broadcasted_iota(jnp.int32, (m, m), 0)
    col = lax.broadcasted_iota(jnp.int32, (m, m), 1)
    recent = (col % GROUP == row % GROUP) & (col // GROUP <= row // GROUP)
    row = lax.broadcasted_iota(jnp.int32, (m, rows), 0)
    col = lax.broadcasted_iota(jnp.int32, (m, rows), 1)
    lengths = len_ref[...].astype(F32)
    for copy in fresh[:3]:
        copy.wait()
    def score(g, h, live):
        part = slice(g * GROUP, (g + 1) * GROUP)
        cut = slice(h * DH, (h + 1) * DH)
        q = q_ref[:, part, cut].reshape(m, DH)
        so = dot_nt(q, ck_ref[part, :, cut].reshape(n, DH)) * factor
        sn = dot_nt(q, kn_ref[:, part, cut].reshape(m, DH)) * factor
        return jnp.where(live, so, NEVER), jnp.where(recent, sn, NEVER)

    def soften(so, sn):
        top = jnp.maximum(jnp.max(so, axis=1, keepdims=True), jnp.max(sn, axis=1, keepdims=True))
        eo = jnp.exp(so - top)
        en = jnp.exp(sn - top)
        total = jnp.sum(eo, axis=1, keepdims=True) + jnp.sum(en, axis=1, keepdims=True)
        return eo.astype(BF16), en.astype(BF16), 1.0 / total

    def gather(g, h, eo, en, inverse):
        part = slice(g * GROUP, (g + 1) * GROUP)
        cut = slice(h * DH, (h + 1) * DH)
        w = jnp.dot(
            eo, cv_ref[part, :, cut].reshape(n, DH), preferred_element_type=F32
        ) + jnp.dot(en, vn_ref[:, part, cut].reshape(m, DH), preferred_element_type=F32)
        return (w * inverse).astype(BF16).reshape(steps, GROUP, DH)

    scores = []
    for g in range(groups):
        if g % (groups // 2) == 0:
            for copy in old[g : g + 2]:
                copy.wait()
        length = jnp.sum(
            jnp.where(col == row % GROUP + g * GROUP, lengths, 0.0), axis=1, keepdims=True
        )
        live = own & (place < length.astype(jnp.int32))
        scores += [(g, h, *score(g, h, live)) for h in range(width // DH)]
    soft = [(g, h, *soften(so, sn)) for g, h, so, sn in scores]
    for g, h, *rest in soft:
        part = slice(g * GROUP, (g + 1) * GROUP)
        heads[:, part, h * DH : (h + 1) * DH] = gather(g, h, *rest)
    every = steps * rows
    half = every // 2
    mine = keep_ref.shape[1]
    own_rows = mine // steps
    j = lax.broadcasted_iota(jnp.int32, (every, 1), 0)
    core = jnp.where(j < half, parity, 1 - parity)
    chip = (j % half) // mine
    step = (j % mine) // own_rows
    wanted = step * rows + (chip * 2 + core) * own_rows + j % own_rows
    source = lax.broadcasted_iota(jnp.int32, (every, every), 1)
    order = jnp.where(source == wanted, 1.0, 0.0).astype(BF16)
    h = jnp.dot(order, heads[...].reshape(every, width), preferred_element_type=F32)
    h = h.astype(BF16)
    fresh[3].wait()
    block = out_ref.shape[1]
    chips = half // mine
    for side, ref in enumerate((keep_ref, send_ref)):
        part = jnp.dot(
            h[side * half : (side + 1) * half], out_ref[...], preferred_element_type=F32
        )
        ref[:, :, :block] = part.astype(BF16).reshape(chips, mine, block)
        lane = lax.broadcasted_iota(jnp.int32, (chips, mine, ref.shape[2] - block), 2)
        ref[:, :, block:] = jnp.where(lane == side, bucket, 0).astype(F32).astype(BF16)


def attention(owner, queries, new_keys, new_values, cache_keys, cache_values, lengths, out, chips):
    steps, rows, width = queries.shape
    mine = steps * rows // (2 * chips)
    shape = (chips, mine, out.shape[1] + 128)
    vm = pl.BlockSpec(memory_space=VMEM)
    hbm = pl.BlockSpec(memory_space=pltpu.HBM)
    operands = (queries, new_keys, new_values, cache_keys, cache_values, out)
    return pl.pallas_call(
        attention_kernel,
        in_specs=[pl.BlockSpec(memory_space=SMEM), vm] + [hbm] * len(operands),
        out_specs=[vm, vm],
        out_shape=[jax.ShapeDtypeStruct(shape, BF16)] * 2,
        scratch_shapes=[VMEM(x.shape, BF16) for x in operands]
        + [
            VMEM((steps, rows, width), BF16),
            pltpu.SemaphoreType.DMA((8,)),
        ],
        compiler_params=FETCH,
        name="attention",
    )(owner, lengths, *operands)


def select_kernel(bucket_ref, res_ref, gain_ref, out_ref, norm):
    blocks, rows, block = res_ref.shape
    total = jnp.zeros((rows, block), F32)
    for b in range(blocks):
        x = res_ref[b].astype(F32)
        total = total + x * x
    mean = jnp.sum(total, axis=1, keepdims=True) / (blocks * block)
    scale = lax.rsqrt(mean + EPSILON)
    for b in range(blocks):
        gain = gain_ref[:, b * block : (b + 1) * block]
        norm[b] = (res_ref[b].astype(F32) * scale * gain).astype(BF16)
    for c in range(out_ref.shape[0]):
        out_ref[c] = norm[bucket_ref[c]]


def select(buckets, residual, gain):
    blocks, rows, block = residual.shape
    chips = buckets.shape[0]
    vm = pl.BlockSpec(memory_space=VMEM)
    return pl.pallas_call(
        select_kernel,
        in_specs=[pl.BlockSpec(memory_space=SMEM), vm, vm],
        out_specs=vm,
        out_shape=jax.ShapeDtypeStruct((chips, rows, block), BF16),
        scratch_shapes=[VMEM(residual.shape, BF16)],
        compiler_params=ROOM,
        name="select",
    )(buckets, residual, gain)


def gate_up_kernel(x_ref, w_hbm, out_ref, w_ref, sems):
    hidden = w_ref.shape[2]
    tile = 256
    copies = [pltpu.make_async_copy(w_hbm.at[i], w_ref.at[i], sems.at[i]) for i in range(2)]
    for copy in copies:
        copy.start()
    for i, copy in enumerate(copies):
        copy.wait()
        for j in range(0, hidden, tile):
            part = jnp.dot(x_ref[...], w_ref[i, :, j : j + tile], preferred_element_type=F32)
            out_ref[:, i * hidden + j : i * hidden + j + tile] = part.astype(BF16)


def gate_up(x, weight):
    vm = pl.BlockSpec(memory_space=VMEM)
    hidden = weight.shape[2]
    return pl.pallas_call(
        gate_up_kernel,
        in_specs=[vm, pl.BlockSpec(memory_space=pltpu.HBM)],
        out_specs=vm,
        out_shape=jax.ShapeDtypeStruct((x.shape[0], 2 * hidden), BF16),
        scratch_shapes=[
            VMEM((2,) + weight.shape[1:], BF16),
            pltpu.SemaphoreType.DMA((2,)),
        ],
        compiler_params=MOST,
        name="gate_up",
    )(x, weight)


def down_kernel(x_ref, w_ref, out_ref):
    tile = 128
    for j in range(0, w_ref.shape[1], tile):
        out_ref[:, j : j + tile] = dot_nt(x_ref[...], w_ref[2, j : j + tile]).astype(BF16)


def down(x, weight):
    vm = pl.BlockSpec(memory_space=VMEM)
    return pl.pallas_call(
        down_kernel,
        in_specs=[vm, vm],
        out_specs=vm,
        out_shape=jax.ShapeDtypeStruct((x.shape[0], weight.shape[1]), BF16),
        compiler_params=ROOM,
        name="down",
    )(x, weight)


def combine_kernel(bucket_ref, ids_ref, logits_ref, keep_ref, got_ref, out_ref, acc):
    chips, rows, block = keep_ref.shape
    steps = ids_ref.shape[0]
    ids = jnp.concatenate([ids_ref[t] for t in range(steps)], axis=0)
    logits = jnp.concatenate([logits_ref[t] for t in range(steps)], axis=0)
    affinity = 1.0 / (1.0 + jnp.exp(-logits))
    weight = ROUTE_SCALE * affinity / jnp.sum(affinity, axis=1, keepdims=True)
    parity = lax.axis_index("ep") % 2
    col = lax.broadcasted_iota(jnp.int32, (rows, 2 * chips), 1)
    expert = jnp.where(col < chips, 2 * col + parity, 2 * (col - chips) + 1 - parity)
    share = jnp.zeros((rows, 2 * chips), F32)
    for k in range(ids.shape[1]):
        share = share + jnp.where(ids[:, k : k + 1] == expert, weight[:, k : k + 1], 0.0)
    acc[...] = jnp.zeros_like(acc)
    for side, ref in enumerate((keep_ref, got_ref)):
        for c in range(chips):
            e = side * chips + c
            b = bucket_ref[e]
            acc[b] = acc[b] + share[:, e : e + 1] * ref[c].astype(F32)
    done = acc[...].astype(BF16)
    for r in range(out_ref.shape[0]):
        out_ref[r] = done


def combine(buckets, ids, logits, keep, got, ranks):
    _, rows, block = keep.shape
    vm = pl.BlockSpec(memory_space=VMEM)
    return pl.pallas_call(
        combine_kernel,
        in_specs=[pl.BlockSpec(memory_space=SMEM), vm, vm, vm, vm],
        out_specs=vm,
        out_shape=jax.ShapeDtypeStruct((ranks, ranks, rows, block), BF16),
        scratch_shapes=[VMEM((ranks, rows, block), F32)],
        compiler_params=ROOM,
        name="combine",
    )(buckets, ids, logits, keep, got)


def finish_kernel(part_ref, res_ref, out_ref):
    ranks, blocks, rows, block = part_ref.shape
    own = out_ref.shape[1]
    for b in range(blocks):
        x = res_ref[b, :rows].astype(F32)
        for r in range(ranks):
            x = x + part_ref[r, b].astype(F32)
        for t in range(out_ref.shape[0]):
            row = x[t * own : (t + 1) * own].astype(BF16)
            out_ref[t, :, b * block : (b + 1) * block] = row


def finish(parts, residual, steps, own):
    _, blocks, _, block = parts.shape
    vm = pl.BlockSpec(memory_space=VMEM)
    return pl.pallas_call(
        finish_kernel,
        in_specs=[vm, vm],
        out_specs=vm,
        out_shape=jax.ShapeDtypeStruct((steps, own, blocks * block), BF16),
        compiler_params=ROOM,
        name="finish",
    )(parts, residual)


def on_device(
    hidden_in,
    queries,
    new_keys,
    new_values,
    cache_keys,
    cache_values,
    cache_lengths,
    expert_ids,
    router_logits,
    norm_gain,
    out_sectioned,
    expert_sectioned,
    bucket_owner,
):
    steps, own_rows, width = hidden_in.shape
    n_ep = lax.axis_size("ep")
    n_rep = lax.axis_size("rep")
    chips = n_ep // 2
    block = width // n_rep
    mine = own_rows * steps
    rank = lax.axis_index("rep")
    pair = [(j, j ^ 1) for j in range(n_ep)]
    cores = [[j for j in range(n_ep) if j % 2 == k] for k in range(2)]

    def swap(x):
        return lax.ppermute(x, "ep", pair)

    def across(x):
        return lax.all_to_all(x, "ep", 0, 0, tiled=True, axis_index_groups=cores)

    def over_rep(x):
        return lax.all_to_all(x, "rep", 0, 0, tiled=True)

    keep, send = attention(
        bucket_owner,
        queries,
        new_keys,
        new_values,
        cache_keys,
        cache_values,
        cache_lengths[None],
        out_sectioned,
        chips,
    )
    parts = across((keep.astype(F32) + swap(send).astype(F32)).astype(BF16))
    buckets = parts[:, 0, block : block + 2].astype(jnp.int32).T
    own_buckets, buckets = buckets[0], buckets.reshape(-1)
    own_block = lax.dynamic_slice_in_dim(hidden_in, rank * block, block, 2).reshape(mine, block)
    residual = jnp.sum(parts[:, :, :block].astype(F32), axis=0) + own_block.astype(F32)
    residual = residual.astype(BF16)
    residual = jnp.concatenate([residual, swap(residual)], axis=0)
    residual = over_rep(jnp.broadcast_to(residual, (n_rep,) + residual.shape))
    residual, own_buckets, buckets = lax.optimization_barrier((residual, own_buckets, buckets))
    chosen = select(own_buckets, residual, norm_gain.reshape(1, width))
    arrivals = across(chosen).reshape(-1, block)
    weight = jnp.transpose(expert_sectioned[0], (1, 0, 2))
    hidden = weight.shape[2]
    partial = gate_up(arrivals, weight)
    partial = over_rep(partial.reshape(n_rep, -1, 2 * hidden))
    partial = jnp.sum(partial.astype(F32), axis=0)
    activated = (jax.nn.silu(partial[:, :hidden]) * partial[:, hidden:]).astype(BF16)
    activated = over_rep(jnp.broadcast_to(activated, (n_rep,) + activated.shape))
    result = down(activated.reshape(-1, hidden), weight)
    back = across(result.reshape(chips, 2 * mine, block))
    routed = combine(
        buckets, expert_ids, router_logits, back[:, :mine], swap(back[:, mine:]), n_rep
    )
    return finish(over_rep(routed), residual, steps, own_rows)


def solution(mesh):
    return jax.shard_map(
        on_device,
        mesh=mesh,
        in_specs=(
            P(None, "ep", None),
            P(None, None, "ep"),
            P(None, None, "ep"),
            P(None, None, "ep"),
            P(None, None, "ep"),
            P(None, None, "ep"),
            P(),
            P(None, "ep", None),
            P(None, "ep", None),
            P(),
            P("ep", "rep"),
            P("ep", "rep", None, None),
            P("ep", None),
        ),
        out_specs=P(None, "ep", None),
        check_vma=False,
    )
```

time: 156 us -> 137 us (0.88)
  blocking collectives: 47.7 us -> 83.8 us
  waiting for transfers between devices: 47.7 us -> 21.5 us
  starting transfers between devices: 27.5 us -> 16.3 us
  Pallas kernels: 18.3 us -> 11.3 us
  local copies, waits for them, and re-layouts: 7.22 us -> 1 us
  other arithmetic: 5.78 us -> 2.71 us
    all_to_all x1 -> x2, blocking collectives: 19.1 us -> 38.6 us  [across(): return lax.all_to_all(x, 'ep', 0, 0, tiled=True, axis_index_groups=cores)]
    all_to_all x2 -> x3, blocking collectives: 28.6 us -> 45.2 us  [over_rep(): return lax.all_to_all(x, 'rep', 0, 0, tiled=True)]
    all_to_all x2 -> x1, waiting for transfers between devices: 21 us -> 6.08 us  [over_rep(): return lax.all_to_all(x, 'rep', 0, 0, tiled=True)]
    all_to_all x2 -> x1, waiting for transfers between devices: 24.5 us -> 11.2 us  [across(): return lax.all_to_all(x, 'ep', 0, 0, tiled=True, axis_index_groups=cores)]
    all_to_all x2 -> x1, starting transfers between devices: 16.5 us -> 10.3 us  [across(): return lax.all_to_all(x, 'ep', 0, 0, tiled=True, axis_index_groups=cores)]
    all_to_all x2 -> x1, starting transfers between devices: 10.3 us -> 5.76 us  [over_rep(): return lax.all_to_all(x, 'rep', 0, 0, tiled=True)]
    pallas_call x3 -> x4, Pallas kernels: 13.9 us -> 9.54 us  [the longest x1 4.51 us: attention(): pl.pallas_call(attention_kernel, in_specs=[pl.BlockSpec(memory_space=SMEM...]
    another operation x2 -> x0, other arithmetic: 2.74 us -> none  [the longest x1 1.39 us: on_device(): bucket = jnp.argmax(bucket_owner[0] == rank).astype(jnp.int32)]
  transfers between devices with their start and end apart: 8 -> 5, of which waited for: 6 -> 5; matrix products, arithmetic and copies ran while one was open for 3% -> 1% of each run, Pallas kernels for 0% -> 0%
where the time goes in v3:
time: 137 us
  blocking collectives  83.8 us (61%)
  waiting for transfers between devices  21.5 us (16%)
  starting transfers between devices  16.3 us (12%)
  Pallas kernels  11.3 us (8%)
  other arithmetic  2.71 us (2%)
    all_to_all x3, blocking collectives, over_rep(): return lax.all_to_all(x, 'rep', 0, 0, tiled=True)  45.2 us
    all_to_all x2, blocking collectives, across(): return lax.all_to_all(x, 'ep', 0, 0, tiled=True, axis_index_groups=cores)  38.6 us
    all_to_all x1, waiting for transfers between devices, across(): return lax.all_to_all(x, 'ep', 0, 0, tiled=True, axis_index_groups=cores)  11.2 us
    all_to_all x1, starting transfers between devices, across(): return lax.all_to_all(x, 'ep', 0, 0, tiled=True, axis_index_groups=cores)  10.3 us
    all_to_all x1, waiting for transfers between devices, over_rep(): return lax.all_to_all(x, 'rep', 0, 0, tiled=True)  6.08 us
    all_to_all x1, starting transfers between devices, over_rep(): return lax.all_to_all(x, 'rep', 0, 0, tiled=True)  5.76 us
    pallas_call x1, Pallas kernels, attention(): pl.pallas_call(attention_kernel, in_specs=[pl.BlockSpec(memory_space=SMEM...  4.51 us
    ppermute x3, waiting for transfers between devices, swap(): return lax.ppermute(x, 'ep', pair)  4.19 us
  transfers between devices with their start and end apart: 5, of which 5 were waited for; matrix products, arithmetic and copies ran while one was open for 1% of the time, Pallas kernels for 0%

profile of v3, /device:TPU:8, one launch (start us, length us, event | category | flops | bytes accessed | tf_op | source)
XLA Modules:
  0.0 136.7 jit_solution(4735709103374553890)
XLA Ops:
  0.0 4.5 %attention.1 = (bf16[16,8,1024]{2,1,0:T(8,128)(2,1)}, bf16[16,8,1024]{2,1,0:T(8,128)(2,1)}) custom-call(s32[1,8]{1,0:T(1,128)} %owner_ref.1, s32[1,64]{1,0:T(1,128)} %bitcast.25, bf16[4,64,256]{2,1,0:T(8,128)(2,1)} %q_hbm.1, bf16[4,64,256]{2,1,0:T(8,128)(2,1)} %kn_hbm.1, bf16[4,64,256]{2,1,0:T(8,128)(2,1)} %vn_hbm.1, bf16[64,32,256]{2,1,0:T(8,128)(2,1)} %ck_hbm.1, ...), custom_call_target="tpu_custom_call" | custom-call | tf_op jit(solution)/shard_map/attention/pallas_call | solution.py:155
  4.6 1.7 %collective-permute-done = bf16[16,8,1024]{2,1,0:T(8,128)(2,1)S(1)} collective-permute-done((bf16[16,8,1024]{2,1,0:T(8,128)(2,1)}, bf16[16,8,1024]{2,1,0:T(8,128)(2,1)S(1)}, u32[]{:S(2)}, u32[]{:S(2)}) %collective-permute-start) | collective-permute-done | bytes 262176 | tf_op jit(solution)/shard_map/ppermute | solution.py:337
  6.4 1.7 %add_convert_fusion = bf16[16,8,1024]{2,1,0:T(8,128)(2,1)} fusion(bf16[16,8,1024]{2,1,0:T(8,128)(2,1)S(1)} %collective-permute-done, bf16[16,8,1024]{2,1,0:T(8,128)(2,1)} %get-tuple-element.10), kind=kLoop, calls=%fused_computation.1 | loop fusion | flops 524288 | bytes 786432 | tf_op jit(solution)/shard_map/convert_element_type | solution.py:356
  8.1 10.3 %all-to-all-start = ((bf16[16,8,1024]{2,1,0:T(8,128)(2,1)}), bf16[16,8,1024]{2,1,0:T(8,128)(2,1)S(1)}, u32[]{:S(2)}, u32[]{:S(2)}) async-start(bf16[16,8,1024]{2,1,0:T(8,128)(2,1)} %add_convert_fusion), calls=%async_computation | async-start | bytes 524288 | tf_op jit(solution)/shard_map/all_to_all | solution.py:340
  18.4 0.7 dynamic-slice_convert_fusion
  19.2 11.2 %all-to-all-done = bf16[16,8,1024]{2,1,0:T(8,128)(2,1)S(1)} async-done(((bf16[16,8,1024]{2,1,0:T(8,128)(2,1)}), bf16[16,8,1024]{2,1,0:T(8,128)(2,1)S(1)}, u32[]{:S(2)}, u32[]{:S(2)}) %all-to-all-start) | async-done | bytes 262176 | tf_op jit(solution)/shard_map/all_to_all | solution.py:340
  30.4 0.1 collective-permute-start.1
  30.7 1.0 collective-permute-done.1
  31.7 0.7 broadcast_in_dim.10
  32.4 5.8 %all-to-all-start.1 = ((bf16[8,16,896]{2,1,0:T(8,128)(2,1)}), bf16[8,16,896]{2,1,0:T(8,128)(2,1)S(1)}, u32[]{:S(2)}, u32[]{:S(2)}) async-start(bf16[8,16,896]{2,1,0:T(8,128)(2,1)} %broadcast_in_dim.10), calls=%async_computation.1 | async-start | bytes 458752 | tf_op jit(solution)/shard_map/all_to_all | solution.py:343
  38.1 6.1 %all-to-all-done.1.res_ref = bf16[8,16,896]{2,1,0:T(8,128)(2,1)S(1)} async-done(((bf16[8,16,896]{2,1,0:T(8,128)(2,1)}), bf16[8,16,896]{2,1,0:T(8,128)(2,1)S(1)}, u32[]{:S(2)}, u32[]{:S(2)}) %all-to-all-start.1) | async-done | bytes 229408 | tf_op jit(solution)/shard_map/all_to_all | solution.py:343
  44.2 0.7 select.1
  45.0 18.8 %all_to_all.35 = bf16[16,16,896]{2,1,0:T(8,128)(2,1)S(1)} all-to-all(bf16[16,16,896]{2,1,0:T(8,128)(2,1)S(1)} %select.1), channel_id=1, replica_groups={{0,2,4,6,8,10,12,14,16,18,20,22,24,26,28,30},{1,3,5,7,9,11,13,15,17,19,..., dimensions={0} | all-to-all | bytes 917504 | tf_op jit(solution)/shard_map/all_to_all | solution.py:340
  63.8 3.1 %gate_up.1 = bf16[256,2048]{1,0:T(8,128)(2,1)S(1)} custom-call(bf16[256,896]{1,0:T(8,128)(2,1)S(1)} %bitcast.21, bf16[3,896,1024]{2,1,0:T(8,128)(2,1)} %bitcast.14), custom_call_target="tpu_custom_call" | custom-call | tf_op jit(solution)/shard_map/gate_up/pallas_call | solution.py:216
  66.9 16.6 %all_to_all.36 = bf16[8,32,2048]{2,1,0:T(8,128)(2,1)S(1)} all-to-all(bf16[8,32,2048]{2,1,0:T(8,128)(2,1)S(1)} %bitcast.18), channel_id=1, replica_groups=mesh['rep'=8,'ep'=32] {'rep'}, dimensions={0} | all-to-all | bytes 2097152 | tf_op jit(solution)/shard_map/all_to_all | solution.py:343
  83.5 0.1 convert_reduce_fusion
  83.8 11.2 %all_to_all.37 = bf16[8,32,1024]{2,1,0:T(8,128)(2,1)S(1)} all-to-all(bf16[8,32,1024]{2,1,0:T(8,128)(2,1)S(1)} %broadcast_in_dim.11), channel_id=1, replica_groups=mesh['rep'=8,'ep'=32] {'rep'}, dimensions={0} | all-to-all | bytes 1048576 | tf_op jit(solution)/shard_map/all_to_all | solution.py:343
  95.0 1.1 down.1
  96.1 19.7 %all_to_all.38 = bf16[16,16,896]{2,1,0:T(8,128)(2,1)S(1)} all-to-all(bf16[16,16,896]{2,1,0:T(8,128)(2,1)S(1)} %bitcast.20), channel_id=1, replica_groups={{0,2,4,6,8,10,12,14,16,18,20,22,24,26,28,30},{1,3,5,7,9,11,13,15,17,19,..., dimensions={0} | all-to-all | bytes 917504 | tf_op jit(solution)/shard_map/all_to_all | solution.py:340
  115.9 0.1 collective-permute-start.2
  116.0 1.5 %collective-permute-done.2.got_ref = bf16[16,8,896]{2,1,0:T(8,128)(2,1)S(1)} collective-permute-done((bf16[16,8,896]{2,1,0:T(8,128)(2,1)S(1)}, bf16[16,8,896]{2,1,0:T(8,128)(2,1)S(1)}, u32[]{:S(2)}, u32[]{:S(2)}) %collective-permute-start.2) | collective-permute-done | bytes 229408 | tf_op jit(solution)/shard_map/ppermute | solution.py:337
  117.5 1.0 combine.1
  118.5 17.4 %all_to_all.39.part_ref = bf16[8,8,8,896]{3,2,1,0:T(8,128)(2,1)S(1)} all-to-all(bf16[8,8,8,896]{3,2,1,0:T(8,128)(2,1)S(1)} %combine.1), channel_id=1, replica_groups=mesh['rep'=8,'ep'=32] {'rep'}, dimensions={0} | all-to-all | bytes 1835008 | tf_op jit(solution)/shard_map/all_to_all | solution.py:343
  135.9 0.8 finish.1
  (23 shorter events, 0.5 us)
Async XLA Ops:
  0.0 44.2 %copy-start = (f32[7168]{0:T(1024)S(1)}, f32[7168]{0:T(1024)}, u32[]{:S(2)}) copy-start(f32[7168]{0:T(1024)} %param.22) | copy-start | bytes 86020
  4.5 1.8 %collective-permute-start = (bf16[16,8,1024]{2,1,0:T(8,128)(2,1)}, bf16[16,8,1024]{2,1,0:T(8,128)(2,1)S(1)}, u32[]{:S(2)}, u32[]{:S(2)}) collective-permute-start(bf16[16,8,1024]{2,1,0:T(8,128)(2,1)} %get-tuple-element.11), channel_id=1, source_target_pairs={{0,1},{1,0},{2,3},{3,2},{4,5},{5,4},{6,7},{7,6},{8,9},{9,8},{10,11... | collective-permute-start | bytes 786440 | tf_op jit(solution)/shard_map/ppermute | solution.py:337
  8.1 22.3 %all-to-all-start = ((bf16[16,8,1024]{2,1,0:T(8,128)(2,1)}), bf16[16,8,1024]{2,1,0:T(8,128)(2,1)S(1)}, u32[]{:S(2)}, u32[]{:S(2)}) async-start(bf16[16,8,1024]{2,1,0:T(8,128)(2,1)} %add_convert_fusion), calls=%async_computation | async-start | bytes 524288 | tf_op jit(solution)/shard_map/all_to_all | solution.py:340
  30.4 1.3 collective-permute-start.1
  32.4 11.8 %all-to-all-start.1 = ((bf16[8,16,896]{2,1,0:T(8,128)(2,1)}), bf16[8,16,896]{2,1,0:T(8,128)(2,1)S(1)}, u32[]{:S(2)}, u32[]{:S(2)}) async-start(bf16[8,16,896]{2,1,0:T(8,128)(2,1)} %broadcast_in_dim.10), calls=%async_computation.1 | async-start | bytes 458752 | tf_op jit(solution)/shard_map/all_to_all | solution.py:343
  63.8 31.2 %slice-start = ((s8[5505024]{0:T(1024)(128)(4,1)}), s8[4194304]{0:T(1024)(128)(4,1)S(1)}, s32[]{:S(2)}) async-start(s8[5505024]{0:T(1024)(128)(4,1)} %bitcast.15), calls=%async_computation.7 | async-start | bytes 8388608
  63.8 31.2 %slice-start.1 = ((s8[5505024]{0:T(1024)(128)(4,1)}), s8[1310720]{0:T(1024)(128)(4,1)S(1)}, s32[]{:S(2)}) async-start(s8[5505024]{0:T(1024)(128)(4,1)} %bitcast.15), calls=%async_computation.8 | async-start | bytes 2621440
  83.5 33.9 %copy-start.1 = (s32[4,2,8]{2,1,0:T(2,128)S(1)}, s32[4,2,8]{2,1,0:T(2,128)}, u32[]{:S(2)}) copy-start(s32[4,2,8]{2,1,0:T(2,128)} %ids_ref.1) | copy-start | bytes 772
  83.5 33.9 %copy-start.2 = (f32[4,2,8]{2,1,0:T(2,128)S(1)}, f32[4,2,8]{2,1,0:T(2,128)}, u32[]{:S(2)}) copy-start(f32[4,2,8]{2,1,0:T(2,128)} %logits_ref.1) | copy-start | bytes 772
  115.9 1.6 %collective-permute-start.2 = (bf16[16,8,896]{2,1,0:T(8,128)(2,1)S(1)}, bf16[16,8,896]{2,1,0:T(8,128)(2,1)S(1)}, u32[]{:S(2)}, u32[]{:S(2)}) collective-permute-start(bf16[16,8,896]{2,1,0:T(8,128)(2,1)S(1)} %get-tuple-element.15), channel_id=1, source_target_pairs={{0,1},{1,0},{2,3},{3,2},{4,5},{5,4},{6,7},{7,6},{8,9},{9,8},{10,11... | collective-permute-start | bytes 688136 | tf_op jit(solution)/shard_map/ppermute | solution.py:337

commit v4 on v3

--- a/solution.py
+++ b/solution.py
@@ -197,14 +197,28 @@
     )(buckets, residual, gain)
 
 
-def gate_up_kernel(x_ref, w_hbm, out_ref, w_ref, sems):
+def fetch_kernel(w_hbm, out_ref, sem):
+    copy = pltpu.make_async_copy(w_hbm.at[pl.ds(0, out_ref.shape[0])], out_ref, sem)
+    copy.start()
+    copy.wait()
+
+
+def fetch(weight, count):
+    return pl.pallas_call(
+        fetch_kernel,
+        in_specs=[pl.BlockSpec(memory_space=pltpu.HBM)],
+        out_specs=pl.BlockSpec(memory_space=VMEM),
+        out_shape=jax.ShapeDtypeStruct((count,) + weight.shape[1:], BF16),
+        scratch_shapes=[pltpu.SemaphoreType.DMA],
+        compiler_params=MOST,
+        name="fetch",
+    )(weight)
+
+
+def gate_up_kernel(x_ref, w_ref, out_ref):
     hidden = w_ref.shape[2]
     tile = 256
-    copies = [pltpu.make_async_copy(w_hbm.at[i], w_ref.at[i], sems.at[i]) for i in range(2)]
-    for copy in copies:
-        copy.start()
-    for i, copy in enumerate(copies):
-        copy.wait()
+    for i in range(2):
         for j in range(0, hidden, tile):
             part = jnp.dot(x_ref[...], w_ref[i, :, j : j + tile], preferred_element_type=F32)
             out_ref[:, i * hidden + j : i * hidden + j + tile] = part.astype(BF16)
@@ -212,17 +226,12 @@
 
 def gate_up(x, weight):
     vm = pl.BlockSpec(memory_space=VMEM)
-    hidden = weight.shape[2]
     return pl.pallas_call(
         gate_up_kernel,
-        in_specs=[vm, pl.BlockSpec(memory_space=pltpu.HBM)],
+        in_specs=[vm, vm],
         out_specs=vm,
-        out_shape=jax.ShapeDtypeStruct((x.shape[0], 2 * hidden), BF16),
-        scratch_shapes=[
-            VMEM((2,) + weight.shape[1:], BF16),
-            pltpu.SemaphoreType.DMA((2,)),
-        ],
-        compiler_params=MOST,
+        out_shape=jax.ShapeDtypeStruct((x.shape[0], 2 * weight.shape[2]), BF16),
+        compiler_params=ROOM,
         name="gate_up",
     )(x, weight)
 
@@ -353,20 +362,27 @@
         out_sectioned,
         chips,
     )
-    parts = across((keep.astype(F32) + swap(send).astype(F32)).astype(BF16))
+    own_block = lax.dynamic_slice_in_dim(hidden_in, rank * block, block, 2).reshape(mine, block)
+    both = (keep.astype(F32) + swap(send).astype(F32)).astype(BF16)
+    both, own_block = lax.optimization_barrier((both, own_block))
+    parts = across(both)
     buckets = parts[:, 0, block : block + 2].astype(jnp.int32).T
     own_buckets, buckets = buckets[0], buckets.reshape(-1)
-    own_block = lax.dynamic_slice_in_dim(hidden_in, rank * block, block, 2).reshape(mine, block)
     residual = jnp.sum(parts[:, :, :block].astype(F32), axis=0) + own_block.astype(F32)
     residual = residual.astype(BF16)
-    residual = jnp.concatenate([residual, swap(residual)], axis=0)
+    weight = jnp.transpose(expert_sectioned[0], (1, 0, 2))
+    residual, weight = lax.optimization_barrier((residual, weight))
+    other = swap(residual)
+    into = fetch(weight, 2)
+    other, into, own_buckets, buckets = lax.optimization_barrier(
+        (other, into, own_buckets, buckets)
+    )
+    residual = jnp.concatenate([residual, other], axis=0)
     residual = over_rep(jnp.broadcast_to(residual, (n_rep,) + residual.shape))
-    residual, own_buckets, buckets = lax.optimization_barrier((residual, own_buckets, buckets))
     chosen = select(own_buckets, residual, norm_gain.reshape(1, width))
     arrivals = across(chosen).reshape(-1, block)
-    weight = jnp.transpose(expert_sectioned[0], (1, 0, 2))
     hidden = weight.shape[2]
-    partial = gate_up(arrivals, weight)
+    partial = gate_up(arrivals, into)
     partial = over_rep(partial.reshape(n_rep, -1, 2 * hidden))
     partial = jnp.sum(partial.astype(F32), axis=0)
     activated = (jax.nn.silu(partial[:, :hidden]) * partial[:, hidden:]).astype(BF16)

time: 137 us -> 135 us (0.985)
  blocking collectives: 83.8 us -> 118 us
  waiting for transfers between devices: 21.5 us -> 3.15 us
  starting transfers between devices: 16.3 us -> 0.28 us
  other arithmetic: 2.71 us -> 1.27 us
    all_to_all x2 -> x3, blocking collectives: 38.6 us -> 60.8 us  [across(): return lax.all_to_all(x, 'ep', 0, 0, tiled=True, axis_index_groups=cores)]
    all_to_all x2 -> x0, waiting for transfers between devices: 17.3 us -> none  [the longest x1 11.2 us: across(): return lax.all_to_all(x, 'ep', 0, 0, tiled=True, axis_index_groups=cores)]
    all_to_all x2 -> x0, starting transfers between devices: 16.1 us -> none  [the longest x1 10.3 us: across(): return lax.all_to_all(x, 'ep', 0, 0, tiled=True, axis_index_groups=cores)]
    all_to_all x3 -> x4, blocking collectives: 45.2 us -> 56.8 us  [over_rep(): return lax.all_to_all(x, 'rep', 0, 0, tiled=True)]
    convert_element_type x2 -> x1, other arithmetic: 2.45 us -> 1.02 us  [on_device(): both = (keep.astype(F32) + swap(send).astype(F32)).astype(BF16)]
    pallas_call x1 -> x2, Pallas kernels: 3.12 us -> 3.3 us  [the longest x1 2.05 us: fetch(): pl.pallas_call(fetch_kernel, in_specs=[pl.BlockSpec(memory_space=pltpu.HB...]
  transfers between devices with their start and end apart: 5 -> 3, of which waited for: 5 -> 2; matrix products, arithmetic and copies ran while one was open for 1% -> 0% of each run, Pallas kernels for 0% -> 2%
where the time goes in v4:
time: 135 us; the launch traced here: 134 us
  blocking collectives  118 us (87%)
  Pallas kernels  11.5 us (9%)
  waiting for transfers between devices  3.15 us (2%)
    all_to_all x3, blocking collectives, across(): return lax.all_to_all(x, 'ep', 0, 0, tiled=True, axis_index_groups=cores)  60.8 us
    all_to_all x4, blocking collectives, over_rep(): return lax.all_to_all(x, 'rep', 0, 0, tiled=True)  56.8 us
    pallas_call x1, Pallas kernels, attention(): pl.pallas_call(attention_kernel, in_specs=[pl.BlockSpec(memory_space=SMEM...  4.51 us
    ppermute x3, waiting for transfers between devices, swap(): return lax.ppermute(x, 'ep', pair)  3.15 us
  transfers between devices with their start and end apart: 3, of which 2 were waited for; matrix products, arithmetic and copies ran while one was open for 0% of the time, Pallas kernels for 2%

profile of v4, /device:TPU:8, one launch (start us, length us, event | category | flops | bytes accessed | tf_op | source)
XLA Modules:
  0.0 134.3 jit_solution(14255030219236709377)
XLA Ops:
  0.0 4.5 %attention.1 = (bf16[16,8,1024]{2,1,0:T(8,128)(2,1)}, bf16[16,8,1024]{2,1,0:T(8,128)(2,1)}) custom-call(s32[1,8]{1,0:T(1,128)} %owner_ref.1, s32[1,64]{1,0:T(1,128)} %bitcast.25, bf16[4,64,256]{2,1,0:T(8,128)(2,1)} %q_hbm.1, bf16[4,64,256]{2,1,0:T(8,128)(2,1)} %kn_hbm.1, bf16[4,64,256]{2,1,0:T(8,128)(2,1)} %vn_hbm.1, bf16[64,32,256]{2,1,0:T(8,128)(2,1)} %ck_hbm.1, ...), custom_call_target="tpu_custom_call" | custom-call | tf_op jit(solution)/shard_map/attention/pallas_call | solution.py:155
  4.5 0.1 collective-permute-start
  4.7 1.7 %collective-permute-done = bf16[16,8,1024]{2,1,0:T(8,128)(2,1)S(1)} collective-permute-done((bf16[16,8,1024]{2,1,0:T(8,128)(2,1)}, bf16[16,8,1024]{2,1,0:T(8,128)(2,1)S(1)}, u32[]{:S(2)}, u32[]{:S(2)}) %collective-permute-start) | collective-permute-done | bytes 262176 | tf_op jit(solution)/shard_map/ppermute | solution.py:346
  6.4 1.0 add_convert_fusion
  7.4 22.1 %all_to_all.35 = bf16[16,8,1024]{2,1,0:T(8,128)(2,1)S(1)} all-to-all(bf16[16,8,1024]{2,1,0:T(8,128)(2,1)S(1)} %add_convert_fusion), channel_id=1, replica_groups={{0,2,4,6,8,10,12,14,16,18,20,22,24,26,28,30},{1,3,5,7,9,11,13,15,17,19,..., dimensions={0} | all-to-all | bytes 524288 | tf_op jit(solution)/shard_map/all_to_all | solution.py:349
  29.5 0.1 copy.15
  29.6 0.1 collective-permute-start.1
  29.7 0.1 reshape.24.bucket_ref
  29.8 2.1 %fetch.1.w_ref = bf16[2,896,1024]{2,1,0:T(8,128)(2,1)S(1)} custom-call(bf16[3,896,1024]{2,1,0:T(8,128)(2,1)} %bitcast.14), custom_call_target="tpu_custom_call" | custom-call | tf_op jit(solution)/shard_map/fetch/pallas_call | solution.py:207
  31.9 12.0 %all_to_all.36.res_ref = bf16[8,16,896]{2,1,0:T(8,128)(2,1)S(1)} all-to-all(bf16[8,16,896]{2,1,0:T(8,128)(2,1)S(1)} %broadcast_in_dim.10), channel_id=1, replica_groups=mesh['rep'=8,'ep'=32] {'rep'}, dimensions={0} | all-to-all | bytes 458752 | tf_op jit(solution)/shard_map/all_to_all | solution.py:352
  43.9 0.7 select.1
  44.6 19.5 %all_to_all.37 = bf16[16,16,896]{2,1,0:T(8,128)(2,1)S(1)} all-to-all(bf16[16,16,896]{2,1,0:T(8,128)(2,1)S(1)} %select.1), channel_id=1, replica_groups={{0,2,4,6,8,10,12,14,16,18,20,22,24,26,28,30},{1,3,5,7,9,11,13,15,17,19,..., dimensions={0} | all-to-all | bytes 917504 | tf_op jit(solution)/shard_map/all_to_all | solution.py:349
  64.1 1.2 gate_up.1
  65.3 16.1 %all_to_all.38 = bf16[8,32,2048]{2,1,0:T(8,128)(2,1)S(1)} all-to-all(bf16[8,32,2048]{2,1,0:T(8,128)(2,1)S(1)} %bitcast.18), channel_id=1, replica_groups=mesh['rep'=8,'ep'=32] {'rep'}, dimensions={0} | all-to-all | bytes 2097152 | tf_op jit(solution)/shard_map/all_to_all | solution.py:352
  81.4 0.1 convert_reduce_fusion
  81.6 0.1 broadcast_in_dim.11
  81.7 11.2 %all_to_all.39 = bf16[8,32,1024]{2,1,0:T(8,128)(2,1)S(1)} all-to-all(bf16[8,32,1024]{2,1,0:T(8,128)(2,1)S(1)} %broadcast_in_dim.11), channel_id=1, replica_groups=mesh['rep'=8,'ep'=32] {'rep'}, dimensions={0} | all-to-all | bytes 1048576 | tf_op jit(solution)/shard_map/all_to_all | solution.py:352
  92.9 1.1 down.1
  94.0 19.3 %all_to_all.40 = bf16[16,16,896]{2,1,0:T(8,128)(2,1)S(1)} all-to-all(bf16[16,16,896]{2,1,0:T(8,128)(2,1)S(1)} %bitcast.21), channel_id=1, replica_groups={{0,2,4,6,8,10,12,14,16,18,20,22,24,26,28,30},{1,3,5,7,9,11,13,15,17,19,..., dimensions={0} | all-to-all | bytes 917504 | tf_op jit(solution)/shard_map/all_to_all | solution.py:349
  113.3 0.1 collective-permute-start.2
  113.4 1.5 %collective-permute-done.2.got_ref = bf16[16,8,896]{2,1,0:T(8,128)(2,1)S(1)} collective-permute-done((bf16[16,8,896]{2,1,0:T(8,128)(2,1)S(1)}, bf16[16,8,896]{2,1,0:T(8,128)(2,1)S(1)}, u32[]{:S(2)}, u32[]{:S(2)}) %collective-permute-start.2) | collective-permute-done | bytes 229408 | tf_op jit(solution)/shard_map/ppermute | solution.py:346
  114.9 1.0 combine.1
  115.9 17.5 %all_to_all.41.part_ref = bf16[8,8,8,896]{3,2,1,0:T(8,128)(2,1)S(1)} all-to-all(bf16[8,8,8,896]{3,2,1,0:T(8,128)(2,1)S(1)} %combine.1), channel_id=1, replica_groups=mesh['rep'=8,'ep'=32] {'rep'}, dimensions={0} | all-to-all | bytes 1835008 | tf_op jit(solution)/shard_map/all_to_all | solution.py:352
  133.5 0.8 finish.1
  (24 shorter events, 0.2 us)
Async XLA Ops:
  0.0 4.6 %copy-start = (bf16[4,2,7168]{2,1,0:T(2,128)(2,1)S(1)}, bf16[4,2,7168]{2,1,0:T(2,128)(2,1)}, u32[]{:S(2)}) copy-start(bf16[4,2,7168]{2,1,0:T(2,128)(2,1)} %param.13) | copy-start | bytes 344068
  4.5 1.8 %collective-permute-start = (bf16[16,8,1024]{2,1,0:T(8,128)(2,1)}, bf16[16,8,1024]{2,1,0:T(8,128)(2,1)S(1)}, u32[]{:S(2)}, u32[]{:S(2)}) collective-permute-start(bf16[16,8,1024]{2,1,0:T(8,128)(2,1)} %get-tuple-element.16), channel_id=1, source_target_pairs={{0,1},{1,0},{2,3},{3,2},{4,5},{5,4},{6,7},{7,6},{8,9},{9,8},{10,11... | collective-permute-start | bytes 786440 | tf_op jit(solution)/shard_map/ppermute | solution.py:346
  29.6 2.3 %collective-permute-start.1 = (bf16[8,896]{1,0:T(8,128)(2,1)S(1)}, bf16[8,896]{1,0:T(8,128)(2,1)S(1)}, u32[]{:S(2)}, u32[]{:S(2)}) collective-permute-start(bf16[8,896]{1,0:T(8,128)(2,1)S(1)} %add_convert_fusion.1), channel_id=1, source_target_pairs={{0,1},{1,0},{2,3},{3,2},{4,5},{5,4},{6,7},{7,6},{8,9},{9,8},{10,11... | collective-permute-start | bytes 43016 | tf_op jit(solution)/shard_map/ppermute | solution.py:346
  29.8 14.1 %copy-start.1 = (f32[7168]{0:T(1024)S(1)}, f32[7168]{0:T(1024)}, u32[]{:S(2)}) copy-start(f32[7168]{0:T(1024)} %param.22) | copy-start | bytes 86020
  44.6 48.3 %slice-start = ((s8[5505024]{0:T(1024)(128)(4,1)}), s8[4194304]{0:T(1024)(128)(4,1)S(1)}, s32[]{:S(2)}) async-start(s8[5505024]{0:T(1024)(128)(4,1)} %bitcast.15), calls=%async_computation.7 | async-start | bytes 8388608
  64.1 28.8 %slice-start.1 = ((s8[5505024]{0:T(1024)(128)(4,1)}), s8[1310720]{0:T(1024)(128)(4,1)S(1)}, s32[]{:S(2)}) async-start(s8[5505024]{0:T(1024)(128)(4,1)} %bitcast.15), calls=%async_computation.8 | async-start | bytes 2621440
  92.9 22.0 %copy-start.2 = (s32[4,2,8]{2,1,0:T(2,128)S(1)}, s32[4,2,8]{2,1,0:T(2,128)}, u32[]{:S(2)}) copy-start(s32[4,2,8]{2,1,0:T(2,128)} %ids_ref.1) | copy-start | bytes 772
  92.9 22.0 %copy-start.3 = (f32[4,2,8]{2,1,0:T(2,128)S(1)}, f32[4,2,8]{2,1,0:T(2,128)}, u32[]{:S(2)}) copy-start(f32[4,2,8]{2,1,0:T(2,128)} %logits_ref.1) | copy-start | bytes 772
  113.3 1.6 %collective-permute-start.2 = (bf16[16,8,896]{2,1,0:T(8,128)(2,1)S(1)}, bf16[16,8,896]{2,1,0:T(8,128)(2,1)S(1)}, u32[]{:S(2)}, u32[]{:S(2)}) collective-permute-start(bf16[16,8,896]{2,1,0:T(8,128)(2,1)S(1)} %get-tuple-element.25), channel_id=1, source_target_pairs={{0,1},{1,0},{2,3},{3,2},{4,5},{5,4},{6,7},{7,6},{8,9},{9,8},{10,11... | collective-permute-start | bytes 688136 | tf_op jit(solution)/shard_map/ppermute | solution.py:346

commit v5 on v4

--- a/solution.py
+++ b/solution.py
@@ -27,8 +27,8 @@
 
 
 def attention_kernel(
-    owner_ref,
-    len_ref,
+    owner_hbm,
+    len_hbm,
     q_hbm,
     kn_hbm,
     vn_hbm,
@@ -37,6 +37,8 @@
     out_hbm,
     keep_ref,
     send_ref,
+    owner_ref,
+    len_ref,
     q_ref,
     kn_ref,
     vn_ref,
@@ -55,19 +57,19 @@
             ((q_hbm, q_ref), (kn_hbm, kn_ref), (vn_hbm, vn_ref), (out_hbm, out_ref))
         )
     ]
+    small = [
+        pltpu.make_async_copy(len_hbm, len_ref, sems.at[8]),
+        pltpu.make_async_copy(owner_hbm, owner_ref, sems.at[9]),
+    ]
     old = []
     for g in range(2):
         part = pl.ds(g * (rows // 2), rows // 2)
         for i, (src, dst) in enumerate(((ck_hbm, ck_ref), (cv_hbm, cv_ref))):
             sem = sems.at[4 + 2 * g + i]
             old.append(pltpu.make_async_copy(src.at[part], dst.at[part], sem))
-    for copy in fresh[:3] + old + fresh[3:]:
+    for copy in fresh[:3] + old[:1] + small + old[1:] + fresh[3:]:
         copy.start()
-    rank = lax.axis_index("rep")
     parity = lax.axis_index("ep") % 2
-    bucket = jnp.int32(0)
-    for b in range(owner_ref.shape[1]):
-        bucket = jnp.where(owner_ref[0, b] == rank, b, bucket)
     m = steps * GROUP
     n = GROUP * cached
     factor = 1.0 / math.sqrt(DH)
@@ -80,9 +82,9 @@
     recent = (col % GROUP == row % GROUP) & (col // GROUP <= row // GROUP)
     row = lax.broadcasted_iota(jnp.int32, (m, rows), 0)
     col = lax.broadcasted_iota(jnp.int32, (m, rows), 1)
+    for copy in fresh[:3] + small[:1]:
+        copy.wait()
     lengths = len_ref[...].astype(F32)
-    for copy in fresh[:3]:
-        copy.wait()
     def score(g, h, live):
         part = slice(g * GROUP, (g + 1) * GROUP)
         cut = slice(h * DH, (h + 1) * DH)
@@ -133,6 +135,11 @@
     order = jnp.where(source == wanted, 1.0, 0.0).astype(BF16)
     h = jnp.dot(order, heads[...].reshape(every, width), preferred_element_type=F32)
     h = h.astype(BF16)
+    small[1].wait()
+    rank = lax.axis_index("rep")
+    bucket = jnp.int32(0)
+    for b in range(owner_ref.shape[1]):
+        bucket = jnp.where(owner_ref[0, b] == rank, b, bucket)
     fresh[3].wait()
     block = out_ref.shape[1]
     chips = half // mine
@@ -154,20 +161,23 @@
     operands = (queries, new_keys, new_values, cache_keys, cache_values, out)
     return pl.pallas_call(
         attention_kernel,
-        in_specs=[pl.BlockSpec(memory_space=SMEM), vm] + [hbm] * len(operands),
+        in_specs=[hbm] * (2 + len(operands)),
         out_specs=[vm, vm],
         out_shape=[jax.ShapeDtypeStruct(shape, BF16)] * 2,
-        scratch_shapes=[VMEM(x.shape, BF16) for x in operands]
+        scratch_shapes=[SMEM(owner.shape, jnp.int32), VMEM(lengths.shape, jnp.int32)]
+        + [VMEM(x.shape, BF16) for x in operands]
         + [
             VMEM((steps, rows, width), BF16),
-            pltpu.SemaphoreType.DMA((8,)),
+            pltpu.SemaphoreType.DMA((10,)),
         ],
         compiler_params=FETCH,
         name="attention",
     )(owner, lengths, *operands)
 
 
-def select_kernel(bucket_ref, res_ref, gain_ref, out_ref, norm):
+def select_kernel(bucket_any, res_ref, gain_ref, out_ref, norm, bucket_ref, sem):
+    fetch_buckets = pltpu.make_async_copy(bucket_any, bucket_ref, sem)
+    fetch_buckets.start()
     blocks, rows, block = res_ref.shape
     total = jnp.zeros((rows, block), F32)
     for b in range(blocks):
@@ -178,6 +188,7 @@
     for b in range(blocks):
         gain = gain_ref[:, b * block : (b + 1) * block]
         norm[b] = (res_ref[b].astype(F32) * scale * gain).astype(BF16)
+    fetch_buckets.wait()
     for c in range(out_ref.shape[0]):
         out_ref[c] = norm[bucket_ref[c]]
 
@@ -188,10 +199,14 @@
     vm = pl.BlockSpec(memory_space=VMEM)
     return pl.pallas_call(
         select_kernel,
-        in_specs=[pl.BlockSpec(memory_space=SMEM), vm, vm],
+        in_specs=[pl.BlockSpec(memory_space=pl.ANY), vm, vm],
         out_specs=vm,
         out_shape=jax.ShapeDtypeStruct((chips, rows, block), BF16),
-        scratch_shapes=[VMEM(residual.shape, BF16)],
+        scratch_shapes=[
+            VMEM(residual.shape, BF16),
+            SMEM(buckets.shape, jnp.int32),
+            pltpu.SemaphoreType.DMA,
+        ],
         compiler_params=ROOM,
         name="select",
     )(buckets, residual, gain)
@@ -254,7 +269,11 @@
     )(x, weight)
 
 
-def combine_kernel(bucket_ref, ids_ref, logits_ref, keep_ref, got_ref, out_ref, acc):
+def combine_kernel(
+    bucket_any, ids_ref, logits_ref, keep_ref, got_ref, out_ref, acc, bucket_ref, sem
+):
+    fetch_buckets = pltpu.make_async_copy(bucket_any, bucket_ref, sem)
+    fetch_buckets.start()
     chips, rows, block = keep_ref.shape
     steps = ids_ref.shape[0]
     ids = jnp.concatenate([ids_ref[t] for t in range(steps)], axis=0)
@@ -268,14 +287,13 @@
     for k in range(ids.shape[1]):
         share = share + jnp.where(ids[:, k : k + 1] == expert, weight[:, k : k + 1], 0.0)
     acc[...] = jnp.zeros_like(acc)
+    fetch_buckets.wait()
     for side, ref in enumerate((keep_ref, got_ref)):
         for c in range(chips):
             e = side * chips + c
             b = bucket_ref[e]
             acc[b] = acc[b] + share[:, e : e + 1] * ref[c].astype(F32)
-    done = acc[...].astype(BF16)
-    for r in range(out_ref.shape[0]):
-        out_ref[r] = done
+    out_ref[...] = acc[...].astype(BF16)
 
 
 def combine(buckets, ids, logits, keep, got, ranks):
@@ -283,10 +301,14 @@
     vm = pl.BlockSpec(memory_space=VMEM)
     return pl.pallas_call(
         combine_kernel,
-        in_specs=[pl.BlockSpec(memory_space=SMEM), vm, vm, vm, vm],
+        in_specs=[pl.BlockSpec(memory_space=pl.ANY), vm, vm, vm, vm],
         out_specs=vm,
-        out_shape=jax.ShapeDtypeStruct((ranks, ranks, rows, block), BF16),
-        scratch_shapes=[VMEM((ranks, rows, block), F32)],
+        out_shape=jax.ShapeDtypeStruct((ranks, rows, block), BF16),
+        scratch_shapes=[
+            VMEM((ranks, rows, block), F32),
+            SMEM(buckets.shape, jnp.int32),
+            pltpu.SemaphoreType.DMA,
+        ],
         compiler_params=ROOM,
         name="combine",
     )(buckets, ids, logits, keep, got)
@@ -392,7 +414,12 @@
     routed = combine(
         buckets, expert_ids, router_logits, back[:, :mine], swap(back[:, mine:]), n_rep
     )
-    return finish(over_rep(routed), residual, steps, own_rows)
+    near = [(j, j ^ 1) for j in range(n_rep)]
+    lines = [[j for j in range(n_rep) if j % 2 == k] for k in range(2)]
+    routed = (routed.astype(F32) + lax.ppermute(routed, "rep", near).astype(F32)).astype(BF16)
+    routed = jnp.broadcast_to(routed, (n_rep // 2,) + routed.shape)
+    routed = lax.all_to_all(routed, "rep", 0, 0, tiled=True, axis_index_groups=lines)
+    return finish(routed, residual, steps, own_rows)
 
 
 def solution(mesh):

time: 135 us -> 133 us (0.985)
  blocking collectives: 118 us -> 111 us
  waiting for transfers between devices: 3.15 us -> 6.92 us
  starting transfers between devices: 0.28 us -> 1.78 us
    all_to_all x4 -> x3, blocking collectives: 56.8 us -> 39.2 us  [over_rep(): return lax.all_to_all(x, 'rep', 0, 0, tiled=True)]
    all_to_all x0 -> x1, blocking collectives: none -> 10.9 us  [on_device(): lax.all_to_all(routed, 'rep', 0, 0, tiled=True, axis_index_groups=lines)]
    ppermute x0 -> x1, waiting for transfers between devices: none -> 3.77 us  [on_device(): lax.ppermute(routed, 'rep', near).astype(F32)]
    ppermute x0 -> x1, starting transfers between devices: none -> 1.51 us  [on_device(): lax.ppermute(routed, 'rep', near).astype(F32)]
  transfers between devices with their start and end apart: 3 -> 4, of which waited for: 2 -> 3; matrix products, arithmetic and copies ran while one was open for 0% -> 0% of each run, Pallas kernels for 2% -> 2%
where the time goes in v5:
time: 133 us; the launch traced here: 132 us
  blocking collectives  111 us (83%)
  Pallas kernels  10.3 us (8%)
  waiting for transfers between devices  6.92 us (5%)
  starting transfers between devices  1.78 us (1%)
    all_to_all x3, blocking collectives, across(): return lax.all_to_all(x, 'ep', 0, 0, tiled=True, axis_index_groups=cores)  60.8 us
    all_to_all x3, blocking collectives, over_rep(): return lax.all_to_all(x, 'rep', 0, 0, tiled=True)  39.2 us
    all_to_all x1, blocking collectives, on_device(): lax.all_to_all(routed, 'rep', 0, 0, tiled=True, axis_index_groups=lines)  10.9 us
    pallas_call x1, Pallas kernels, attention(): pl.pallas_call(attention_kernel, in_specs=[hbm] * (2 + len(operands)), ou...  3.81 us
    ppermute x1, waiting for transfers between devices, on_device(): lax.ppermute(routed, 'rep', near).astype(F32)  3.77 us
    ppermute x3, waiting for transfers between devices, swap(): return lax.ppermute(x, 'ep', pair)  3.15 us
  transfers between devices with their start and end apart: 4, of which 3 were waited for; matrix products, arithmetic and copies ran while one was open for 0% of the time, Pallas kernels for 2%

profile of v5, /device:TPU:8, one launch (start us, length us, event | category | flops | bytes accessed | tf_op | source)
XLA Modules:
  0.0 131.9 jit_solution(3558157395177398677)
XLA Ops:
  0.0 3.8 %attention.1 = (bf16[16,8,1024]{2,1,0:T(8,128)(2,1)}, bf16[16,8,1024]{2,1,0:T(8,128)(2,1)}) custom-call(s32[1,8]{1,0:T(1,128)} %owner_hbm.1, s32[1,64]{1,0:T(1,128)} %bitcast.25, bf16[4,64,256]{2,1,0:T(8,128)(2,1)} %q_hbm.1, bf16[4,64,256]{2,1,0:T(8,128)(2,1)} %kn_hbm.1, bf16[4,64,256]{2,1,0:T(8,128)(2,1)} %vn_hbm.1, bf16[64,32,256]{2,1,0:T(8,128)(2,1)} %ck_hbm.1, ...), custom_call_target="tpu_custom_call" | custom-call | tf_op jit(solution)/shard_map/attention/pallas_call | solution.py:162
  3.8 0.1 collective-permute-start
  4.0 1.7 %collective-permute-done = bf16[16,8,1024]{2,1,0:T(8,128)(2,1)S(1)} collective-permute-done((bf16[16,8,1024]{2,1,0:T(8,128)(2,1)}, bf16[16,8,1024]{2,1,0:T(8,128)(2,1)S(1)}, u32[]{:S(2)}, u32[]{:S(2)}) %collective-permute-start) | collective-permute-done | bytes 262176 | tf_op jit(solution)/shard_map/ppermute | solution.py:368
  5.7 1.0 add_convert_fusion
  6.7 22.1 %all_to_all.35 = bf16[16,8,1024]{2,1,0:T(8,128)(2,1)S(1)} all-to-all(bf16[16,8,1024]{2,1,0:T(8,128)(2,1)S(1)} %add_convert_fusion), channel_id=1, replica_groups={{0,2,4,6,8,10,12,14,16,18,20,22,24,26,28,30},{1,3,5,7,9,11,13,15,17,19,..., dimensions={0} | all-to-all | bytes 524288 | tf_op jit(solution)/shard_map/all_to_all | solution.py:371
  28.9 0.1 collective-permute-start.1
  29.0 0.1 reshape.24.bucket_any
  29.1 2.1 %fetch.1.w_ref = bf16[2,896,1024]{2,1,0:T(8,128)(2,1)S(1)} custom-call(bf16[3,896,1024]{2,1,0:T(8,128)(2,1)} %bitcast.14), custom_call_target="tpu_custom_call" | custom-call | tf_op jit(solution)/shard_map/fetch/pallas_call | solution.py:222
  31.2 12.0 %all_to_all.36.res_ref = bf16[8,16,896]{2,1,0:T(8,128)(2,1)S(1)} all-to-all(bf16[8,16,896]{2,1,0:T(8,128)(2,1)S(1)} %broadcast_in_dim.13), channel_id=1, replica_groups=mesh['rep'=8,'ep'=32] {'rep'}, dimensions={0} | all-to-all | bytes 458752 | tf_op jit(solution)/shard_map/all_to_all | solution.py:374
  43.2 0.6 select.1
  43.8 19.5 %all_to_all.37 = bf16[16,16,896]{2,1,0:T(8,128)(2,1)S(1)} all-to-all(bf16[16,16,896]{2,1,0:T(8,128)(2,1)S(1)} %select.1), channel_id=1, replica_groups={{0,2,4,6,8,10,12,14,16,18,20,22,24,26,28,30},{1,3,5,7,9,11,13,15,17,19,..., dimensions={0} | all-to-all | bytes 917504 | tf_op jit(solution)/shard_map/all_to_all | solution.py:371
  63.2 1.2 gate_up.1
  64.5 16.1 %all_to_all.38 = bf16[8,32,2048]{2,1,0:T(8,128)(2,1)S(1)} all-to-all(bf16[8,32,2048]{2,1,0:T(8,128)(2,1)S(1)} %bitcast.18), channel_id=1, replica_groups=mesh['rep'=8,'ep'=32] {'rep'}, dimensions={0} | all-to-all | bytes 2097152 | tf_op jit(solution)/shard_map/all_to_all | solution.py:374
  80.6 0.1 convert_reduce_fusion
  80.8 11.2 %all_to_all.39 = bf16[8,32,1024]{2,1,0:T(8,128)(2,1)S(1)} all-to-all(bf16[8,32,1024]{2,1,0:T(8,128)(2,1)S(1)} %broadcast_in_dim.14), channel_id=1, replica_groups=mesh['rep'=8,'ep'=32] {'rep'}, dimensions={0} | all-to-all | bytes 1048576 | tf_op jit(solution)/shard_map/all_to_all | solution.py:374
  92.1 1.1 down.1
  93.2 19.3 %all_to_all.40 = bf16[16,16,896]{2,1,0:T(8,128)(2,1)S(1)} all-to-all(bf16[16,16,896]{2,1,0:T(8,128)(2,1)S(1)} %bitcast.21), channel_id=1, replica_groups={{0,2,4,6,8,10,12,14,16,18,20,22,24,26,28,30},{1,3,5,7,9,11,13,15,17,19,..., dimensions={0} | all-to-all | bytes 917504 | tf_op jit(solution)/shard_map/all_to_all | solution.py:371
  112.5 0.1 collective-permute-start.2
  112.6 1.5 %collective-permute-done.2.got_ref = bf16[16,8,896]{2,1,0:T(8,128)(2,1)S(1)} collective-permute-done((bf16[16,8,896]{2,1,0:T(8,128)(2,1)S(1)}, bf16[16,8,896]{2,1,0:T(8,128)(2,1)S(1)}, u32[]{:S(2)}, u32[]{:S(2)}) %collective-permute-start.2) | collective-permute-done | bytes 229408 | tf_op jit(solution)/shard_map/ppermute | solution.py:368
  114.1 0.8 combine.1
  114.9 1.5 %collective-permute-start.3 = (bf16[8,8,896]{2,1,0:T(8,128)(2,1)S(1)}, bf16[8,8,896]{2,1,0:T(8,128)(2,1)S(1)}, u32[]{:S(2)}, u32[]{:S(2)}) collective-permute-start(bf16[8,8,896]{2,1,0:T(8,128)(2,1)S(1)} %combine.1), channel_id=1, source_target_pairs={{0,32},{32,0},{64,96},{96,64},{128,160},{160,128},{192,224},{224,1... | collective-permute-start | bytes 344072 | tf_op jit(solution)/shard_map/ppermute | solution.py:419
  116.4 3.8 %collective-permute-done.3 = bf16[8,8,896]{2,1,0:T(8,128)(2,1)S(1)} collective-permute-done((bf16[8,8,896]{2,1,0:T(8,128)(2,1)S(1)}, bf16[8,8,896]{2,1,0:T(8,128)(2,1)S(1)}, u32[]{:S(2)}, u32[]{:S(2)}) %collective-permute-start.3) | collective-permute-done | bytes 114720 | tf_op jit(solution)/shard_map/ppermute | solution.py:419
  120.2 10.9 %all_to_all.41.part_ref = bf16[4,8,8,896]{3,2,1,0:T(8,128)(2,1)S(1)} all-to-all(bf16[4,8,8,896]{3,2,1,0:T(8,128)(2,1)S(1)} %broadcast_in_dim.15), channel_id=1, replica_groups={{0,64,128,192},{32,96,160,224},{1,65,129,193},{33,97,161,225},{2,66,130..., dimensions={0} | all-to-all | bytes 917504 | tf_op jit(solution)/shard_map/all_to_all | solution.py:421
  131.1 0.7 finish.1
  (28 shorter events, 0.4 us)
Async XLA Ops:
  0.0 3.9 %copy-start = (bf16[4,2,7168]{2,1,0:T(2,128)(2,1)S(1)}, bf16[4,2,7168]{2,1,0:T(2,128)(2,1)}, u32[]{:S(2)}) copy-start(bf16[4,2,7168]{2,1,0:T(2,128)(2,1)} %param.13) | copy-start | bytes 344068
  3.8 1.8 %collective-permute-start = (bf16[16,8,1024]{2,1,0:T(8,128)(2,1)}, bf16[16,8,1024]{2,1,0:T(8,128)(2,1)S(1)}, u32[]{:S(2)}, u32[]{:S(2)}) collective-permute-start(bf16[16,8,1024]{2,1,0:T(8,128)(2,1)} %get-tuple-element.16), channel_id=1, source_target_pairs={{0,1},{1,0},{2,3},{3,2},{4,5},{5,4},{6,7},{7,6},{8,9},{9,8},{10,11... | collective-permute-start | bytes 786440 | tf_op jit(solution)/shard_map/ppermute | solution.py:368
  28.9 2.3 %collective-permute-start.1 = (bf16[8,896]{1,0:T(8,128)(2,1)S(1)}, bf16[8,896]{1,0:T(8,128)(2,1)S(1)}, u32[]{:S(2)}, u32[]{:S(2)}) collective-permute-start(bf16[8,896]{1,0:T(8,128)(2,1)S(1)} %add_convert_fusion.2), channel_id=1, source_target_pairs={{0,1},{1,0},{2,3},{3,2},{4,5},{5,4},{6,7},{7,6},{8,9},{9,8},{10,11... | collective-permute-start | bytes 43016 | tf_op jit(solution)/shard_map/ppermute | solution.py:368
  29.1 14.1 %copy-start.1 = (f32[7168]{0:T(1024)S(1)}, f32[7168]{0:T(1024)}, u32[]{:S(2)}) copy-start(f32[7168]{0:T(1024)} %param.22) | copy-start | bytes 86020
  43.8 48.3 %slice-start = ((s8[5505024]{0:T(1024)(128)(4,1)}), s8[4194304]{0:T(1024)(128)(4,1)S(1)}, s32[]{:S(2)}) async-start(s8[5505024]{0:T(1024)(128)(4,1)} %bitcast.15), calls=%async_computation.7 | async-start | bytes 8388608
  63.2 28.8 %slice-start.1 = ((s8[5505024]{0:T(1024)(128)(4,1)}), s8[1310720]{0:T(1024)(128)(4,1)S(1)}, s32[]{:S(2)}) async-start(s8[5505024]{0:T(1024)(128)(4,1)} %bitcast.15), calls=%async_computation.8 | async-start | bytes 2621440
  92.0 22.0 %copy-start.2 = (s32[4,2,8]{2,1,0:T(2,128)S(1)}, s32[4,2,8]{2,1,0:T(2,128)}, u32[]{:S(2)}) copy-start(s32[4,2,8]{2,1,0:T(2,128)} %ids_ref.1) | copy-start | bytes 772
  92.0 22.0 %copy-start.3 = (f32[4,2,8]{2,1,0:T(2,128)S(1)}, f32[4,2,8]{2,1,0:T(2,128)}, u32[]{:S(2)}) copy-start(f32[4,2,8]{2,1,0:T(2,128)} %logits_ref.1) | copy-start | bytes 772
  112.5 1.6 %collective-permute-start.2 = (bf16[16,8,896]{2,1,0:T(8,128)(2,1)S(1)}, bf16[16,8,896]{2,1,0:T(8,128)(2,1)S(1)}, u32[]{:S(2)}, u32[]{:S(2)}) collective-permute-start(bf16[16,8,896]{2,1,0:T(8,128)(2,1)S(1)} %get-tuple-element.25), channel_id=1, source_target_pairs={{0,1},{1,0},{2,3},{3,2},{4,5},{5,4},{6,7},{7,6},{8,9},{9,8},{10,11... | collective-permute-start | bytes 688136 | tf_op jit(solution)/shard_map/ppermute | solution.py:368
  114.9 5.3 %collective-permute-start.3 = (bf16[8,8,896]{2,1,0:T(8,128)(2,1)S(1)}, bf16[8,8,896]{2,1,0:T(8,128)(2,1)S(1)}, u32[]{:S(2)}, u32[]{:S(2)}) collective-permute-start(bf16[8,8,896]{2,1,0:T(8,128)(2,1)S(1)} %combine.1), channel_id=1, source_target_pairs={{0,32},{32,0},{64,96},{96,64},{128,160},{160,128},{192,224},{224,1... | collective-permute-start | bytes 344072 | tf_op jit(solution)/shard_map/ppermute | solution.py:419

commit v6 on v5

--- a/solution.py
+++ b/solution.py
@@ -270,7 +270,7 @@
 
 
 def combine_kernel(
-    bucket_any, ids_ref, logits_ref, keep_ref, got_ref, out_ref, acc, bucket_ref, sem
+    bucket_any, ids_ref, logits_ref, keep_ref, got_ref, low_ref, high_ref, acc, bucket_ref, sem
 ):
     fetch_buckets = pltpu.make_async_copy(bucket_any, bucket_ref, sem)
     fetch_buckets.start()
@@ -293,7 +293,9 @@
             e = side * chips + c
             b = bucket_ref[e]
             acc[b] = acc[b] + share[:, e : e + 1] * ref[c].astype(F32)
-    out_ref[...] = acc[...].astype(BF16)
+    half = low_ref.shape[0]
+    low_ref[...] = acc[:half].astype(BF16)
+    high_ref[...] = acc[half:].astype(BF16)
 
 
 def combine(buckets, ids, logits, keep, got, ranks):
@@ -302,8 +304,8 @@
     return pl.pallas_call(
         combine_kernel,
         in_specs=[pl.BlockSpec(memory_space=pl.ANY), vm, vm, vm, vm],
-        out_specs=vm,
-        out_shape=jax.ShapeDtypeStruct((ranks, rows, block), BF16),
+        out_specs=[vm, vm],
+        out_shape=[jax.ShapeDtypeStruct((ranks // 2, rows, block), BF16)] * 2,
         scratch_shapes=[
             VMEM((ranks, rows, block), F32),
             SMEM(buckets.shape, jnp.int32),
@@ -314,29 +316,28 @@
     )(buckets, ids, logits, keep, got)
 
 
-def finish_kernel(part_ref, res_ref, out_ref):
-    ranks, blocks, rows, block = part_ref.shape
+def finish_kernel(low_ref, high_ref, res_ref, out_ref):
+    half, rows, block = low_ref.shape
     own = out_ref.shape[1]
-    for b in range(blocks):
-        x = res_ref[b, :rows].astype(F32)
-        for r in range(ranks):
-            x = x + part_ref[r, b].astype(F32)
+    for b in range(2 * half):
+        part = low_ref[b] if b < half else high_ref[b - half]
+        x = res_ref[b, :rows].astype(F32) + part.astype(F32)
         for t in range(out_ref.shape[0]):
             row = x[t * own : (t + 1) * own].astype(BF16)
             out_ref[t, :, b * block : (b + 1) * block] = row
 
 
-def finish(parts, residual, steps, own):
-    _, blocks, _, block = parts.shape
+def finish(low, high, residual, steps, own):
+    blocks, _, block = residual.shape
     vm = pl.BlockSpec(memory_space=VMEM)
     return pl.pallas_call(
         finish_kernel,
-        in_specs=[vm, vm],
+        in_specs=[vm, vm, vm],
         out_specs=vm,
         out_shape=jax.ShapeDtypeStruct((steps, own, blocks * block), BF16),
         compiler_params=ROOM,
         name="finish",
-    )(parts, residual)
+    )(low, high, residual)
 
 
 def on_device(
@@ -411,15 +412,21 @@
     activated = over_rep(jnp.broadcast_to(activated, (n_rep,) + activated.shape))
     result = down(activated.reshape(-1, hidden), weight)
     back = across(result.reshape(chips, 2 * mine, block))
-    routed = combine(
+    low, high = combine(
         buckets, expert_ids, router_logits, back[:, :mine], swap(back[:, mine:]), n_rep
     )
-    near = [(j, j ^ 1) for j in range(n_rep)]
-    lines = [[j for j in range(n_rep) if j % 2 == k] for k in range(2)]
-    routed = (routed.astype(F32) + lax.ppermute(routed, "rep", near).astype(F32)).astype(BF16)
-    routed = jnp.broadcast_to(routed, (n_rep // 2,) + routed.shape)
-    routed = lax.all_to_all(routed, "rep", 0, 0, tiled=True, axis_index_groups=lines)
-    return finish(routed, residual, steps, own_rows)
+    lines = n_rep // 2
+    turns = (
+        [(j, j ^ 1) for j in range(n_rep)],
+        [(j, j ^ 2) for j in range(n_rep)],
+        [(j, ((j // 2 + (1 if j // 2 % 2 else -1)) % lines) * 2 + j % 2) for j in range(n_rep)],
+    )
+    def add(x, turn):
+        return (x.astype(F32) + lax.ppermute(x, "rep", turn).astype(F32)).astype(BF16)
+
+    for i in range(3):
+        low, high = add(low, turns[i]), add(high, turns[(i + 1) % 3])
+    return finish(low, high, residual, steps, own_rows)
 
 
 def solution(mesh):

time: 133 us -> 132 us (level)
  blocking collectives: 111 us -> 100 us
  waiting for transfers between devices: 6.92 us -> 13.2 us
  starting transfers between devices: 1.78 us -> 5.92 us
    all_to_all x1 -> x0, blocking collectives: 10.9 us -> none  [on_device(): lax.all_to_all(routed, 'rep', 0, 0, tiled=True, axis_index_groups=lines)]
    ppermute x1 -> x6, waiting for transfers between devices: 3.77 us -> 10.1 us  [add(): lax.ppermute(x, 'rep', turn).astype(F32)]
    ppermute x1 -> x6, starting transfers between devices: 1.51 us -> 5.64 us  [add(): lax.ppermute(x, 'rep', turn).astype(F32)]
  transfers between devices with their start and end apart: 4 -> 9, of which waited for: 3 -> 8; matrix products, arithmetic and copies ran while one was open for 0% -> 0% of each run, Pallas kernels for 2% -> 2%
where the time goes in v6:
time: 132 us; the launch traced here: 131 us
  blocking collectives  100 us (76%)
  waiting for transfers between devices  13.2 us (10%)
  Pallas kernels  10.3 us (8%)
  starting transfers between devices  5.92 us (4%)
  other arithmetic  1.37 us (1%)
    all_to_all x3, blocking collectives, across(): return lax.all_to_all(x, 'ep', 0, 0, tiled=True, axis_index_groups=cores)  60.8 us
    all_to_all x3, blocking collectives, over_rep(): return lax.all_to_all(x, 'rep', 0, 0, tiled=True)  39.2 us
    ppermute x6, waiting for transfers between devices, add(): lax.ppermute(x, 'rep', turn).astype(F32)  10.1 us
    ppermute x6, starting transfers between devices, add(): lax.ppermute(x, 'rep', turn).astype(F32)  5.64 us
    pallas_call x1, Pallas kernels, attention(): pl.pallas_call(attention_kernel, in_specs=[hbm] * (2 + len(operands)), ou...  3.8 us
    ppermute x3, waiting for transfers between devices, swap(): return lax.ppermute(x, 'ep', pair)  3.15 us
  transfers between devices with their start and end apart: 9, of which 8 were waited for; matrix products, arithmetic and copies ran while one was open for 0% of the time, Pallas kernels for 2%

profile of v6, /device:TPU:8, one launch (start us, length us, event | category | flops | bytes accessed | tf_op | source)
XLA Modules:
  0.0 131.4 jit_solution(9370302521999804201)
XLA Ops:
  0.0 3.8 %attention.1 = (bf16[16,8,1024]{2,1,0:T(8,128)(2,1)}, bf16[16,8,1024]{2,1,0:T(8,128)(2,1)}) custom-call(s32[1,8]{1,0:T(1,128)} %owner_hbm.1, s32[1,64]{1,0:T(1,128)} %bitcast.25, bf16[4,64,256]{2,1,0:T(8,128)(2,1)} %q_hbm.1, bf16[4,64,256]{2,1,0:T(8,128)(2,1)} %kn_hbm.1, bf16[4,64,256]{2,1,0:T(8,128)(2,1)} %vn_hbm.1, bf16[64,32,256]{2,1,0:T(8,128)(2,1)} %ck_hbm.1, ...), custom_call_target="tpu_custom_call" | custom-call | tf_op jit(solution)/shard_map/attention/pallas_call | solution.py:162
  4.0 1.7 %collective-permute-done = bf16[16,8,1024]{2,1,0:T(8,128)(2,1)S(1)} collective-permute-done((bf16[16,8,1024]{2,1,0:T(8,128)(2,1)}, bf16[16,8,1024]{2,1,0:T(8,128)(2,1)S(1)}, u32[]{:S(2)}, u32[]{:S(2)}) %collective-permute-start) | collective-permute-done | bytes 262176 | tf_op jit(solution)/shard_map/ppermute | solution.py:369
  5.6 1.0 add_convert_fusion
  6.7 22.1 %all_to_all.30 = bf16[16,8,1024]{2,1,0:T(8,128)(2,1)S(1)} all-to-all(bf16[16,8,1024]{2,1,0:T(8,128)(2,1)S(1)} %add_convert_fusion), channel_id=1, replica_groups={{0,2,4,6,8,10,12,14,16,18,20,22,24,26,28,30},{1,3,5,7,9,11,13,15,17,19,..., dimensions={0} | all-to-all | bytes 524288 | tf_op jit(solution)/shard_map/all_to_all | solution.py:372
  29.1 2.1 %fetch.1.w_ref = bf16[2,896,1024]{2,1,0:T(8,128)(2,1)S(1)} custom-call(bf16[3,896,1024]{2,1,0:T(8,128)(2,1)} %bitcast.14), custom_call_target="tpu_custom_call" | custom-call | tf_op jit(solution)/shard_map/fetch/pallas_call | solution.py:222
  31.2 12.0 %all_to_all.31.res_ref = bf16[8,16,896]{2,1,0:T(8,128)(2,1)S(1)} all-to-all(bf16[8,16,896]{2,1,0:T(8,128)(2,1)S(1)} %broadcast_in_dim.10), channel_id=1, replica_groups=mesh['rep'=8,'ep'=32] {'rep'}, dimensions={0} | all-to-all | bytes 458752 | tf_op jit(solution)/shard_map/all_to_all | solution.py:375
  43.8 19.5 %all_to_all.32 = bf16[16,16,896]{2,1,0:T(8,128)(2,1)S(1)} all-to-all(bf16[16,16,896]{2,1,0:T(8,128)(2,1)S(1)} %select.1), channel_id=1, replica_groups={{0,2,4,6,8,10,12,14,16,18,20,22,24,26,28,30},{1,3,5,7,9,11,13,15,17,19,..., dimensions={0} | all-to-all | bytes 917504 | tf_op jit(solution)/shard_map/all_to_all | solution.py:372
  63.2 1.2 gate_up.1
  64.5 16.1 %all_to_all.33 = bf16[8,32,2048]{2,1,0:T(8,128)(2,1)S(1)} all-to-all(bf16[8,32,2048]{2,1,0:T(8,128)(2,1)S(1)} %bitcast.18), channel_id=1, replica_groups=mesh['rep'=8,'ep'=32] {'rep'}, dimensions={0} | all-to-all | bytes 2097152 | tf_op jit(solution)/shard_map/all_to_all | solution.py:375
  80.8 11.2 %all_to_all.34 = bf16[8,32,1024]{2,1,0:T(8,128)(2,1)S(1)} all-to-all(bf16[8,32,1024]{2,1,0:T(8,128)(2,1)S(1)} %broadcast_in_dim.11), channel_id=1, replica_groups=mesh['rep'=8,'ep'=32] {'rep'}, dimensions={0} | all-to-all | bytes 1048576 | tf_op jit(solution)/shard_map/all_to_all | solution.py:375
  92.0 1.1 down.1
  93.2 19.3 %all_to_all.35 = bf16[16,16,896]{2,1,0:T(8,128)(2,1)S(1)} all-to-all(bf16[16,16,896]{2,1,0:T(8,128)(2,1)S(1)} %bitcast.21), channel_id=1, replica_groups={{0,2,4,6,8,10,12,14,16,18,20,22,24,26,28,30},{1,3,5,7,9,11,13,15,17,19,..., dimensions={0} | all-to-all | bytes 917504 | tf_op jit(solution)/shard_map/all_to_all | solution.py:372
  112.6 1.5 %collective-permute-done.2.got_ref = bf16[16,8,896]{2,1,0:T(8,128)(2,1)S(1)} collective-permute-done((bf16[16,8,896]{2,1,0:T(8,128)(2,1)S(1)}, bf16[16,8,896]{2,1,0:T(8,128)(2,1)S(1)}, u32[]{:S(2)}, u32[]{:S(2)}) %collective-permute-start.2) | collective-permute-done | bytes 229408 | tf_op jit(solution)/shard_map/ppermute | solution.py:369
  114.0 0.8 combine.1
  114.8 1.5 %collective-permute-start.3 = (bf16[4,8,896]{2,1,0:T(8,128)(2,1)S(1)}, bf16[4,8,896]{2,1,0:T(8,128)(2,1)S(1)}, u32[]{:S(2)}, u32[]{:S(2)}) collective-permute-start(bf16[4,8,896]{2,1,0:T(8,128)(2,1)S(1)} %get-tuple-element.27), channel_id=1, source_target_pairs={{0,32},{32,0},{64,96},{96,64},{128,160},{160,128},{192,224},{224,1... | collective-permute-start | bytes 172040 | tf_op jit(solution)/shard_map/ppermute | solution.py:425
  116.7 2.4 %collective-permute-done.3 = bf16[4,8,896]{2,1,0:T(8,128)(2,1)S(1)} collective-permute-done((bf16[4,8,896]{2,1,0:T(8,128)(2,1)S(1)}, bf16[4,8,896]{2,1,0:T(8,128)(2,1)S(1)}, u32[]{:S(2)}, u32[]{:S(2)}) %collective-permute-start.3) | collective-permute-done | bytes 57376 | tf_op jit(solution)/shard_map/ppermute | solution.py:425
  119.1 0.8 collective-permute-start.4
  120.5 1.3 collective-permute-start.7
  121.8 1.6 %collective-permute-done.4 = bf16[4,8,896]{2,1,0:T(8,128)(2,1)S(1)} collective-permute-done((bf16[4,8,896]{2,1,0:T(8,128)(2,1)S(1)}, bf16[4,8,896]{2,1,0:T(8,128)(2,1)S(1)}, u32[]{:S(2)}, u32[]{:S(2)}) %collective-permute-start.4) | collective-permute-done | bytes 57376 | tf_op jit(solution)/shard_map/ppermute | solution.py:425
  123.4 1.3 collective-permute-start.5
  124.7 1.7 %collective-permute-done.7 = bf16[4,8,896]{2,1,0:T(8,128)(2,1)S(1)} collective-permute-done((bf16[4,8,896]{2,1,0:T(8,128)(2,1)S(1)}, bf16[4,8,896]{2,1,0:T(8,128)(2,1)S(1)}, u32[]{:S(2)}, u32[]{:S(2)}) %collective-permute-start.7) | collective-permute-done | bytes 57376 | tf_op jit(solution)/shard_map/ppermute | solution.py:425
  126.9 2.0 %collective-permute-done.5 = bf16[4,8,896]{2,1,0:T(8,128)(2,1)S(1)} collective-permute-done((bf16[4,8,896]{2,1,0:T(8,128)(2,1)S(1)}, bf16[4,8,896]{2,1,0:T(8,128)(2,1)S(1)}, u32[]{:S(2)}, u32[]{:S(2)}) %collective-permute-start.5) | collective-permute-done | bytes 57376 | tf_op jit(solution)/shard_map/ppermute | solution.py:425
  128.9 1.8 %collective-permute-done.8 = bf16[4,8,896]{2,1,0:T(8,128)(2,1)S(1)} collective-permute-done((bf16[4,8,896]{2,1,0:T(8,128)(2,1)S(1)}, bf16[4,8,896]{2,1,0:T(8,128)(2,1)S(1)}, u32[]{:S(2)}, u32[]{:S(2)}) %collective-permute-start.8) | collective-permute-done | bytes 57376 | tf_op jit(solution)/shard_map/ppermute | solution.py:425
  130.7 0.7 finish.1
  (41 shorter events, 3.0 us)
Async XLA Ops:
  0.0 3.9 %copy-start = (bf16[4,2,7168]{2,1,0:T(2,128)(2,1)S(1)}, bf16[4,2,7168]{2,1,0:T(2,128)(2,1)}, u32[]{:S(2)}) copy-start(bf16[4,2,7168]{2,1,0:T(2,128)(2,1)} %param.13) | copy-start | bytes 344068
  3.8 1.8 %collective-permute-start = (bf16[16,8,1024]{2,1,0:T(8,128)(2,1)}, bf16[16,8,1024]{2,1,0:T(8,128)(2,1)S(1)}, u32[]{:S(2)}, u32[]{:S(2)}) collective-permute-start(bf16[16,8,1024]{2,1,0:T(8,128)(2,1)} %get-tuple-element.18), channel_id=1, source_target_pairs={{0,1},{1,0},{2,3},{3,2},{4,5},{5,4},{6,7},{7,6},{8,9},{9,8},{10,11... | collective-permute-start | bytes 786440 | tf_op jit(solution)/shard_map/ppermute | solution.py:369
  28.9 2.3 %collective-permute-start.1 = (bf16[8,896]{1,0:T(8,128)(2,1)S(1)}, bf16[8,896]{1,0:T(8,128)(2,1)S(1)}, u32[]{:S(2)}, u32[]{:S(2)}) collective-permute-start(bf16[8,896]{1,0:T(8,128)(2,1)S(1)} %add_convert_fusion.7), channel_id=1, source_target_pairs={{0,1},{1,0},{2,3},{3,2},{4,5},{5,4},{6,7},{7,6},{8,9},{9,8},{10,11... | collective-permute-start | bytes 43016 | tf_op jit(solution)/shard_map/ppermute | solution.py:369
  29.1 14.1 %copy-start.1 = (f32[7168]{0:T(1024)S(1)}, f32[7168]{0:T(1024)}, u32[]{:S(2)}) copy-start(f32[7168]{0:T(1024)} %param.22) | copy-start | bytes 86020
  43.7 48.3 %slice-start = ((s8[5505024]{0:T(1024)(128)(4,1)}), s8[4194304]{0:T(1024)(128)(4,1)S(1)}, s32[]{:S(2)}) async-start(s8[5505024]{0:T(1024)(128)(4,1)} %bitcast.15), calls=%async_computation.6 | async-start | bytes 8388608
  63.2 28.8 %slice-start.1 = ((s8[5505024]{0:T(1024)(128)(4,1)}), s8[1310720]{0:T(1024)(128)(4,1)S(1)}, s32[]{:S(2)}) async-start(s8[5505024]{0:T(1024)(128)(4,1)} %bitcast.15), calls=%async_computation.7 | async-start | bytes 2621440
  92.0 22.0 %copy-start.2 = (s32[4,2,8]{2,1,0:T(2,128)S(1)}, s32[4,2,8]{2,1,0:T(2,128)}, u32[]{:S(2)}) copy-start(s32[4,2,8]{2,1,0:T(2,128)} %ids_ref.1) | copy-start | bytes 772
  92.0 22.0 %copy-start.3 = (f32[4,2,8]{2,1,0:T(2,128)S(1)}, f32[4,2,8]{2,1,0:T(2,128)}, u32[]{:S(2)}) copy-start(f32[4,2,8]{2,1,0:T(2,128)} %logits_ref.1) | copy-start | bytes 772
  112.5 1.6 %collective-permute-start.2 = (bf16[16,8,896]{2,1,0:T(8,128)(2,1)S(1)}, bf16[16,8,896]{2,1,0:T(8,128)(2,1)S(1)}, u32[]{:S(2)}, u32[]{:S(2)}) collective-permute-start(bf16[16,8,896]{2,1,0:T(8,128)(2,1)S(1)} %get-tuple-element.29), channel_id=1, source_target_pairs={{0,1},{1,0},{2,3},{3,2},{4,5},{5,4},{6,7},{7,6},{8,9},{9,8},{10,11... | collective-permute-start | bytes 688136 | tf_op jit(solution)/shard_map/ppermute | solution.py:369
  114.8 4.3 %collective-permute-start.3 = (bf16[4,8,896]{2,1,0:T(8,128)(2,1)S(1)}, bf16[4,8,896]{2,1,0:T(8,128)(2,1)S(1)}, u32[]{:S(2)}, u32[]{:S(2)}) collective-permute-start(bf16[4,8,896]{2,1,0:T(8,128)(2,1)S(1)} %get-tuple-element.27), channel_id=1, source_target_pairs={{0,32},{32,0},{64,96},{96,64},{128,160},{160,128},{192,224},{224,1... | collective-permute-start | bytes 172040 | tf_op jit(solution)/shard_map/ppermute | solution.py:425
  116.3 4.2 %collective-permute-start.6 = (bf16[4,8,896]{2,1,0:T(8,128)(2,1)S(1)}, bf16[4,8,896]{2,1,0:T(8,128)(2,1)S(1)}, u32[]{:S(2)}, u32[]{:S(2)}) collective-permute-start(bf16[4,8,896]{2,1,0:T(8,128)(2,1)S(1)} %get-tuple-element.28), channel_id=1, source_target_pairs={{0,64},{32,96},{64,0},{96,32},{128,192},{160,224},{192,128},{224,1... | collective-permute-start | bytes 172040 | tf_op jit(solution)/shard_map/ppermute | solution.py:425
  119.1 4.3 %collective-permute-start.4 = (bf16[4,8,896]{2,1,0:T(8,128)(2,1)S(1)}, bf16[4,8,896]{2,1,0:T(8,128)(2,1)S(1)}, u32[]{:S(2)}, u32[]{:S(2)}) collective-permute-start(bf16[4,8,896]{2,1,0:T(8,128)(2,1)S(1)} %add_convert_fusion.6), channel_id=1, source_target_pairs={{0,64},{32,96},{64,0},{96,32},{128,192},{160,224},{192,128},{224,1... | collective-permute-start | bytes 172040 | tf_op jit(solution)/shard_map/ppermute | solution.py:425
  120.5 5.8 %collective-permute-start.7 = (bf16[4,8,896]{2,1,0:T(8,128)(2,1)S(1)}, bf16[4,8,896]{2,1,0:T(8,128)(2,1)S(1)}, u32[]{:S(2)}, u32[]{:S(2)}) collective-permute-start(bf16[4,8,896]{2,1,0:T(8,128)(2,1)S(1)} %add_convert_fusion.3), channel_id=1, source_target_pairs={{0,192},{32,224},{64,128},{96,160},{128,64},{160,96},{192,0},{224,... | collective-permute-start | bytes 172040 | tf_op jit(solution)/shard_map/ppermute | solution.py:425
  123.4 5.5 %collective-permute-start.5 = (bf16[4,8,896]{2,1,0:T(8,128)(2,1)S(1)}, bf16[4,8,896]{2,1,0:T(8,128)(2,1)S(1)}, u32[]{:S(2)}, u32[]{:S(2)}) collective-permute-start(bf16[4,8,896]{2,1,0:T(8,128)(2,1)S(1)} %add_convert_fusion.5), channel_id=1, source_target_pairs={{0,192},{32,224},{64,128},{96,160},{128,64},{160,96},{192,0},{224,... | collective-permute-start | bytes 172040 | tf_op jit(solution)/shard_map/ppermute | solution.py:425
  126.4 4.3 %collective-permute-start.8 = (bf16[4,8,896]{2,1,0:T(8,128)(2,1)S(1)}, bf16[4,8,896]{2,1,0:T(8,128)(2,1)S(1)}, u32[]{:S(2)}, u32[]{:S(2)}) collective-permute-start(bf16[4,8,896]{2,1,0:T(8,128)(2,1)S(1)} %add_convert_fusion.2), channel_id=1, source_target_pairs={{0,32},{32,0},{64,96},{96,64},{128,160},{160,128},{192,224},{224,1... | collective-permute-start | bytes 172040 | tf_op jit(solution)/shard_map/ppermute | solution.py:425

commit v7 on v6

--- a/solution.py
+++ b/solution.py
@@ -1,3 +1,4 @@
+import functools
 import math
 
 import jax
@@ -269,51 +270,58 @@
     )(x, weight)
 
 
-def combine_kernel(
-    bucket_any, ids_ref, logits_ref, keep_ref, got_ref, low_ref, high_ref, acc, bucket_ref, sem
-):
+def combine_kernel(side, bucket_any, ids_ref, logits_ref, part_ref, *rest):
+    *given, bucket_ref, sem = rest
     fetch_buckets = pltpu.make_async_copy(bucket_any, bucket_ref, sem)
     fetch_buckets.start()
-    chips, rows, block = keep_ref.shape
+    chips, rows, block = part_ref.shape
     steps = ids_ref.shape[0]
     ids = jnp.concatenate([ids_ref[t] for t in range(steps)], axis=0)
     logits = jnp.concatenate([logits_ref[t] for t in range(steps)], axis=0)
     affinity = 1.0 / (1.0 + jnp.exp(-logits))
     weight = ROUTE_SCALE * affinity / jnp.sum(affinity, axis=1, keepdims=True)
     parity = lax.axis_index("ep") % 2
-    col = lax.broadcasted_iota(jnp.int32, (rows, 2 * chips), 1)
-    expert = jnp.where(col < chips, 2 * col + parity, 2 * (col - chips) + 1 - parity)
-    share = jnp.zeros((rows, 2 * chips), F32)
+    core = parity if side == 0 else 1 - parity
+    expert = 2 * lax.broadcasted_iota(jnp.int32, (rows, chips), 1) + core
+    share = jnp.zeros((rows, chips), F32)
     for k in range(ids.shape[1]):
         share = share + jnp.where(ids[:, k : k + 1] == expert, weight[:, k : k + 1], 0.0)
-    acc[...] = jnp.zeros_like(acc)
+    if side == 0:
+        (acc,) = given
+        acc[...] = jnp.zeros_like(acc)
+    else:
+        start_ref, low_ref, high_ref, acc = given
+        acc[...] = start_ref[...]
     fetch_buckets.wait()
-    for side, ref in enumerate((keep_ref, got_ref)):
-        for c in range(chips):
-            e = side * chips + c
-            b = bucket_ref[e]
-            acc[b] = acc[b] + share[:, e : e + 1] * ref[c].astype(F32)
-    half = low_ref.shape[0]
-    low_ref[...] = acc[:half].astype(BF16)
-    high_ref[...] = acc[half:].astype(BF16)
-
-
-def combine(buckets, ids, logits, keep, got, ranks):
-    _, rows, block = keep.shape
-    vm = pl.BlockSpec(memory_space=VMEM)
-    return pl.pallas_call(
-        combine_kernel,
-        in_specs=[pl.BlockSpec(memory_space=pl.ANY), vm, vm, vm, vm],
-        out_specs=[vm, vm],
-        out_shape=[jax.ShapeDtypeStruct((ranks // 2, rows, block), BF16)] * 2,
-        scratch_shapes=[
-            VMEM((ranks, rows, block), F32),
-            SMEM(buckets.shape, jnp.int32),
-            pltpu.SemaphoreType.DMA,
-        ],
+    for c in range(chips):
+        b = bucket_ref[side * chips + c]
+        acc[b] = acc[b] + share[:, c : c + 1] * part_ref[c].astype(F32)
+    if side == 1:
+        half = low_ref.shape[0]
+        low_ref[...] = acc[:half].astype(BF16)
+        high_ref[...] = acc[half:].astype(BF16)
+
+
+def combine(buckets, ids, logits, part, ranks, start=None):
+    _, rows, block = part.shape
+    vm = pl.BlockSpec(memory_space=VMEM)
+    shape = (ranks, rows, block)
+    small = [SMEM(buckets.shape, jnp.int32), pltpu.SemaphoreType.DMA]
+    if start is None:
+        side, operands, scratch = 0, (ids, logits, part), small
+        out_shape = [jax.ShapeDtypeStruct(shape, F32)]
+    else:
+        side, operands, scratch = 1, (ids, logits, part, start), [VMEM(shape, F32)] + small
+        out_shape = [jax.ShapeDtypeStruct((ranks // 2, rows, block), BF16)] * 2
+    return pl.pallas_call(
+        functools.partial(combine_kernel, side),
+        in_specs=[pl.BlockSpec(memory_space=pl.ANY)] + [vm] * len(operands),
+        out_specs=[vm] * len(out_shape),
+        out_shape=out_shape,
+        scratch_shapes=scratch,
         compiler_params=ROOM,
         name="combine",
-    )(buckets, ids, logits, keep, got)
+    )(buckets, *operands)
 
 
 def finish_kernel(low_ref, high_ref, res_ref, out_ref):
@@ -321,7 +329,7 @@
     own = out_ref.shape[1]
     for b in range(2 * half):
         part = low_ref[b] if b < half else high_ref[b - half]
-        x = res_ref[b, :rows].astype(F32) + part.astype(F32)
+        x = res_ref[b].astype(F32)[:rows] + part.astype(F32)
         for t in range(out_ref.shape[0]):
             row = x[t * own : (t + 1) * own].astype(BF16)
             out_ref[t, :, b * block : (b + 1) * block] = row
@@ -412,9 +420,9 @@
     activated = over_rep(jnp.broadcast_to(activated, (n_rep,) + activated.shape))
     result = down(activated.reshape(-1, hidden), weight)
     back = across(result.reshape(chips, 2 * mine, block))
-    low, high = combine(
-        buckets, expert_ids, router_logits, back[:, :mine], swap(back[:, mine:]), n_rep
-    )
+    got = swap(back[:, mine:])
+    (start,) = combine(buckets, expert_ids, router_logits, back[:, :mine], n_rep)
+    low, high = combine(buckets, expert_ids, router_logits, got, n_rep, start)
     lines = n_rep // 2
     turns = (
         [(j, j ^ 1) for j in range(n_rep)],

time: 132 us -> 132 us (level)
  no operation moved by 1% of the time
where the time goes in v7:
time: 132 us; the launch traced here: 131 us
  blocking collectives  100 us (76%)
  waiting for transfers between devices  12.5 us (9%)
  Pallas kernels  10.9 us (8%)
  starting transfers between devices  5.92 us (4%)
  other arithmetic  1.37 us (1%)
    all_to_all x3, blocking collectives, across(): return lax.all_to_all(x, 'ep', 0, 0, tiled=True, axis_index_groups=cores)  60.8 us
    all_to_all x3, blocking collectives, over_rep(): return lax.all_to_all(x, 'rep', 0, 0, tiled=True)  39.2 us
    ppermute x6, waiting for transfers between devices, add(): lax.ppermute(x, 'rep', turn).astype(F32)  10.1 us
    ppermute x6, starting transfers between devices, add(): lax.ppermute(x, 'rep', turn).astype(F32)  5.64 us
    pallas_call x1, Pallas kernels, attention(): pl.pallas_call(attention_kernel, in_specs=[hbm] * (2 + len(operands)), ou...  3.8 us
  transfers between devices with their start and end apart: 9, of which 8 were waited for; matrix products, arithmetic and copies ran while one was open for 0% of the time, Pallas kernels for 2%

profile of v7, /device:TPU:8, one launch (start us, length us, event | category | flops | bytes accessed | tf_op | source)
XLA Modules:
  0.0 131.3 jit_solution(7647667633556699451)
XLA Ops:
  0.0 3.8 %attention.1 = (bf16[16,8,1024]{2,1,0:T(8,128)(2,1)}, bf16[16,8,1024]{2,1,0:T(8,128)(2,1)}) custom-call(s32[1,8]{1,0:T(1,128)} %owner_hbm.1, s32[1,64]{1,0:T(1,128)} %bitcast.25, bf16[4,64,256]{2,1,0:T(8,128)(2,1)} %q_hbm.1, bf16[4,64,256]{2,1,0:T(8,128)(2,1)} %kn_hbm.1, bf16[4,64,256]{2,1,0:T(8,128)(2,1)} %vn_hbm.1, bf16[64,32,256]{2,1,0:T(8,128)(2,1)} %ck_hbm.1, ...), custom_call_target="tpu_custom_call" | custom-call | tf_op jit(solution)/shard_map/attention/pallas_call | solution.py:163
  4.0 1.7 %collective-permute-done = bf16[16,8,1024]{2,1,0:T(8,128)(2,1)S(1)} collective-permute-done((bf16[16,8,1024]{2,1,0:T(8,128)(2,1)}, bf16[16,8,1024]{2,1,0:T(8,128)(2,1)S(1)}, u32[]{:S(2)}, u32[]{:S(2)}) %collective-permute-start) | collective-permute-done | bytes 262176 | tf_op jit(solution)/shard_map/ppermute | solution.py:377
  5.6 1.0 add_convert_fusion
  6.7 22.1 %all_to_all.30 = bf16[16,8,1024]{2,1,0:T(8,128)(2,1)S(1)} all-to-all(bf16[16,8,1024]{2,1,0:T(8,128)(2,1)S(1)} %add_convert_fusion), channel_id=1, replica_groups={{0,2,4,6,8,10,12,14,16,18,20,22,24,26,28,30},{1,3,5,7,9,11,13,15,17,19,..., dimensions={0} | all-to-all | bytes 524288 | tf_op jit(solution)/shard_map/all_to_all | solution.py:380
  29.1 2.1 %fetch.1.w_ref = bf16[2,896,1024]{2,1,0:T(8,128)(2,1)S(1)} custom-call(bf16[3,896,1024]{2,1,0:T(8,128)(2,1)} %bitcast.14), custom_call_target="tpu_custom_call" | custom-call | tf_op jit(solution)/shard_map/fetch/pallas_call | solution.py:223
  31.2 12.0 %all_to_all.31.res_ref = bf16[8,16,896]{2,1,0:T(8,128)(2,1)S(1)} all-to-all(bf16[8,16,896]{2,1,0:T(8,128)(2,1)S(1)} %broadcast_in_dim.10), channel_id=1, replica_groups=mesh['rep'=8,'ep'=32] {'rep'}, dimensions={0} | all-to-all | bytes 458752 | tf_op jit(solution)/shard_map/all_to_all | solution.py:383
  43.8 19.5 %all_to_all.32 = bf16[16,16,896]{2,1,0:T(8,128)(2,1)S(1)} all-to-all(bf16[16,16,896]{2,1,0:T(8,128)(2,1)S(1)} %select.1), channel_id=1, replica_groups={{0,2,4,6,8,10,12,14,16,18,20,22,24,26,28,30},{1,3,5,7,9,11,13,15,17,19,..., dimensions={0} | all-to-all | bytes 917504 | tf_op jit(solution)/shard_map/all_to_all | solution.py:380
  63.2 1.2 gate_up.1
  64.5 16.1 %all_to_all.33 = bf16[8,32,2048]{2,1,0:T(8,128)(2,1)S(1)} all-to-all(bf16[8,32,2048]{2,1,0:T(8,128)(2,1)S(1)} %bitcast.18), channel_id=1, replica_groups=mesh['rep'=8,'ep'=32] {'rep'}, dimensions={0} | all-to-all | bytes 2097152 | tf_op jit(solution)/shard_map/all_to_all | solution.py:383
  80.8 11.2 %all_to_all.34 = bf16[8,32,1024]{2,1,0:T(8,128)(2,1)S(1)} all-to-all(bf16[8,32,1024]{2,1,0:T(8,128)(2,1)S(1)} %broadcast_in_dim.11), channel_id=1, replica_groups=mesh['rep'=8,'ep'=32] {'rep'}, dimensions={0} | all-to-all | bytes 1048576 | tf_op jit(solution)/shard_map/all_to_all | solution.py:383
  92.0 1.1 down.1
  93.2 19.3 %all_to_all.35 = bf16[16,16,896]{2,1,0:T(8,128)(2,1)S(1)} all-to-all(bf16[16,16,896]{2,1,0:T(8,128)(2,1)S(1)} %bitcast.21), channel_id=1, replica_groups={{0,2,4,6,8,10,12,14,16,18,20,22,24,26,28,30},{1,3,5,7,9,11,13,15,17,19,..., dimensions={0} | all-to-all | bytes 917504 | tf_op jit(solution)/shard_map/all_to_all | solution.py:380
  113.3 0.8 collective-permute-done.2.part_ref
  114.0 0.7 combine.3
  114.8 1.5 %collective-permute-start.3 = (bf16[4,8,896]{2,1,0:T(8,128)(2,1)S(1)}, bf16[4,8,896]{2,1,0:T(8,128)(2,1)S(1)}, u32[]{:S(2)}, u32[]{:S(2)}) collective-permute-start(bf16[4,8,896]{2,1,0:T(8,128)(2,1)S(1)} %get-tuple-element.27), channel_id=1, source_target_pairs={{0,32},{32,0},{64,96},{96,64},{128,160},{160,128},{192,224},{224,1... | collective-permute-start | bytes 172040 | tf_op jit(solution)/shard_map/ppermute | solution.py:433
  116.6 2.4 %collective-permute-done.3 = bf16[4,8,896]{2,1,0:T(8,128)(2,1)S(1)} collective-permute-done((bf16[4,8,896]{2,1,0:T(8,128)(2,1)S(1)}, bf16[4,8,896]{2,1,0:T(8,128)(2,1)S(1)}, u32[]{:S(2)}, u32[]{:S(2)}) %collective-permute-start.3) | collective-permute-done | bytes 57376 | tf_op jit(solution)/shard_map/ppermute | solution.py:433
  119.0 0.8 collective-permute-start.4
  120.5 1.3 collective-permute-start.7
  121.7 1.6 %collective-permute-done.4 = bf16[4,8,896]{2,1,0:T(8,128)(2,1)S(1)} collective-permute-done((bf16[4,8,896]{2,1,0:T(8,128)(2,1)S(1)}, bf16[4,8,896]{2,1,0:T(8,128)(2,1)S(1)}, u32[]{:S(2)}, u32[]{:S(2)}) %collective-permute-start.4) | collective-permute-done | bytes 57376 | tf_op jit(solution)/shard_map/ppermute | solution.py:433
  123.3 1.3 collective-permute-start.5
  124.6 1.7 %collective-permute-done.7 = bf16[4,8,896]{2,1,0:T(8,128)(2,1)S(1)} collective-permute-done((bf16[4,8,896]{2,1,0:T(8,128)(2,1)S(1)}, bf16[4,8,896]{2,1,0:T(8,128)(2,1)S(1)}, u32[]{:S(2)}, u32[]{:S(2)}) %collective-permute-start.7) | collective-permute-done | bytes 57376 | tf_op jit(solution)/shard_map/ppermute | solution.py:433
  126.8 2.0 %collective-permute-done.5 = bf16[4,8,896]{2,1,0:T(8,128)(2,1)S(1)} collective-permute-done((bf16[4,8,896]{2,1,0:T(8,128)(2,1)S(1)}, bf16[4,8,896]{2,1,0:T(8,128)(2,1)S(1)}, u32[]{:S(2)}, u32[]{:S(2)}) %collective-permute-start.5) | collective-permute-done | bytes 57376 | tf_op jit(solution)/shard_map/ppermute | solution.py:433
  128.8 1.8 %collective-permute-done.8 = bf16[4,8,896]{2,1,0:T(8,128)(2,1)S(1)} collective-permute-done((bf16[4,8,896]{2,1,0:T(8,128)(2,1)S(1)}, bf16[4,8,896]{2,1,0:T(8,128)(2,1)S(1)}, u32[]{:S(2)}, u32[]{:S(2)}) %collective-permute-start.8) | collective-permute-done | bytes 57376 | tf_op jit(solution)/shard_map/ppermute | solution.py:433
  130.6 0.7 finish.1
  (42 shorter events, 3.7 us)
Async XLA Ops:
  0.0 3.9 %copy-start = (bf16[4,2,7168]{2,1,0:T(2,128)(2,1)S(1)}, bf16[4,2,7168]{2,1,0:T(2,128)(2,1)}, u32[]{:S(2)}) copy-start(bf16[4,2,7168]{2,1,0:T(2,128)(2,1)} %param.13) | copy-start | bytes 344068
  3.8 1.8 %collective-permute-start = (bf16[16,8,1024]{2,1,0:T(8,128)(2,1)}, bf16[16,8,1024]{2,1,0:T(8,128)(2,1)S(1)}, u32[]{:S(2)}, u32[]{:S(2)}) collective-permute-start(bf16[16,8,1024]{2,1,0:T(8,128)(2,1)} %get-tuple-element.18), channel_id=1, source_target_pairs={{0,1},{1,0},{2,3},{3,2},{4,5},{5,4},{6,7},{7,6},{8,9},{9,8},{10,11... | collective-permute-start | bytes 786440 | tf_op jit(solution)/shard_map/ppermute | solution.py:377
  28.9 2.3 %collective-permute-start.1 = (bf16[8,896]{1,0:T(8,128)(2,1)S(1)}, bf16[8,896]{1,0:T(8,128)(2,1)S(1)}, u32[]{:S(2)}, u32[]{:S(2)}) collective-permute-start(bf16[8,896]{1,0:T(8,128)(2,1)S(1)} %add_convert_fusion.7), channel_id=1, source_target_pairs={{0,1},{1,0},{2,3},{3,2},{4,5},{5,4},{6,7},{7,6},{8,9},{9,8},{10,11... | collective-permute-start | bytes 43016 | tf_op jit(solution)/shard_map/ppermute | solution.py:377
  29.1 14.1 %copy-start.1 = (f32[7168]{0:T(1024)S(1)}, f32[7168]{0:T(1024)}, u32[]{:S(2)}) copy-start(f32[7168]{0:T(1024)} %param.22) | copy-start | bytes 86020
  43.7 48.3 %slice-start = ((s8[5505024]{0:T(1024)(128)(4,1)}), s8[4194304]{0:T(1024)(128)(4,1)S(1)}, s32[]{:S(2)}) async-start(s8[5505024]{0:T(1024)(128)(4,1)} %bitcast.15), calls=%async_computation.6 | async-start | bytes 8388608
  63.2 28.8 %slice-start.1 = ((s8[5505024]{0:T(1024)(128)(4,1)}), s8[1310720]{0:T(1024)(128)(4,1)S(1)}, s32[]{:S(2)}) async-start(s8[5505024]{0:T(1024)(128)(4,1)} %bitcast.15), calls=%async_computation.7 | async-start | bytes 2621440
  92.0 20.5 %copy-start.2 = (s32[4,2,8]{2,1,0:T(2,128)S(1)}, s32[4,2,8]{2,1,0:T(2,128)}, u32[]{:S(2)}) copy-start(s32[4,2,8]{2,1,0:T(2,128)} %ids_ref.3) | copy-start | bytes 772
  92.0 20.5 %copy-start.3 = (f32[4,2,8]{2,1,0:T(2,128)S(1)}, f32[4,2,8]{2,1,0:T(2,128)}, u32[]{:S(2)}) copy-start(f32[4,2,8]{2,1,0:T(2,128)} %logits_ref.3) | copy-start | bytes 772
  112.5 1.6 %collective-permute-start.2 = (bf16[16,8,896]{2,1,0:T(8,128)(2,1)S(1)}, bf16[16,8,896]{2,1,0:T(8,128)(2,1)S(1)}, u32[]{:S(2)}, u32[]{:S(2)}) collective-permute-start(bf16[16,8,896]{2,1,0:T(8,128)(2,1)S(1)} %get-tuple-element.30), channel_id=1, source_target_pairs={{0,1},{1,0},{2,3},{3,2},{4,5},{5,4},{6,7},{7,6},{8,9},{9,8},{10,11... | collective-permute-start | bytes 688136 | tf_op jit(solution)/shard_map/ppermute | solution.py:377
  114.8 4.3 %collective-permute-start.3 = (bf16[4,8,896]{2,1,0:T(8,128)(2,1)S(1)}, bf16[4,8,896]{2,1,0:T(8,128)(2,1)S(1)}, u32[]{:S(2)}, u32[]{:S(2)}) collective-permute-start(bf16[4,8,896]{2,1,0:T(8,128)(2,1)S(1)} %get-tuple-element.27), channel_id=1, source_target_pairs={{0,32},{32,0},{64,96},{96,64},{128,160},{160,128},{192,224},{224,1... | collective-permute-start | bytes 172040 | tf_op jit(solution)/shard_map/ppermute | solution.py:433
  116.3 4.2 %collective-permute-start.6 = (bf16[4,8,896]{2,1,0:T(8,128)(2,1)S(1)}, bf16[4,8,896]{2,1,0:T(8,128)(2,1)S(1)}, u32[]{:S(2)}, u32[]{:S(2)}) collective-permute-start(bf16[4,8,896]{2,1,0:T(8,128)(2,1)S(1)} %get-tuple-element.28), channel_id=1, source_target_pairs={{0,64},{32,96},{64,0},{96,32},{128,192},{160,224},{192,128},{224,1... | collective-permute-start | bytes 172040 | tf_op jit(solution)/shard_map/ppermute | solution.py:433
  119.0 4.3 %collective-permute-start.4 = (bf16[4,8,896]{2,1,0:T(8,128)(2,1)S(1)}, bf16[4,8,896]{2,1,0:T(8,128)(2,1)S(1)}, u32[]{:S(2)}, u32[]{:S(2)}) collective-permute-start(bf16[4,8,896]{2,1,0:T(8,128)(2,1)S(1)} %add_convert_fusion.6), channel_id=1, source_target_pairs={{0,64},{32,96},{64,0},{96,32},{128,192},{160,224},{192,128},{224,1... | collective-permute-start | bytes 172040 | tf_op jit(solution)/shard_map/ppermute | solution.py:433
  120.5 5.8 %collective-permute-start.7 = (bf16[4,8,896]{2,1,0:T(8,128)(2,1)S(1)}, bf16[4,8,896]{2,1,0:T(8,128)(2,1)S(1)}, u32[]{:S(2)}, u32[]{:S(2)}) collective-permute-start(bf16[4,8,896]{2,1,0:T(8,128)(2,1)S(1)} %add_convert_fusion.3), channel_id=1, source_target_pairs={{0,192},{32,224},{64,128},{96,160},{128,64},{160,96},{192,0},{224,... | collective-permute-start | bytes 172040 | tf_op jit(solution)/shard_map/ppermute | solution.py:433
  123.3 5.5 %collective-permute-start.5 = (bf16[4,8,896]{2,1,0:T(8,128)(2,1)S(1)}, bf16[4,8,896]{2,1,0:T(8,128)(2,1)S(1)}, u32[]{:S(2)}, u32[]{:S(2)}) collective-permute-start(bf16[4,8,896]{2,1,0:T(8,128)(2,1)S(1)} %add_convert_fusion.5), channel_id=1, source_target_pairs={{0,192},{32,224},{64,128},{96,160},{128,64},{160,96},{192,0},{224,... | collective-permute-start | bytes 172040 | tf_op jit(solution)/shard_map/ppermute | solution.py:433
  126.3 4.3 %collective-permute-start.8 = (bf16[4,8,896]{2,1,0:T(8,128)(2,1)S(1)}, bf16[4,8,896]{2,1,0:T(8,128)(2,1)S(1)}, u32[]{:S(2)}, u32[]{:S(2)}) collective-permute-start(bf16[4,8,896]{2,1,0:T(8,128)(2,1)S(1)} %add_convert_fusion.2), channel_id=1, source_target_pairs={{0,32},{32,0},{64,96},{96,64},{128,160},{160,128},{192,224},{224,1... | collective-permute-start | bytes 172040 | tf_op jit(solution)/shard_map/ppermute | solution.py:433

commit v8 on v7

--- a/solution.py
+++ b/solution.py
@@ -253,9 +253,10 @@
 
 
 def down_kernel(x_ref, w_ref, out_ref):
-    tile = 128
-    for j in range(0, w_ref.shape[1], tile):
-        out_ref[:, j : j + tile] = dot_nt(x_ref[...], w_ref[2, j : j + tile]).astype(BF16)
+    width = w_ref.shape[1]
+    for j in range(0, width, 256):
+        part = slice(j, min(j + 256, width))
+        out_ref[:, part] = dot_nt(x_ref[...], w_ref[2, part]).astype(BF16)
 
 
 def down(x, weight):

time: 132 us -> 131 us (level)
  no operation moved by 1% of the time
where the time goes in v8:
time: 131 us
  blocking collectives  100 us (76%)
  waiting for transfers between devices  12.5 us (10%)
  Pallas kernels  10.5 us (8%)
  starting transfers between devices  5.9 us (5%)
  other arithmetic  1.37 us (1%)
    all_to_all x3, blocking collectives, across(): return lax.all_to_all(x, 'ep', 0, 0, tiled=True, axis_index_groups=cores)  60.8 us
    all_to_all x3, blocking collectives, over_rep(): return lax.all_to_all(x, 'rep', 0, 0, tiled=True)  39.3 us
    ppermute x6, waiting for transfers between devices, add(): lax.ppermute(x, 'rep', turn).astype(F32)  10.1 us
    ppermute x6, starting transfers between devices, add(): lax.ppermute(x, 'rep', turn).astype(F32)  5.63 us
    pallas_call x1, Pallas kernels, attention(): pl.pallas_call(attention_kernel, in_specs=[hbm] * (2 + len(operands)), ou...  3.8 us
  transfers between devices with their start and end apart: 9, of which 8 were waited for; matrix products, arithmetic and copies ran while one was open for 0% of the time, Pallas kernels for 2%

profile of v8, /device:TPU:8, one launch (start us, length us, event | category | flops | bytes accessed | tf_op | source)
XLA Modules:
  0.0 130.9 jit_solution(843933195375053951)
XLA Ops:
  0.0 3.8 %attention.1 = (bf16[16,8,1024]{2,1,0:T(8,128)(2,1)}, bf16[16,8,1024]{2,1,0:T(8,128)(2,1)}) custom-call(s32[1,8]{1,0:T(1,128)} %owner_hbm.1, s32[1,64]{1,0:T(1,128)} %bitcast.25, bf16[4,64,256]{2,1,0:T(8,128)(2,1)} %q_hbm.1, bf16[4,64,256]{2,1,0:T(8,128)(2,1)} %kn_hbm.1, bf16[4,64,256]{2,1,0:T(8,128)(2,1)} %vn_hbm.1, bf16[64,32,256]{2,1,0:T(8,128)(2,1)} %ck_hbm.1, ...), custom_call_target="tpu_custom_call" | custom-call | tf_op jit(solution)/shard_map/attention/pallas_call | solution.py:163
  4.0 1.7 %collective-permute-done = bf16[16,8,1024]{2,1,0:T(8,128)(2,1)S(1)} collective-permute-done((bf16[16,8,1024]{2,1,0:T(8,128)(2,1)}, bf16[16,8,1024]{2,1,0:T(8,128)(2,1)S(1)}, u32[]{:S(2)}, u32[]{:S(2)}) %collective-permute-start) | collective-permute-done | bytes 262176 | tf_op jit(solution)/shard_map/ppermute | solution.py:378
  5.6 1.0 add_convert_fusion
  6.7 22.1 %all_to_all.30 = bf16[16,8,1024]{2,1,0:T(8,128)(2,1)S(1)} all-to-all(bf16[16,8,1024]{2,1,0:T(8,128)(2,1)S(1)} %add_convert_fusion), channel_id=1, replica_groups={{0,2,4,6,8,10,12,14,16,18,20,22,24,26,28,30},{1,3,5,7,9,11,13,15,17,19,..., dimensions={0} | all-to-all | bytes 524288 | tf_op jit(solution)/shard_map/all_to_all | solution.py:381
  29.1 2.1 %fetch.1.w_ref = bf16[2,896,1024]{2,1,0:T(8,128)(2,1)S(1)} custom-call(bf16[3,896,1024]{2,1,0:T(8,128)(2,1)} %bitcast.14), custom_call_target="tpu_custom_call" | custom-call | tf_op jit(solution)/shard_map/fetch/pallas_call | solution.py:223
  31.2 12.0 %all_to_all.31.res_ref = bf16[8,16,896]{2,1,0:T(8,128)(2,1)S(1)} all-to-all(bf16[8,16,896]{2,1,0:T(8,128)(2,1)S(1)} %broadcast_in_dim.10), channel_id=1, replica_groups=mesh['rep'=8,'ep'=32] {'rep'}, dimensions={0} | all-to-all | bytes 458752 | tf_op jit(solution)/shard_map/all_to_all | solution.py:384
  43.8 19.5 %all_to_all.32 = bf16[16,16,896]{2,1,0:T(8,128)(2,1)S(1)} all-to-all(bf16[16,16,896]{2,1,0:T(8,128)(2,1)S(1)} %select.1), channel_id=1, replica_groups={{0,2,4,6,8,10,12,14,16,18,20,22,24,26,28,30},{1,3,5,7,9,11,13,15,17,19,..., dimensions={0} | all-to-all | bytes 917504 | tf_op jit(solution)/shard_map/all_to_all | solution.py:381
  63.2 1.2 gate_up.1
  64.5 16.1 %all_to_all.33 = bf16[8,32,2048]{2,1,0:T(8,128)(2,1)S(1)} all-to-all(bf16[8,32,2048]{2,1,0:T(8,128)(2,1)S(1)} %bitcast.18), channel_id=1, replica_groups=mesh['rep'=8,'ep'=32] {'rep'}, dimensions={0} | all-to-all | bytes 2097152 | tf_op jit(solution)/shard_map/all_to_all | solution.py:384
  80.8 11.2 %all_to_all.34 = bf16[8,32,1024]{2,1,0:T(8,128)(2,1)S(1)} all-to-all(bf16[8,32,1024]{2,1,0:T(8,128)(2,1)S(1)} %broadcast_in_dim.11), channel_id=1, replica_groups=mesh['rep'=8,'ep'=32] {'rep'}, dimensions={0} | all-to-all | bytes 1048576 | tf_op jit(solution)/shard_map/all_to_all | solution.py:384
  92.1 0.7 down.1
  92.8 19.3 %all_to_all.35 = bf16[16,16,896]{2,1,0:T(8,128)(2,1)S(1)} all-to-all(bf16[16,16,896]{2,1,0:T(8,128)(2,1)S(1)} %bitcast.21), channel_id=1, replica_groups={{0,2,4,6,8,10,12,14,16,18,20,22,24,26,28,30},{1,3,5,7,9,11,13,15,17,19,..., dimensions={0} | all-to-all | bytes 917504 | tf_op jit(solution)/shard_map/all_to_all | solution.py:381
  112.9 0.8 collective-permute-done.2.part_ref
  113.7 0.7 combine.3
  114.4 1.5 %collective-permute-start.3 = (bf16[4,8,896]{2,1,0:T(8,128)(2,1)S(1)}, bf16[4,8,896]{2,1,0:T(8,128)(2,1)S(1)}, u32[]{:S(2)}, u32[]{:S(2)}) collective-permute-start(bf16[4,8,896]{2,1,0:T(8,128)(2,1)S(1)} %get-tuple-element.27), channel_id=1, source_target_pairs={{0,32},{32,0},{64,96},{96,64},{128,160},{160,128},{192,224},{224,1... | collective-permute-start | bytes 172040 | tf_op jit(solution)/shard_map/ppermute | solution.py:434
  116.3 2.4 %collective-permute-done.3 = bf16[4,8,896]{2,1,0:T(8,128)(2,1)S(1)} collective-permute-done((bf16[4,8,896]{2,1,0:T(8,128)(2,1)S(1)}, bf16[4,8,896]{2,1,0:T(8,128)(2,1)S(1)}, u32[]{:S(2)}, u32[]{:S(2)}) %collective-permute-start.3) | collective-permute-done | bytes 57376 | tf_op jit(solution)/shard_map/ppermute | solution.py:434
  118.7 0.8 collective-permute-start.4
  120.1 1.3 collective-permute-start.7
  121.4 1.6 %collective-permute-done.4 = bf16[4,8,896]{2,1,0:T(8,128)(2,1)S(1)} collective-permute-done((bf16[4,8,896]{2,1,0:T(8,128)(2,1)S(1)}, bf16[4,8,896]{2,1,0:T(8,128)(2,1)S(1)}, u32[]{:S(2)}, u32[]{:S(2)}) %collective-permute-start.4) | collective-permute-done | bytes 57376 | tf_op jit(solution)/shard_map/ppermute | solution.py:434
  123.0 1.3 collective-permute-start.5
  124.2 1.7 %collective-permute-done.7 = bf16[4,8,896]{2,1,0:T(8,128)(2,1)S(1)} collective-permute-done((bf16[4,8,896]{2,1,0:T(8,128)(2,1)S(1)}, bf16[4,8,896]{2,1,0:T(8,128)(2,1)S(1)}, u32[]{:S(2)}, u32[]{:S(2)}) %collective-permute-start.7) | collective-permute-done | bytes 57376 | tf_op jit(solution)/shard_map/ppermute | solution.py:434
  126.4 2.0 %collective-permute-done.5 = bf16[4,8,896]{2,1,0:T(8,128)(2,1)S(1)} collective-permute-done((bf16[4,8,896]{2,1,0:T(8,128)(2,1)S(1)}, bf16[4,8,896]{2,1,0:T(8,128)(2,1)S(1)}, u32[]{:S(2)}, u32[]{:S(2)}) %collective-permute-start.5) | collective-permute-done | bytes 57376 | tf_op jit(solution)/shard_map/ppermute | solution.py:434
  128.5 1.7 %collective-permute-done.8 = bf16[4,8,896]{2,1,0:T(8,128)(2,1)S(1)} collective-permute-done((bf16[4,8,896]{2,1,0:T(8,128)(2,1)S(1)}, bf16[4,8,896]{2,1,0:T(8,128)(2,1)S(1)}, u32[]{:S(2)}, u32[]{:S(2)}) %collective-permute-start.8) | collective-permute-done | bytes 57376 | tf_op jit(solution)/shard_map/ppermute | solution.py:434
  130.2 0.7 finish.1
  (42 shorter events, 3.7 us)
Async XLA Ops:
  0.0 3.9 %copy-start = (bf16[4,2,7168]{2,1,0:T(2,128)(2,1)S(1)}, bf16[4,2,7168]{2,1,0:T(2,128)(2,1)}, u32[]{:S(2)}) copy-start(bf16[4,2,7168]{2,1,0:T(2,128)(2,1)} %param.13) | copy-start | bytes 344068
  3.8 1.8 %collective-permute-start = (bf16[16,8,1024]{2,1,0:T(8,128)(2,1)}, bf16[16,8,1024]{2,1,0:T(8,128)(2,1)S(1)}, u32[]{:S(2)}, u32[]{:S(2)}) collective-permute-start(bf16[16,8,1024]{2,1,0:T(8,128)(2,1)} %get-tuple-element.18), channel_id=1, source_target_pairs={{0,1},{1,0},{2,3},{3,2},{4,5},{5,4},{6,7},{7,6},{8,9},{9,8},{10,11... | collective-permute-start | bytes 786440 | tf_op jit(solution)/shard_map/ppermute | solution.py:378
  28.9 2.3 %collective-permute-start.1 = (bf16[8,896]{1,0:T(8,128)(2,1)S(1)}, bf16[8,896]{1,0:T(8,128)(2,1)S(1)}, u32[]{:S(2)}, u32[]{:S(2)}) collective-permute-start(bf16[8,896]{1,0:T(8,128)(2,1)S(1)} %add_convert_fusion.7), channel_id=1, source_target_pairs={{0,1},{1,0},{2,3},{3,2},{4,5},{5,4},{6,7},{7,6},{8,9},{9,8},{10,11... | collective-permute-start | bytes 43016 | tf_op jit(solution)/shard_map/ppermute | solution.py:378
  29.1 14.1 %copy-start.1 = (f32[7168]{0:T(1024)S(1)}, f32[7168]{0:T(1024)}, u32[]{:S(2)}) copy-start(f32[7168]{0:T(1024)} %param.22) | copy-start | bytes 86020
  43.8 48.3 %slice-start = ((s8[5505024]{0:T(1024)(128)(4,1)}), s8[4194304]{0:T(1024)(128)(4,1)S(1)}, s32[]{:S(2)}) async-start(s8[5505024]{0:T(1024)(128)(4,1)} %bitcast.15), calls=%async_computation.6 | async-start | bytes 8388608
  63.2 28.8 %slice-start.1 = ((s8[5505024]{0:T(1024)(128)(4,1)}), s8[1310720]{0:T(1024)(128)(4,1)S(1)}, s32[]{:S(2)}) async-start(s8[5505024]{0:T(1024)(128)(4,1)} %bitcast.15), calls=%async_computation.7 | async-start | bytes 2621440
  92.0 20.2 %copy-start.2 = (s32[4,2,8]{2,1,0:T(2,128)S(1)}, s32[4,2,8]{2,1,0:T(2,128)}, u32[]{:S(2)}) copy-start(s32[4,2,8]{2,1,0:T(2,128)} %ids_ref.3) | copy-start | bytes 772
  92.0 20.2 %copy-start.3 = (f32[4,2,8]{2,1,0:T(2,128)S(1)}, f32[4,2,8]{2,1,0:T(2,128)}, u32[]{:S(2)}) copy-start(f32[4,2,8]{2,1,0:T(2,128)} %logits_ref.3) | copy-start | bytes 772
  112.1 1.6 %collective-permute-start.2 = (bf16[16,8,896]{2,1,0:T(8,128)(2,1)S(1)}, bf16[16,8,896]{2,1,0:T(8,128)(2,1)S(1)}, u32[]{:S(2)}, u32[]{:S(2)}) collective-permute-start(bf16[16,8,896]{2,1,0:T(8,128)(2,1)S(1)} %get-tuple-element.30), channel_id=1, source_target_pairs={{0,1},{1,0},{2,3},{3,2},{4,5},{5,4},{6,7},{7,6},{8,9},{9,8},{10,11... | collective-permute-start | bytes 688136 | tf_op jit(solution)/shard_map/ppermute | solution.py:378
  114.4 4.3 %collective-permute-start.3 = (bf16[4,8,896]{2,1,0:T(8,128)(2,1)S(1)}, bf16[4,8,896]{2,1,0:T(8,128)(2,1)S(1)}, u32[]{:S(2)}, u32[]{:S(2)}) collective-permute-start(bf16[4,8,896]{2,1,0:T(8,128)(2,1)S(1)} %get-tuple-element.27), channel_id=1, source_target_pairs={{0,32},{32,0},{64,96},{96,64},{128,160},{160,128},{192,224},{224,1... | collective-permute-start | bytes 172040 | tf_op jit(solution)/shard_map/ppermute | solution.py:434
  115.9 4.2 %collective-permute-start.6 = (bf16[4,8,896]{2,1,0:T(8,128)(2,1)S(1)}, bf16[4,8,896]{2,1,0:T(8,128)(2,1)S(1)}, u32[]{:S(2)}, u32[]{:S(2)}) collective-permute-start(bf16[4,8,896]{2,1,0:T(8,128)(2,1)S(1)} %get-tuple-element.28), channel_id=1, source_target_pairs={{0,64},{32,96},{64,0},{96,32},{128,192},{160,224},{192,128},{224,1... | collective-permute-start | bytes 172040 | tf_op jit(solution)/shard_map/ppermute | solution.py:434
  118.7 4.3 %collective-permute-start.4 = (bf16[4,8,896]{2,1,0:T(8,128)(2,1)S(1)}, bf16[4,8,896]{2,1,0:T(8,128)(2,1)S(1)}, u32[]{:S(2)}, u32[]{:S(2)}) collective-permute-start(bf16[4,8,896]{2,1,0:T(8,128)(2,1)S(1)} %add_convert_fusion.6), channel_id=1, source_target_pairs={{0,64},{32,96},{64,0},{96,32},{128,192},{160,224},{192,128},{224,1... | collective-permute-start | bytes 172040 | tf_op jit(solution)/shard_map/ppermute | solution.py:434
  120.1 5.8 %collective-permute-start.7 = (bf16[4,8,896]{2,1,0:T(8,128)(2,1)S(1)}, bf16[4,8,896]{2,1,0:T(8,128)(2,1)S(1)}, u32[]{:S(2)}, u32[]{:S(2)}) collective-permute-start(bf16[4,8,896]{2,1,0:T(8,128)(2,1)S(1)} %add_convert_fusion.3), channel_id=1, source_target_pairs={{0,192},{32,224},{64,128},{96,160},{128,64},{160,96},{192,0},{224,... | collective-permute-start | bytes 172040 | tf_op jit(solution)/shard_map/ppermute | solution.py:434
  123.0 5.5 %collective-permute-start.5 = (bf16[4,8,896]{2,1,0:T(8,128)(2,1)S(1)}, bf16[4,8,896]{2,1,0:T(8,128)(2,1)S(1)}, u32[]{:S(2)}, u32[]{:S(2)}) collective-permute-start(bf16[4,8,896]{2,1,0:T(8,128)(2,1)S(1)} %add_convert_fusion.5), channel_id=1, source_target_pairs={{0,192},{32,224},{64,128},{96,160},{128,64},{160,96},{192,0},{224,... | collective-permute-start | bytes 172040 | tf_op jit(solution)/shard_map/ppermute | solution.py:434
  125.9 4.3 %collective-permute-start.8 = (bf16[4,8,896]{2,1,0:T(8,128)(2,1)S(1)}, bf16[4,8,896]{2,1,0:T(8,128)(2,1)S(1)}, u32[]{:S(2)}, u32[]{:S(2)}) collective-permute-start(bf16[4,8,896]{2,1,0:T(8,128)(2,1)S(1)} %add_convert_fusion.2), channel_id=1, source_target_pairs={{0,32},{32,0},{64,96},{96,64},{128,160},{160,128},{192,224},{224,1... | collective-permute-start | bytes 172040 | tf_op jit(solution)/shard_map/ppermute | solution.py:434
